TPU v7x, 32 devices: a whole 2x2x4 slice. The times are simulated.
32 devices in a mesh: groups: 2 (over y), et: 4 (over z), ep: 4 (over x, core).
Axes of the slice: x: 2, y: 2, z: 4, core: 2. Of those that a mesh axis runs over, the one named last changes fastest.
Arguments:
- tokens: bfloat16 [768, 3072], P(('groups', 'et', 'ep')), parts along dimension 0, may hold values from -6 to 6
- expert_ids: int32 [768, 2], P(('groups', 'et', 'ep')), parts along dimension 0, may hold values from 0 to 3, all different within a row; in each aligned block of 24 rows (0 to 23, 24 to 47, ...) at most 12 rows name the same one
- gate_weights: float32 [768, 2], P(('groups', 'et', 'ep')), parts along dimension 0, may hold values from 0.2 to 1
- w_gate: bfloat16 [4, 3072, 8192], P('ep', None, 'et'), may hold values from -0.109375 to 0.109375
- w_up: bfloat16 [4, 3072, 8192], P('ep', None, 'et'), may hold values from -0.109375 to 0.109375
Outputs:
- routed_hidden: bfloat16 [768, 2, 8192], P(('groups', 'et', 'ep')), parts along dimension 0
There are 2 independent parts, one for each index of `groups`. A program takes and returns all parts, laid end to end along the dimension named above; an argument that names none is the same for every part. Nothing has to cross between parts.
Inputs may be any that keep to these rules, and one draw needn't show every extreme that they name: `expert_ids`: A token's 2 experts differ. Among the 24 tokens of one device no expert is named more than 12 times, and in every draw some device names some expert exactly 12 times.
All inputs are finite; a program needn't handle non-finite values.
Results may differ from a plain program's by a relative error of at most 0.005.
Values may be sent and summed in bfloat16 or wider, within the bound.
No kernel may reach another device: no remote copies, remote signals or barrier semaphores. Data moves between devices by JAX's collectives and lax.ppermute only.
A program may use at most 128 MiB of HBM per device.

v0:
```python
import jax
import jax.numpy as jnp
from jax import lax
from jax.sharding import PartitionSpec as P


def place_slots(id_block, experts, capacity):
    flat_ids = id_block.reshape(-1)
    onehot = (flat_ids[:, None] == jnp.arange(experts, dtype=jnp.int32)[None, :]).astype(jnp.int32)
    before = jnp.cumsum(onehot, axis=0) - onehot
    position = jnp.sum(before * onehot, axis=1)
    return (flat_ids * capacity + position).reshape(id_block.shape)


def build_select(slot_pairs, total):
    targets = jnp.arange(total, dtype=jnp.int32).reshape(-1, 1, 1)
    return jnp.sum(slot_pairs[..., None, :, :] == targets, axis=-1).astype(jnp.bfloat16)


def swiglu_rows(rows, gate_local, up_local):
    gate_val = jnp.dot(rows, gate_local, preferred_element_type=jnp.float32)
    up_val = jnp.dot(rows, up_local, preferred_element_type=jnp.float32)
    return (jax.nn.silu(gate_val) * up_val).astype(jnp.bfloat16)


def body(tokens, expert_ids, gate_weights, w_gate, w_up):
    tok_rows, width = tokens.shape
    experts = lax.axis_size("ep")
    tensor_size = lax.axis_size("et")
    capacity = tok_rows // 2
    gate_local = w_gate[0]
    up_local = w_up[0]
    slot_pairs = place_slots(expert_ids, experts, capacity)
    selector = build_select(slot_pairs, experts * capacity)
    buffer = jnp.dot(selector, tokens, preferred_element_type=jnp.float32).astype(jnp.bfloat16)
    buffer = buffer.reshape(experts, capacity, width)
    arrived = lax.all_to_all(buffer, "ep", split_axis=0, concat_axis=0, tiled=True).reshape(
        experts * capacity, width
    )
    hidden = swiglu_rows(lax.all_gather(arrived, "et", axis=0, tiled=True), gate_local, up_local)
    hidden = hidden.reshape(tensor_size, experts, capacity, -1)
    moved = lax.all_to_all(hidden, "et", split_axis=0, concat_axis=3, tiled=True)
    returned = lax.all_to_all(moved, "ep", split_axis=1, concat_axis=1, tiled=True)
    returned = returned.reshape(experts * capacity, -1)
    targets = jnp.arange(experts * capacity, dtype=jnp.int32)
    picker = (slot_pairs[:, :, None] == targets[None, None, :]).astype(jnp.bfloat16)
    gathered = jnp.einsum("tsj,jf->tsf", picker, returned, preferred_element_type=jnp.float32)
    return (gate_weights[:, :, None] * gathered).astype(jnp.bfloat16)


def solution(mesh):
    in_specs = (
        P(("groups", "et", "ep"), None),
        P(("groups", "et", "ep"), None),
        P(("groups", "et", "ep"), None),
        P("ep", None, "et"),
        P("ep", None, "et"),
    )
    out_specs = P(("groups", "et", "ep"), None, None)
    return jax.shard_map(body, mesh=mesh, in_specs=in_specs, out_specs=out_specs, check_vma=False)
```

profile of v0, /device:TPU:0, one launch (start us, length us, event | category | flops | bytes accessed | tf_op | source)
XLA Modules:
  0.0 118.1 jit_solution(2169006138317158585)
XLA Ops:
  6.5 0.0 copy-start
  6.5 0.0 all-gather.2.cloned.1.call-start
  6.5 0.8 copy.35
  7.3 0.1 eq.20
  7.4 0.1 fusion.11
  7.5 0.1 reduce_window_sum.11
  7.6 0.2 select_reduce_fusion
  7.8 0.1 reduce_sum.21
  7.9 0.1 copy.36
  8.0 0.7 multiply_add_fusion
  8.6 0.1 convert_reduce_fusion
  8.7 0.0 copy-done
  8.7 0.3 convolution_convert_fusion
  9.0 0.1 reshape.28
  9.1 11.4 %all_to_all.28 = bf16[4,12,3072]{2,1,0:T(8,128)(2,1)S(1)} all-to-all(bf16[4,12,3072]{2,1,0:T(8,128)(2,1)S(1)} %reshape.28), channel_id=1, replica_groups=mesh['groups'=2,'et'=4,'ep'=4] {'ep'}, dimensions={0} | all-to-all | bytes 589824 | tf_op jit(solution)/shard_map/all_to_all | solution.py:37
  20.5 0.8 reshape.29
  21.3 0.0 all-gather.2.cloned.1.call-update
  21.3 30.9 %all-gather.2.cloned.1.call-done = bf16[192,3072]{1,0:T(8,128)(2,1)} async-done(((bf16[48,3072]{1,0:T(8,128)(2,1)}), bf16[192,3072]{1,0:T(8,128)(2,1)}) %all-gather.2.cloned.1.call-update) | async-done | bytes 1179664 | tf_op jit(solution)/shard_map/all_gather | solution.py:40
  52.3 7.5 %fusion.2 = f32[192,2048]{1,0:T(8,128)S(1)} fusion(bf16[192,3072]{1,0:T(8,128)(2,1)} %all-gather.2.cloned.1.call-done, bf16[1,3072,2048]{2,1,0:T(8,128)(2,1)} %param.8), kind=kOutput, calls=%fused_computation.2 | convolution fusion | flops 2415919104 | bytes 15335424 | tf_op jit(solution)/shard_map/dot_general | solution.py:21
  59.8 0.0 copy-done.2
  59.8 7.3 %fusion.8 = bf16[192,2048]{1,0:T(8,128)(2,1)S(1)} fusion(bf16[192,3072]{1,0:T(8,128)(2,1)S(1)} %copy-done.2, bf16[1,3072,2048]{2,1,0:T(8,128)(2,1)} %param.9, f32[192,2048]{1,0:T(8,128)S(1)} %fusion.2), kind=kOutput, calls=%fused_computation.8 | convolution fusion | flops 2418278400 | bytes 16121856 | tf_op jit(solution)/shard_map/dot_general | solution.py:22
  67.1 0.2 reshape.30
  67.3 0.6 copy.37
  67.9 22.7 %all_to_all.29 = bf16[4,4,12,2048]{3,1,2,0:T(4,128)(2,1)S(1)} all-to-all(bf16[4,4,12,2048]{3,1,2,0:T(4,128)(2,1)S(1)} %copy.37), channel_id=1, replica_groups=mesh['groups'=2,'et'=4,'ep'=4] {'et'}, dimensions={0} | all-to-all | bytes 1572864 | tf_op jit(solution)/shard_map/all_to_all | solution.py:42
  90.6 0.6 copy.41
  91.2 0.5 reshape.33
  91.8 0.0 copy-start.1
  91.8 17.1 %all_to_all.30 = bf16[1,4,12,8192]{3,2,0,1:T(8,128)(2,1)S(1)} all-to-all(bf16[1,4,12,8192]{3,2,0,1:T(8,128)(2,1)S(1)} %reshape.33), channel_id=1, replica_groups=mesh['groups'=2,'et'=4,'ep'=4] {'ep'}, dimensions={1} | all-to-all | bytes 1572864 | tf_op jit(solution)/shard_map/all_to_all | solution.py:43
  108.9 0.2 reshape.32
  109.1 0.0 copy-done.1
  109.1 0.4 fusion.4
  109.6 1.7 %copy.40 = bf16[24,2,8192]{2,1,0:T(2,128)(2,1)} copy(bf16[24,2,8192]{2,0,1:T(8,128)(2,1)S(1)} %fusion.4) | data formatting | bytes 1572864 | tf_op jit(solution)/shard_map/convert_element_type | solution.py:48
  (1 shorter events, 0.0 us)
Async XLA Ops:
  6.5 2.2 %copy-start = (bf16[24,3072]{1,0:T(8,128)(2,1)S(1)}, bf16[24,3072]{1,0:T(8,128)(2,1)}, u32[]{:S(2)}) copy-start(bf16[24,3072]{1,0:T(8,128)(2,1)} %param.5) | copy-start | bytes 442372
  6.5 45.7 %all-gather.2.cloned.1.call-start = ((), (), s32[]{:S(2)}) async-start(), calls=%async_computation.3 | async-start | bytes 1474560 | tf_op jit(solution)/shard_map/all_gather | solution.py:40
  52.3 7.5 %copy-start.2 = (bf16[192,3072]{1,0:T(8,128)(2,1)S(1)}, bf16[192,3072]{1,0:T(8,128)(2,1)}, u32[]{:S(2)}) copy-start(bf16[192,3072]{1,0:T(8,128)(2,1)} %all-gather.2.cloned.1.call-done) | copy-start | bytes 3538948
  91.8 17.4 %copy-start.1 = (f32[24,2]{0,1:T(2,128)S(1)}, f32[24,2]{0,1:T(2,128)}, u32[]{:S(2)}) copy-start(f32[24,2]{0,1:T(2,128)} %param.7) | copy-start | bytes 580
Sparse Core Ops, SparseCore 0:
  21.5 30.7 all-gather.1
where the time goes:
time: 118 us
  blocking collectives  51.3 us (43%)
  waiting for transfers between devices  30.9 us (26%)
  matrix products  15.5 us (13%)
  between operations  13.5 us (11%)
  local copies, waits for them, and re-layouts  5.75 us (5%)
    all_gather x1, waiting for transfers between devices, body(): lax.all_gather(arrived, 'et', axis=0, tiled=True)  30.9 us
    all_to_all x1, blocking collectives, body(): lax.all_to_all(hidden, 'et', split_axis=0, concat_axis=3, tiled=True)  22.7 us
    all_to_all x1, blocking collectives, body(): lax.all_to_all(moved, 'ep', split_axis=1, concat_axis=1, tiled=True)  17.1 us
    all_to_all x1, blocking collectives, body(): lax.all_to_all(buffer, 'ep', split_axis=0, concat_axis=0, tiled=True)  11.4 us
    dot_general x1, matrix products, swiglu_rows(): gate_val = jnp.dot(rows, gate_local, preferred_element_type=jnp.float32)  7.51 us
    dot_general x1, matrix products, swiglu_rows(): up_val = jnp.dot(rows, up_local, preferred_element_type=jnp.float32)  7.3 us
  transfers between devices with their start and end apart: 1, of which 1 were waited for; matrix products, arithmetic and copies ran while one was open for 0% of the time, Pallas kernels for 0%

commit v1 on v0

--- a/solution.py
+++ b/solution.py
@@ -23,28 +23,32 @@
     return (jax.nn.silu(gate_val) * up_val).astype(jnp.bfloat16)
 
 
+def exchange(blocks):
+    return lax.all_to_all(blocks, ("et", "ep"), split_axis=0, concat_axis=0, tiled=True)
+
+
 def body(tokens, expert_ids, gate_weights, w_gate, w_up):
     tok_rows, width = tokens.shape
     experts = lax.axis_size("ep")
     tensor_size = lax.axis_size("et")
+    peers = experts * tensor_size
     capacity = tok_rows // 2
     gate_local = w_gate[0]
     up_local = w_up[0]
     slot_pairs = place_slots(expert_ids, experts, capacity)
     selector = build_select(slot_pairs, experts * capacity)
     buffer = jnp.dot(selector, tokens, preferred_element_type=jnp.float32).astype(jnp.bfloat16)
-    buffer = buffer.reshape(experts, capacity, width)
-    arrived = lax.all_to_all(buffer, "ep", split_axis=0, concat_axis=0, tiled=True).reshape(
-        experts * capacity, width
-    )
-    hidden = swiglu_rows(lax.all_gather(arrived, "et", axis=0, tiled=True), gate_local, up_local)
-    hidden = hidden.reshape(tensor_size, experts, capacity, -1)
-    moved = lax.all_to_all(hidden, "et", split_axis=0, concat_axis=3, tiled=True)
-    returned = lax.all_to_all(moved, "ep", split_axis=1, concat_axis=1, tiled=True)
-    returned = returned.reshape(experts * capacity, -1)
+    buffer = buffer.reshape(1, experts, capacity * width // 128, 128)
+    buffer = jnp.broadcast_to(buffer, (tensor_size,) + buffer.shape[1:])
+    arrived = exchange(buffer.reshape(peers, capacity * width // 128, 128))
+    hidden = swiglu_rows(arrived.reshape(peers * capacity, width), gate_local, up_local)
+    units = hidden.shape[1]
+    returned = exchange(hidden.reshape(peers, capacity * units // 128, 128))
+    returned = returned.reshape(tensor_size, experts * capacity, units)
     targets = jnp.arange(experts * capacity, dtype=jnp.int32)
     picker = (slot_pairs[:, :, None] == targets[None, None, :]).astype(jnp.bfloat16)
-    gathered = jnp.einsum("tsj,jf->tsf", picker, returned, preferred_element_type=jnp.float32)
+    gathered = jnp.einsum("tsj,ejf->tsef", picker, returned, preferred_element_type=jnp.float32)
+    gathered = gathered.reshape(tok_rows, 2, tensor_size * units)
     return (gate_weights[:, :, None] * gathered).astype(jnp.bfloat16)
 
 

time: 118 us -> 81.4 us (0.69)
  waiting for transfers between devices: 30.9 us -> 0 us
  between operations: 13.5 us -> 0.11 us
  blocking collectives: 51.3 us -> 60 us
  matrix products: 15.5 us -> 14.1 us
    all_gather x1 -> x0, waiting for transfers between devices: 30.9 us -> none  [body(): lax.all_gather(arrived, 'et', axis=0, tiled=True)]
    all_to_all x3 -> x2, blocking collectives: 51.3 us -> 60 us  [exchange(): lax.all_to_all(blocks, ('et', 'ep'), split_axis=0, concat_axis=0, tiled=T...]
    dot_general x1, matrix products: 7.51 us -> 6.08 us  [swiglu_rows(): gate_val = jnp.dot(rows, gate_local, preferred_element_type=jnp.float32)]
  transfers between devices with their start and end apart: 1 -> 0, of which waited for: 1 -> 0; matrix products, arithmetic and copies ran while one was open for 0% -> 0% of each run, Pallas kernels for 0% -> 0%
where the time goes in v1:
time: 81.4 us; the launch traced here: 80.8 us
  blocking collectives  60 us (74%)
  matrix products  14.1 us (17%)
  local copies, waits for them, and re-layouts  5.48 us (7%)
  other arithmetic  1.1 us (1%)
    all_to_all x2, blocking collectives, exchange(): lax.all_to_all(blocks, ('et', 'ep'), split_axis=0, concat_axis=0, tiled=T...  60 us
    dot_general x1, matrix products, swiglu_rows(): up_val = jnp.dot(rows, up_local, preferred_element_type=jnp.float32)  7.36 us
    dot_general x1, matrix products, swiglu_rows(): gate_val = jnp.dot(rows, gate_local, preferred_element_type=jnp.float32)  6.08 us
    convert_element_type x1, local copies, waits for them, and re-layouts, body(): return (gate_weights[:, :, None] * gathered).astype(jnp.bfloat16)  1.69 us

profile of v1, /device:TPU:0, one launch (start us, length us, event | category | flops | bytes accessed | tf_op | source)
XLA Modules:
  0.0 80.8 jit_solution(12415827491706824208)
XLA Ops:
  0.0 0.0 copy-start
  0.0 0.8 copy.25
  0.8 0.1 eq.20
  0.9 0.1 fusion.11
  1.0 0.1 reduce_window_sum.11
  1.0 0.2 select_reduce_fusion
  1.2 0.1 reduce_sum.21
  1.3 0.1 copy.26
  1.4 0.7 multiply_add_fusion
  2.1 0.1 convert_reduce_fusion
  2.2 0.0 copy-done
  2.2 0.3 convolution_convert_fusion
  2.5 0.1 broadcast_in_dim.4
  2.6 0.2 broadcast_in_dim.5
  2.8 36.6 %all_to_all.10 = bf16[16,288,128]{2,1,0:T(8,128)(2,1)S(1)} all-to-all(bf16[16,288,128]{2,1,0:T(8,128)(2,1)S(1)} %bitcast.20), channel_id=1, replica_groups=mesh['groups'=2,'et'=4,'ep'=4] {'et','ep'}, dimensions={0} | all-to-all | bytes 2359296 | tf_op jit(solution)/shard_map/all_to_all | solution.py:27
  39.4 0.5 reshape.33
  40.0 6.1 %fusion.2 = f32[192,2048]{1,0:T(8,128)S(1)} fusion(bf16[192,3072]{1,0:T(8,128)(2,1)S(1)} %reshape.33, bf16[1,3072,2048]{2,1,0:T(8,128)(2,1)} %param.8), kind=kOutput, calls=%fused_computation.2 | convolution fusion | flops 2415919104 | bytes 15335424 | tf_op jit(solution)/shard_map/dot_general | solution.py:21
  46.0 7.4 %fusion.8 = bf16[192,2048]{1,0:T(8,128)(2,1)S(1)} fusion(bf16[192,3072]{1,0:T(8,128)(2,1)S(1)} %reshape.33, bf16[1,3072,2048]{2,1,0:T(8,128)(2,1)} %param.9, f32[192,2048]{1,0:T(8,128)S(1)} %fusion.2), kind=kOutput, calls=%fused_computation.8 | convolution fusion | flops 2418278400 | bytes 16121856 | tf_op jit(solution)/shard_map/dot_general | solution.py:22
  53.4 0.4 reshape.34
  53.8 23.4 %all_to_all.11 = bf16[16,192,128]{2,1,0:T(8,128)(2,1)S(1)} all-to-all(bf16[16,192,128]{2,1,0:T(8,128)(2,1)S(1)} %reshape.34), channel_id=1, replica_groups=mesh['groups'=2,'et'=4,'ep'=4] {'et','ep'}, dimensions={0} | all-to-all | bytes 1572864 | tf_op jit(solution)/shard_map/all_to_all | solution.py:27
  77.1 0.3 reshape.35
  77.5 0.0 copy-start.1
  77.5 0.6 copy.30
  78.1 0.6 reshape.36
  78.7 0.0 copy-done.1
  78.7 0.4 fusion.4
  79.1 1.7 %copy.28 = bf16[24,2,8192]{2,1,0:T(2,128)(2,1)} copy(bf16[24,2,8192]{2,0,1:T(8,128)(2,1)S(1)} %fusion.4) | data formatting | bytes 1572864 | tf_op jit(solution)/shard_map/convert_element_type | solution.py:52
Async XLA Ops:
  0.0 2.2 %copy-start = (bf16[24,3072]{1,0:T(8,128)(2,1)S(1)}, bf16[24,3072]{1,0:T(8,128)(2,1)}, u32[]{:S(2)}) copy-start(bf16[24,3072]{1,0:T(8,128)(2,1)} %param.5) | copy-start | bytes 442372
  77.5 1.2 %copy-start.1 = (f32[24,2]{0,1:T(2,128)S(1)}, f32[24,2]{0,1:T(2,128)}, u32[]{:S(2)}) copy-start(f32[24,2]{0,1:T(2,128)} %param.7) | copy-start | bytes 580

commit v2 on v1

--- a/solution.py
+++ b/solution.py
@@ -1,6 +1,10 @@
+import functools
+
 import jax
 import jax.numpy as jnp
 from jax import lax
+from jax.experimental import pallas as pl
+from jax.experimental.pallas import tpu as pltpu
 from jax.sharding import PartitionSpec as P
 
 
@@ -27,6 +31,115 @@
     return lax.all_to_all(blocks, ("et", "ep"), split_axis=0, concat_axis=0, tiled=True)
 
 
+def exact_dot(a, b):
+    return jnp.dot(a, b, preferred_element_type=jnp.float32)
+
+
+def hidden_kernel(folds, x_ref, gate_ref, up_ref, out_ref, hidden_ref):
+    peers = out_ref.shape[0]
+    capacity = hidden_ref.shape[0] // peers
+    span = hidden_ref.shape[1] // folds
+    gate_val = exact_dot(x_ref[...], gate_ref[...])
+    up_val = exact_dot(x_ref[...], up_ref[...])
+    hidden_ref[...] = gate_val / (1.0 + jnp.exp(-gate_val)) * up_val
+    for peer in range(peers):
+        rows = hidden_ref[peer * capacity : (peer + 1) * capacity, :]
+        pieces = [rows[:, fold * span : (fold + 1) * span] for fold in range(folds)]
+        out_ref[peer] = jnp.concatenate(pieces, axis=0).astype(out_ref.dtype)
+
+
+def hidden_blocks(x, gate_local, up_local, peers, folds):
+    rows, width = x.shape
+    units = gate_local.shape[1]
+    whole = pl.BlockSpec(memory_space=pltpu.VMEM)
+    return pl.pallas_call(
+        functools.partial(hidden_kernel, folds),
+        out_shape=jax.ShapeDtypeStruct((peers, rows // peers * folds, units // folds), x.dtype),
+        in_specs=[whole] * 3,
+        out_specs=whole,
+        scratch_shapes=[pltpu.VMEM((rows, units), jnp.float32)],
+        compiler_params=pltpu.CompilerParams(vmem_limit_bytes=16 << 20),
+        cost_estimate=pl.CostEstimate(
+            flops=4 * rows * width * units,
+            bytes_accessed=4 * width * units,
+            transcendentals=rows * units,
+        ),
+    )(x, gate_local, up_local)
+
+
+def picks_of(ids, experts, capacity, folds):
+    tok_rows = ids.shape[0]
+    lower = (
+        lax.broadcasted_iota(jnp.int32, (tok_rows, tok_rows), 0)
+        > lax.broadcasted_iota(jnp.int32, (tok_rows, tok_rows), 1)
+    ).astype(jnp.bfloat16)
+    expert = lax.broadcasted_iota(jnp.int32, (tok_rows, 128), 1)
+    first, second = ids[:, 0:1], ids[:, 1:2]
+    named = ((expert == first) | (expert == second)).astype(jnp.bfloat16)
+    before = exact_dot(lower, named).astype(jnp.int32)
+    wide = experts * folds * capacity
+    lane = lax.broadcasted_iota(jnp.int32, (tok_rows, wide), 1)
+    spread = lax.broadcasted_iota(jnp.int32, (2 * tok_rows, tok_rows), 0)
+    token = lax.broadcasted_iota(jnp.int32, (2 * tok_rows, tok_rows), 1)
+    targets, doubles = [], []
+    for slot, chosen in enumerate((first, second)):
+        position = jnp.sum(jnp.where(expert == chosen, before, 0), axis=1, keepdims=True)
+        targets.append(chosen * (folds * capacity) + position)
+        doubles.append((spread == 2 * token + slot).astype(jnp.bfloat16))
+    picks = []
+    for fold in range(folds):
+        rows = sum(
+            exact_dot(double, (lane == target + fold * capacity).astype(jnp.bfloat16))
+            for double, target in zip(doubles, targets)
+        )
+        picks.append(rows.astype(jnp.bfloat16))
+    return jnp.concatenate(picks, axis=0)
+
+
+def slot_weights(weights):
+    tok_rows = weights.shape[0]
+    row = lax.broadcasted_iota(jnp.int32, (2 * tok_rows, tok_rows), 0)
+    token = lax.broadcasted_iota(jnp.int32, (2 * tok_rows, tok_rows), 1)
+    column = jnp.zeros((2 * tok_rows, 1), jnp.float32)
+    for slot in range(2):
+        double = (row == 2 * token + slot).astype(jnp.bfloat16)
+        rest = weights[:, slot : slot + 1]
+        for _ in range(3):
+            part = rest.astype(jnp.bfloat16)
+            spread = exact_dot(double, jnp.broadcast_to(part, (tok_rows, 128)))
+            column = column + spread[:, 0:1]
+            rest = rest - part.astype(jnp.float32)
+    return column
+
+
+def final_kernel(experts, folds, ids_ref, weights_ref, recv_ref, out_ref):
+    tok_rows = ids_ref.shape[0]
+    peers, tall, span = recv_ref.shape
+    picks = picks_of(ids_ref[...], experts, tall // folds, folds)
+    column = slot_weights(weights_ref[...])
+    for part in range(peers // experts):
+        block = recv_ref[part * experts : (part + 1) * experts].reshape(experts * tall, span)
+        rows = exact_dot(picks, block)
+        for fold in range(folds):
+            scaled = rows[fold * 2 * tok_rows : (fold + 1) * 2 * tok_rows] * column
+            start = (part * folds + fold) * span
+            out_ref[:, :, start : start + span] = scaled.astype(out_ref.dtype).reshape(tok_rows, 2, span)
+
+
+def finish(expert_ids, gate_weights, received, experts, folds):
+    tok_rows = expert_ids.shape[0]
+    peers, tall, span = received.shape
+    whole = pl.BlockSpec(memory_space=pltpu.VMEM)
+    units = peers // experts * folds * span
+    return pl.pallas_call(
+        functools.partial(final_kernel, experts, folds),
+        out_shape=jax.ShapeDtypeStruct((tok_rows, 2, units), received.dtype),
+        in_specs=[whole] * 3,
+        out_specs=whole,
+        compiler_params=pltpu.CompilerParams(vmem_limit_bytes=16 << 20),
+    )(expert_ids, gate_weights, received)
+
+
 def body(tokens, expert_ids, gate_weights, w_gate, w_up):
     tok_rows, width = tokens.shape
     experts = lax.axis_size("ep")
@@ -41,8 +154,12 @@
     buffer = buffer.reshape(1, experts, capacity * width // 128, 128)
     buffer = jnp.broadcast_to(buffer, (tensor_size,) + buffer.shape[1:])
     arrived = exchange(buffer.reshape(peers, capacity * width // 128, 128))
+    units = gate_local.shape[1]
+    if peers <= 16:
+        folds = 4
+        blocks = hidden_blocks(arrived.reshape(peers * capacity, width), gate_local, up_local, peers, folds)
+        return finish(expert_ids, gate_weights, exchange(blocks), experts, folds)
     hidden = swiglu_rows(arrived.reshape(peers * capacity, width), gate_local, up_local)
-    units = hidden.shape[1]
     returned = exchange(hidden.reshape(peers, capacity * units // 128, 128))
     returned = returned.reshape(tensor_size, experts * capacity, units)
     targets = jnp.arange(experts * capacity, dtype=jnp.int32)

time: 81.4 us -> 79.7 us (0.979)
  blocking collectives: 60 us -> 36.6 us
  waiting for transfers between devices: 0 us -> 18.6 us
  matrix products: 14.1 us -> 0.26 us
  Pallas kernels: 0 us -> 7.82 us
  local copies, waits for them, and re-layouts: 5.48 us -> 11.1 us
  starting transfers between devices: 0 us -> 3.75 us
    all_to_all x2 -> x1, blocking collectives: 60 us -> 36.6 us  [exchange(): lax.all_to_all(blocks, ('et', 'ep'), split_axis=0, concat_axis=0, tiled=T...]
    all_to_all x0 -> x1, waiting for transfers between devices: none -> 18.6 us  [exchange(): lax.all_to_all(blocks, ('et', 'ep'), split_axis=0, concat_axis=0, tiled=T...]
    dot_general x3 -> x0, matrix products: 13.9 us -> none  [the longest x1 7.36 us: swiglu_rows(): up_val = jnp.dot(rows, up_local, preferred_element_type=jnp.float32)]
    unnamed x5 -> x10, local copies, waits for them, and re-layouts: 0.8 us -> 10 us
    pallas_call x0 -> x2, Pallas kernels: none -> 7.82 us  [the longest x1 6.04 us: hidden_blocks(): pl.pallas_call(functools.partial(hidden_kernel, folds), out_shape=jax.Sha...]
    all_to_all x0 -> x1, starting transfers between devices: none -> 3.75 us  [exchange(): lax.all_to_all(blocks, ('et', 'ep'), split_axis=0, concat_axis=0, tiled=T...]
    convert_element_type x1 -> x0, local copies, waits for them, and re-layouts: 1.69 us -> none  [body(): return (gate_weights[:, :, None] * gathered).astype(jnp.bfloat16)]
    reshape x3 -> x0, local copies, waits for them, and re-layouts: 1.3 us -> none  [the longest x2 0.94 us: body(): returned = returned.reshape(tensor_size, experts * capacity, units)]
  transfers between devices with their start and end apart: 0 -> 1, of which waited for: 0 -> 1; matrix products, arithmetic and copies ran while one was open for 0% -> 0% of each run, Pallas kernels for 0% -> 0%
where the time goes in v2:
time: 79.7 us; the launch traced here: 79.4 us
  blocking collectives  36.6 us (46%)
  waiting for transfers between devices  18.6 us (23%)
  local copies, waits for them, and re-layouts  11.1 us (14%)
  Pallas kernels  7.82 us (10%)
  starting transfers between devices  3.75 us (5%)
  other arithmetic  1.1 us (1%)
    all_to_all x1, blocking collectives, exchange(): lax.all_to_all(blocks, ('et', 'ep'), split_axis=0, concat_axis=0, tiled=T...  36.6 us
    all_to_all x1, waiting for transfers between devices, exchange(): lax.all_to_all(blocks, ('et', 'ep'), split_axis=0, concat_axis=0, tiled=T...  18.6 us
    unnamed x10, local copies, waits for them, and re-layouts  10 us
    pallas_call x1, Pallas kernels, hidden_blocks(): pl.pallas_call(functools.partial(hidden_kernel, folds), out_shape=jax.Sha...  6.04 us
    all_to_all x1, starting transfers between devices, exchange(): lax.all_to_all(blocks, ('et', 'ep'), split_axis=0, concat_axis=0, tiled=T...  3.75 us
    pallas_call x1, Pallas kernels, finish(): pl.pallas_call(functools.partial(final_kernel, experts, folds), out_shape...  1.78 us
  transfers between devices with their start and end apart: 1, of which 1 were waited for; matrix products, arithmetic and copies ran while one was open for 0% of the time, Pallas kernels for 0%

profile of v2, /device:TPU:0, one launch (start us, length us, event | category | flops | bytes accessed | tf_op | source)
XLA Modules:
  0.0 79.4 jit_solution(8685142253433143525)
XLA Ops:
  0.0 0.0 copy-start
  0.0 0.8 %copy.24.ids_ref = s32[24,2]{1,0:T(8,128)S(1)} copy(s32[24,2]{0,1:T(2,128)} %param.6) | data formatting | bytes 384 | tf_op args[1]
  0.8 0.1 eq.28
  0.9 0.1 fusion
  1.0 0.1 reduce_window_sum.11
  1.0 0.2 select_reduce_fusion
  1.2 0.1 reduce_sum.21
  1.3 0.1 copy.23
  1.4 0.7 multiply_add_fusion
  2.1 0.1 convert_reduce_fusion
  2.2 0.0 copy-done
  2.2 0.3 convolution_convert_fusion
  2.5 0.1 broadcast_in_dim.8
  2.6 0.2 broadcast_in_dim.9
  2.8 36.6 %all_to_all.10 = bf16[16,288,128]{2,1,0:T(8,128)(2,1)S(1)} all-to-all(bf16[16,288,128]{2,1,0:T(8,128)(2,1)S(1)} %bitcast.6), channel_id=1, replica_groups=mesh['groups'=2,'et'=4,'ep'=4] {'et','ep'}, dimensions={0} | all-to-all | bytes 2359296 | tf_op jit(solution)/shard_map/all_to_all | solution.py:31
  39.4 0.5 reshape.18.x_ref
  40.0 0.0 copy-start.1
  40.0 4.6 %copy-done.1 = bf16[1,3072,2048]{2,1,0:T(8,128)(2,1)S(1)} copy-done((bf16[1,3072,2048]{2,1,0:T(8,128)(2,1)S(1)}, bf16[1,3072,2048]{2,1,0:T(8,128)(2,1)}, u32[]{:S(2)}) %copy-start.1) | copy-done | bytes 12582936
  44.5 0.0 copy-start.2
  44.5 4.6 %copy-done.2 = bf16[1,3072,2048]{2,1,0:T(8,128)(2,1)S(1)} copy-done((bf16[1,3072,2048]{2,1,0:T(8,128)(2,1)S(1)}, bf16[1,3072,2048]{2,1,0:T(8,128)(2,1)}, u32[]{:S(2)}) %copy-start.2) | copy-done | bytes 12582936
  49.1 6.0 %shard_map.55 = bf16[16,48,512]{2,1,0:T(8,128)(2,1)} custom-call(bf16[192,3072]{1,0:T(8,128)(2,1)S(1)} %reshape.18.x_ref, bf16[3072,2048]{1,0:T(8,128)(2,1)S(1)} %bitcast.4, bf16[3072,2048]{1,0:T(8,128)(2,1)S(1)} %bitcast.5), custom_call_target="tpu_custom_call" | custom-call | flops 4831838208 | bytes 25165824 | tf_op jit(solution)/shard_map/pallas_call | solution.py:55
  55.1 0.0 copy-start.3
  55.1 3.7 %all-to-all-start.1 = ((bf16[16,48,512]{2,1,0:T(8,128)(2,1)}), bf16[16,48,512]{2,1,0:T(8,128)(2,1)S(1)}, u32[]{:S(2)}, u32[]{:S(2)}) async-start(bf16[16,48,512]{2,1,0:T(8,128)(2,1)} %shard_map.55), calls=%async_computation.1 | async-start | bytes 1572864 | tf_op jit(solution)/shard_map/all_to_all | solution.py:31
  58.9 0.0 copy-done.3
  58.9 0.1 copy.25.weights_ref
  59.0 18.6 %all-to-all-done.1.recv_ref = bf16[16,48,512]{2,1,0:T(8,128)(2,1)S(1)} async-done(((bf16[16,48,512]{2,1,0:T(8,128)(2,1)}), bf16[16,48,512]{2,1,0:T(8,128)(2,1)S(1)}, u32[]{:S(2)}, u32[]{:S(2)}) %all-to-all-start.1) | async-done | bytes 786464 | tf_op jit(solution)/shard_map/all_to_all | solution.py:31
  77.6 1.8 %shard_map.56 = bf16[24,2,8192]{2,1,0:T(2,128)(2,1)} custom-call(s32[24,2]{1,0:T(8,128)S(1)} %copy.24.ids_ref, f32[24,2]{1,0:T(8,128)S(1)} %copy.25.weights_ref, bf16[16,48,512]{2,1,0:T(8,128)(2,1)S(1)} %all-to-all-done.1.recv_ref), custom_call_target="tpu_custom_call" | custom-call | tf_op jit(solution)/shard_map/pallas_call | solution.py:134
Async XLA Ops:
  0.0 2.2 %copy-start = (bf16[24,3072]{1,0:T(8,128)(2,1)S(1)}, bf16[24,3072]{1,0:T(8,128)(2,1)}, u32[]{:S(2)}) copy-start(bf16[24,3072]{1,0:T(8,128)(2,1)} %param.5) | copy-start | bytes 442372
  40.0 4.6 %copy-start.1 = (bf16[1,3072,2048]{2,1,0:T(8,128)(2,1)S(1)}, bf16[1,3072,2048]{2,1,0:T(8,128)(2,1)}, u32[]{:S(2)}) copy-start(bf16[1,3072,2048]{2,1,0:T(8,128)(2,1)} %param.8) | copy-start | bytes 37748740
  44.5 4.6 %copy-start.2 = (bf16[1,3072,2048]{2,1,0:T(8,128)(2,1)S(1)}, bf16[1,3072,2048]{2,1,0:T(8,128)(2,1)}, u32[]{:S(2)}) copy-start(bf16[1,3072,2048]{2,1,0:T(8,128)(2,1)} %param.9) | copy-start | bytes 37748740
  55.1 3.8 %copy-start.3 = (f32[24,2]{0,1:T(2,128)S(1)}, f32[24,2]{0,1:T(2,128)}, u32[]{:S(2)}) copy-start(f32[24,2]{0,1:T(2,128)} %param.7) | copy-start | bytes 580
  55.1 22.4 %all-to-all-start.1 = ((bf16[16,48,512]{2,1,0:T(8,128)(2,1)}), bf16[16,48,512]{2,1,0:T(8,128)(2,1)S(1)}, u32[]{:S(2)}, u32[]{:S(2)}) async-start(bf16[16,48,512]{2,1,0:T(8,128)(2,1)} %shard_map.55), calls=%async_computation.1 | async-start | bytes 1572864 | tf_op jit(solution)/shard_map/all_to_all | solution.py:31

commit v3 on v2

--- a/solution.py
+++ b/solution.py
@@ -35,36 +35,152 @@
     return jnp.dot(a, b, preferred_element_type=jnp.float32)
 
 
-def hidden_kernel(folds, x_ref, gate_ref, up_ref, out_ref, hidden_ref):
+def store_blocks(folds, hidden_ref, out_ref):
     peers = out_ref.shape[0]
     capacity = hidden_ref.shape[0] // peers
     span = hidden_ref.shape[1] // folds
-    gate_val = exact_dot(x_ref[...], gate_ref[...])
-    up_val = exact_dot(x_ref[...], up_ref[...])
-    hidden_ref[...] = gate_val / (1.0 + jnp.exp(-gate_val)) * up_val
     for peer in range(peers):
         rows = hidden_ref[peer * capacity : (peer + 1) * capacity, :]
         pieces = [rows[:, fold * span : (fold + 1) * span] for fold in range(folds)]
         out_ref[peer] = jnp.concatenate(pieces, axis=0).astype(out_ref.dtype)
 
 
-def hidden_blocks(x, gate_local, up_local, peers, folds):
-    rows, width = x.shape
-    units = gate_local.shape[1]
+def rows_of(ids_block, source, mine, experts, rows, tok_rows, capacity):
+    tall = ids_block.shape[0]
+    names = ids_block.astype(jnp.float32)
+    expert = mine.astype(jnp.float32)
+    named = (names[:, 0:1] == expert) | (names[:, 1:2] == expert)
+    later = lax.broadcasted_iota(jnp.int32, (tall, tall), 0)
+    earlier = lax.broadcasted_iota(jnp.int32, (tall, tall), 1)
+    lower = ((later > earlier) & (later // tok_rows == earlier // tok_rows)).astype(jnp.bfloat16)
+    flags = jnp.broadcast_to(named.astype(jnp.float32), (tall, 128)).astype(jnp.bfloat16)
+    before = exact_dot(lower, flags)[:, 0:1].astype(jnp.int32)
+    layer = lax.broadcasted_iota(jnp.int32, (tall, 1), 0) // tok_rows
+    target = jnp.where(named, (layer * experts + source) * capacity + before, -1)
+    return (lax.broadcasted_iota(jnp.int32, (tall, rows), 1) == target).astype(jnp.bfloat16)
+
+
+def transposed_dot(a, b):
+    return lax.dot_general(a, b, (((0,), (0,)), ((), ())), preferred_element_type=jnp.float32)
+
+
+def weight_copies(weights, held, sems, start, step):
+    return [
+        [
+            pltpu.make_async_copy(
+                ref.at[pl.ds(start + part * step, step), :],
+                into.at[pl.ds(part * step, step), :],
+                sems.at[which, part],
+            )
+            for which, (ref, into) in enumerate(zip(weights, held))
+        ]
+        for part in range(held[0].shape[0] // step)
+    ]
+
+
+def first_kernel(step, tok_rows, capacity, experts, *refs):
+    blocks, (gate_hbm, up_hbm, gate_ref, up_ref, sel_ref, x_ref, gate_held, up_held, sems) = refs[:experts], refs[experts:]
+    copies = weight_copies((gate_hbm, up_hbm), (gate_held, up_held), sems, 0, step)
+    for pair in copies:
+        for copy in pair:
+            copy.start()
+    mine = lax.axis_index("ep")
+    rows = gate_ref.shape[0]
+    chosen = 0.0
+    for number, block in enumerate(blocks):
+        tall = block.shape[0]
+        sel = rows_of(block[:, :128], mine ^ number, mine, experts, rows, tok_rows, capacity)
+        sel_ref[number] = sel
+        chosen = chosen + transposed_dot(sel, block[:, 128:])
+    x_ref[...] = chosen.astype(x_ref.dtype)
+    for part, pair in enumerate(copies):
+        span = pl.ds(part * step, step)
+        for copy, held, ref in zip(pair, (gate_held, up_held), (gate_ref, up_ref)):
+            copy.wait()
+            product = exact_dot(x_ref[:, span], held[span, :])
+            ref[...] = product if part == 0 else ref[...] + product
+
+
+def second_kernel(step, start, folds, *refs):
+    experts = len(refs) - 11
+    blocks = refs[:experts]
+    sel_ref, gate_in, up_in, gate_hbm, up_hbm, out_ref, x_ref, gate_held, up_held, hidden_ref, sems = refs[experts:]
+    copies = weight_copies((gate_hbm, up_hbm), (gate_held, up_held), sems, start, step)
+    for pair in copies:
+        for copy in pair:
+            copy.start()
+    x_ref[...] = sum(transposed_dot(sel_ref[number], block[...]) for number, block in enumerate(blocks)).astype(x_ref.dtype)
+    sums = [gate_in[...], up_in[...]]
+    for part, pair in enumerate(copies):
+        span = pl.ds(part * step, step)
+        for which, (copy, held) in enumerate(zip(pair, (gate_held, up_held))):
+            copy.wait()
+            sums[which] = sums[which] + exact_dot(x_ref[:, span], held[span, :])
+    gate_val, up_val = sums
+    hidden_ref[...] = gate_val / (1.0 + jnp.exp(-gate_val)) * up_val
+    store_blocks(folds, hidden_ref, out_ref)
+
+
+def split_hidden(first_blocks, finish_blocks, gate_local, up_local, peers, capacity, tok_rows, folds):
+    width, units = gate_local.shape
+    experts = len(first_blocks)
+    rows = peers * capacity
+    tall = first_blocks[0].shape[0]
+    cut = first_blocks[0].shape[1] - 128
+    step = 256
     whole = pl.BlockSpec(memory_space=pltpu.VMEM)
+    outside = pl.BlockSpec(memory_space=pltpu.HBM)
+    params = pltpu.CompilerParams(vmem_limit_bytes=26 << 20)
+    kind = gate_local.dtype
+
+    def scratch(depth):
+        return [pltpu.VMEM((rows, depth), kind), pltpu.VMEM((depth, units), kind), pltpu.VMEM((depth, units), kind)]
+
+    def cost(depth, activations):
+        return pl.CostEstimate(flops=4 * rows * depth * units, bytes_accessed=4 * depth * units, transcendentals=activations)
+
+    gate_sum, up_sum, sel = pl.pallas_call(
+        functools.partial(first_kernel, step, tok_rows, capacity, experts),
+        out_shape=[jax.ShapeDtypeStruct((rows, units), jnp.float32)] * 2 + [jax.ShapeDtypeStruct((experts, tall, rows), kind)],
+        in_specs=[whole] * experts + [outside] * 2,
+        out_specs=[whole] * 3,
+        scratch_shapes=scratch(cut) + [pltpu.SemaphoreType.DMA((2, cut // step))],
+        compiler_params=params,
+        cost_estimate=cost(cut, 0),
+    )(*first_blocks, gate_local, up_local)
+    rest = width - cut
+    second_blocks, sel = finish_blocks(sel)
     return pl.pallas_call(
-        functools.partial(hidden_kernel, folds),
-        out_shape=jax.ShapeDtypeStruct((peers, rows // peers * folds, units // folds), x.dtype),
-        in_specs=[whole] * 3,
+        functools.partial(second_kernel, step, cut, folds),
+        out_shape=jax.ShapeDtypeStruct((peers, capacity * folds, units // folds), kind),
+        in_specs=[whole] * (experts + 3) + [outside] * 2,
         out_specs=whole,
-        scratch_shapes=[pltpu.VMEM((rows, units), jnp.float32)],
-        compiler_params=pltpu.CompilerParams(vmem_limit_bytes=16 << 20),
-        cost_estimate=pl.CostEstimate(
-            flops=4 * rows * width * units,
-            bytes_accessed=4 * width * units,
-            transcendentals=rows * units,
-        ),
-    )(x, gate_local, up_local)
+        scratch_shapes=scratch(rest) + [pltpu.VMEM((rows, units), jnp.float32), pltpu.SemaphoreType.DMA((2, rest // step))],
+        compiler_params=params,
+        cost_estimate=cost(rest, rows * units),
+    )(*second_blocks, sel, gate_sum, up_sum, gate_local, up_local)
+
+
+def routed_by_columns(tokens, expert_ids, gate_local, up_local, peers, capacity, folds):
+    tok_rows, width = tokens.shape
+    cut = width // 2
+    ids = jnp.pad(expert_ids.astype(tokens.dtype), ((0, 0), (0, 126)))
+    packed = jnp.concatenate([ids, tokens], axis=1)
+    own = lax.all_gather(packed, "et", axis=0, tiled=True)
+
+    def swap(block, bit):
+        return lax.ppermute(block, "ep", [(i, i ^ bit) for i in range(4)])
+
+    part, later = own[:, : 128 + cut], own[:, 128 + cut :]
+    far, later_far = swap(part, 2), swap(later, 2)
+    later_near = swap(later, 1)
+
+    def finish_blocks(sel):
+        held, sel = lax.optimization_barrier((later_far, sel))
+        return [later, later_near, held, swap(held, 1)], sel
+
+    first_blocks = [part, swap(part, 1), far, swap(far, 1)]
+    return split_hidden(first_blocks, finish_blocks, gate_local, up_local, peers, capacity, tok_rows, folds)
 
 
 def picks_of(ids, experts, capacity, folds):
@@ -148,6 +264,10 @@
     capacity = tok_rows // 2
     gate_local = w_gate[0]
     up_local = w_up[0]
+    if experts == 4 and tensor_size == 4:
+        folds = 4
+        blocks = routed_by_columns(tokens, expert_ids, gate_local, up_local, peers, capacity, folds)
+        return finish(expert_ids, gate_weights, exchange(blocks), experts, folds)
     slot_pairs = place_slots(expert_ids, experts, capacity)
     selector = build_select(slot_pairs, experts * capacity)
     buffer = jnp.dot(selector, tokens, preferred_element_type=jnp.float32).astype(jnp.bfloat16)
@@ -155,10 +275,6 @@
     buffer = jnp.broadcast_to(buffer, (tensor_size,) + buffer.shape[1:])
     arrived = exchange(buffer.reshape(peers, capacity * width // 128, 128))
     units = gate_local.shape[1]
-    if peers <= 16:
-        folds = 4
-        blocks = hidden_blocks(arrived.reshape(peers * capacity, width), gate_local, up_local, peers, folds)
-        return finish(expert_ids, gate_weights, exchange(blocks), experts, folds)
     hidden = swiglu_rows(arrived.reshape(peers * capacity, width), gate_local, up_local)
     returned = exchange(hidden.reshape(peers, capacity * units // 128, 128))
     returned = returned.reshape(tensor_size, experts * capacity, units)

time: 79.7 us -> 75.2 us (0.944)
  blocking collectives: 36.6 us -> 18.8 us
  Pallas kernels: 7.82 us -> 15.2 us
  waiting for transfers between devices: 18.6 us -> 25.4 us
  local copies, waits for them, and re-layouts: 11.1 us -> 4.9 us
  starting transfers between devices: 3.75 us -> 8.91 us
    all_to_all x1 -> x0, blocking collectives: 36.6 us -> none  [exchange(): lax.all_to_all(blocks, ('et', 'ep'), split_axis=0, concat_axis=0, tiled=T...]
    all_gather x0 -> x1, blocking collectives: none -> 18.8 us  [routed_by_columns(): own = lax.all_gather(packed, 'et', axis=0, tiled=True)]
    pallas_call x1 -> x2, Pallas kernels: 6.04 us -> 13.4 us  [the longest x1 7.02 us: split_hidden(): pl.pallas_call(functools.partial(second_kernel, step, cut, folds), out_sh...]
    ppermute x0 -> x6, waiting for transfers between devices: none -> 6.84 us  [swap(): return lax.ppermute(block, 'ep', [(i, i ^ bit) for i in range(4)])]
    unnamed x10, local copies, waits for them, and re-layouts: 10 us -> 4.76 us
    ppermute x0 -> x6, starting transfers between devices: none -> 3.7 us  [swap(): return lax.ppermute(block, 'ep', [(i, i ^ bit) for i in range(4)])]
    all_to_all x1, starting transfers between devices: 3.75 us -> 5.22 us  [exchange(): lax.all_to_all(blocks, ('et', 'ep'), split_axis=0, concat_axis=0, tiled=T...]
    concatenate x0 -> x1, other arithmetic: none -> 0.92 us  [routed_by_columns(): packed = jnp.concatenate([ids, tokens], axis=1)]
  transfers between devices with their start and end apart: 1 -> 7, of which waited for: 1 -> 3; matrix products, arithmetic and copies ran while one was open for 0% -> 0% of each run, Pallas kernels for 0% -> 9%
where the time goes in v3:
time: 75.2 us; the launch traced here: 74.8 us
  waiting for transfers between devices  25.4 us (34%)
  blocking collectives  18.8 us (25%)
  Pallas kernels  15.2 us (20%)
  starting transfers between devices  8.91 us (12%)
  local copies, waits for them, and re-layouts  4.9 us (7%)
  other arithmetic  1.61 us (2%)
    all_gather x1, blocking collectives, routed_by_columns(): own = lax.all_gather(packed, 'et', axis=0, tiled=True)  18.8 us
    all_to_all x1, waiting for transfers between devices, exchange(): lax.all_to_all(blocks, ('et', 'ep'), split_axis=0, concat_axis=0, tiled=T...  18.5 us
    pallas_call x1, Pallas kernels, split_hidden(): pl.pallas_call(functools.partial(second_kernel, step, cut, folds), out_sh...  7.02 us
    ppermute x6, waiting for transfers between devices, swap(): return lax.ppermute(block, 'ep', [(i, i ^ bit) for i in range(4)])  6.84 us
    pallas_call x1, Pallas kernels, split_hidden(): pl.pallas_call(functools.partial(first_kernel, step, tok_rows, capacity,...  6.39 us
    all_to_all x1, starting transfers between devices, exchange(): lax.all_to_all(blocks, ('et', 'ep'), split_axis=0, concat_axis=0, tiled=T...  5.22 us
    unnamed x10, local copies, waits for them, and re-layouts  4.76 us
    ppermute x6, starting transfers between devices, swap(): return lax.ppermute(block, 'ep', [(i, i ^ bit) for i in range(4)])  3.7 us
  transfers between devices with their start and end apart: 7, of which 3 were waited for; matrix products, arithmetic and copies ran while one was open for 0% of the time, Pallas kernels for 9%

profile of v3, /device:TPU:0, one launch (start us, length us, event | category | flops | bytes accessed | tf_op | source)
XLA Modules:
  0.0 74.8 jit_solution(227086192011415224)
XLA Ops:
  0.0 0.7 convert_element_type.5
  0.7 0.1 copy.9
  0.8 0.9 %fusion.1 = bf16[24,3200]{1,0:T(8,128)(2,1)S(1)} fusion(bf16[24,2]{1,0:T(8,128)(2,1)S(1)} %copy.9, bf16[24,3072]{1,0:T(8,128)(2,1)} %param.5), kind=kLoop, calls=%fused_computation.2 | loop fusion | flops 460800 | bytes 301152 | tf_op jit(solution)/shard_map/concatenate | solution.py:168
  1.7 18.8 %all_gather.3 = bf16[96,3200]{1,0:T(8,128)(2,1)S(1)} all-gather(bf16[24,3200]{1,0:T(8,128)(2,1)S(1)} %fusion.1), channel_id=1, replica_groups=mesh['groups'=2,'et'=4,'ep'=4] {'et'}, dimensions={0}, use_global_device_ids=true | all-gather | bytes 768000 | tf_op jit(solution)/shard_map/all_gather | solution.py:169
  20.5 1.6 %collective-permute-start.3 = (bf16[96,1664]{1,0:T(8,128)(2,1)S(1)}, bf16[96,1664]{1,0:T(8,128)(2,1)S(1)}, u32[]{:S(2)}, u32[]{:S(2)}) collective-permute-start(bf16[96,1664]{1,0:T(8,128)(2,1)S(1)} %slice.9.refs_0_), channel_id=1, source_target_pairs={{0,2},{1,3},{2,0},{3,1},{4,6},{5,7},{6,4},{7,5},{8,10},{9,11},{10,... | collective-permute-start | bytes 958472 | tf_op jit(solution)/shard_map/ppermute | solution.py:172
  22.1 0.0 collective-permute-start.2
  22.1 5.5 %collective-permute-done.3.refs_2_ = bf16[96,1664]{1,0:T(8,128)(2,1)S(1)} collective-permute-done((bf16[96,1664]{1,0:T(8,128)(2,1)S(1)}, bf16[96,1664]{1,0:T(8,128)(2,1)S(1)}, u32[]{:S(2)}, u32[]{:S(2)}) %collective-permute-start.3) | collective-permute-done | bytes 319520 | tf_op jit(solution)/shard_map/ppermute | solution.py:172
  27.6 0.0 collective-permute-start.4
  27.6 1.6 %collective-permute-start.1 = (bf16[96,1536]{1,0:T(8,128)(2,1)S(1)}, bf16[96,1536]{1,0:T(8,128)(2,1)S(1)}, u32[]{:S(2)}, u32[]{:S(2)}) collective-permute-start(bf16[96,1536]{1,0:T(8,128)(2,1)S(1)} %slice.8.refs_0_), channel_id=1, source_target_pairs={{0,2},{1,3},{2,0},{3,1},{4,6},{5,7},{6,4},{7,5},{8,10},{9,11},{10,... | collective-permute-start | bytes 884744 | tf_op jit(solution)/shard_map/ppermute | solution.py:172
  29.2 0.2 collective-permute-start
  29.4 0.0 collective-permute-done.2.refs_1_
  29.4 0.0 collective-permute-done.4.refs_3_
  29.4 0.0 copy-start
  29.4 4.6 %copy-done = bf16[1,3072,2048]{2,1,0:T(8,128)(2,1)S(1)} copy-done((bf16[1,3072,2048]{2,1,0:T(8,128)(2,1)S(1)}, bf16[1,3072,2048]{2,1,0:T(8,128)(2,1)}, u32[]{:S(2)}) %copy-start) | copy-done | bytes 12582936
  34.0 0.0 copy-start.1
  34.0 6.4 %shard_map.55 = (f32[192,2048]{1,0:T(8,128)S(1)}, f32[192,2048]{1,0:T(8,128)S(1)}, bf16[4,96,192]{2,1,0:T(8,128)(2,1)S(1)}) custom-call(bf16[96,1664]{1,0:T(8,128)(2,1)S(1)} %slice.9.refs_0_, bf16[96,1664]{1,0:T(8,128)(2,1)S(1)} %collective-permute-done.2.refs_1_, bf16[96,1664]{1,0:T(8,128)(2,1)S(1)} %collective-permute-done.3.refs_2_, ...), custom_call_target="tpu_custom_call" | custom-call | flops 2415919104 | bytes 12582912 | tf_op jit(solution)/shard_map/pallas_call | solution.py:142
  40.4 0.0 collective-permute-done.1.refs_2_
  40.4 0.4 collective-permute-start.5
  40.8 0.0 collective-permute-done.refs_1_
  40.8 1.3 %collective-permute-done.5.refs_3_ = bf16[96,1536]{1,0:T(8,128)(2,1)S(1)} collective-permute-done((bf16[96,1536]{1,0:T(8,128)(2,1)S(1)}, bf16[96,1536]{1,0:T(8,128)(2,1)S(1)}, u32[]{:S(2)}, u32[]{:S(2)}) %collective-permute-start.5) | collective-permute-done | bytes 294944 | tf_op jit(solution)/shard_map/ppermute | solution.py:172
  42.1 0.0 copy-done.1
  42.1 0.0 copy-start.2
  42.1 0.0 copy-start.3
  42.1 7.0 %shard_map.56 = bf16[16,48,512]{2,1,0:T(8,128)(2,1)} custom-call(bf16[96,1536]{1,0:T(8,128)(2,1)S(1)} %slice.8.refs_0_, bf16[96,1536]{1,0:T(8,128)(2,1)S(1)} %collective-permute-done.refs_1_, bf16[96,1536]{1,0:T(8,128)(2,1)S(1)} %collective-permute-done.1.refs_2_, bf16[96,1536]{1,0:T(8,128)(2,1)S(1)} %collective-permute-done.5.refs_3_, ...), custom_call_target="tpu_custom_call" | custom-call | flops 2415919104 | bytes 12582912 | tf_op jit(solution)/shard_map/pallas_call | solution.py:153
  49.1 5.2 %all-to-all-start = ((bf16[16,48,512]{2,1,0:T(8,128)(2,1)}), bf16[16,48,512]{2,1,0:T(8,128)(2,1)S(1)}, u32[]{:S(2)}, u32[]{:S(2)}) async-start(bf16[16,48,512]{2,1,0:T(8,128)(2,1)} %shard_map.56), calls=%async_computation | async-start | bytes 1572864 | tf_op jit(solution)/shard_map/all_to_all | solution.py:31
  54.3 0.0 copy-done.2
  54.3 0.1 copy.10.ids_ref
  54.4 0.0 copy-done.3
  54.4 0.1 copy.11.weights_ref
  54.5 18.5 %all-to-all-done.recv_ref = bf16[16,48,512]{2,1,0:T(8,128)(2,1)S(1)} async-done(((bf16[16,48,512]{2,1,0:T(8,128)(2,1)}), bf16[16,48,512]{2,1,0:T(8,128)(2,1)S(1)}, u32[]{:S(2)}, u32[]{:S(2)}) %all-to-all-start) | async-done | bytes 786464 | tf_op jit(solution)/shard_map/all_to_all | solution.py:31
  73.0 1.8 %shard_map.57 = bf16[24,2,8192]{2,1,0:T(2,128)(2,1)} custom-call(s32[24,2]{1,0:T(8,128)S(1)} %copy.10.ids_ref, f32[24,2]{1,0:T(8,128)S(1)} %copy.11.weights_ref, bf16[16,48,512]{2,1,0:T(8,128)(2,1)S(1)} %all-to-all-done.recv_ref), custom_call_target="tpu_custom_call" | custom-call | tf_op jit(solution)/shard_map/pallas_call | solution.py:250
  (2 shorter events, 0.0 us)
Async XLA Ops:
  20.5 7.1 %collective-permute-start.3 = (bf16[96,1664]{1,0:T(8,128)(2,1)S(1)}, bf16[96,1664]{1,0:T(8,128)(2,1)S(1)}, u32[]{:S(2)}, u32[]{:S(2)}) collective-permute-start(bf16[96,1664]{1,0:T(8,128)(2,1)S(1)} %slice.9.refs_0_), channel_id=1, source_target_pairs={{0,2},{1,3},{2,0},{3,1},{4,6},{5,7},{6,4},{7,5},{8,10},{9,11},{10,... | collective-permute-start | bytes 958472 | tf_op jit(solution)/shard_map/ppermute | solution.py:172
  22.1 7.4 %collective-permute-start.2 = (bf16[96,1664]{1,0:T(8,128)(2,1)S(1)}, bf16[96,1664]{1,0:T(8,128)(2,1)S(1)}, u32[]{:S(2)}, u32[]{:S(2)}) collective-permute-start(bf16[96,1664]{1,0:T(8,128)(2,1)S(1)} %slice.9.refs_0_), channel_id=1, source_target_pairs={{0,1},{1,0},{2,3},{3,2},{4,5},{5,4},{6,7},{7,6},{8,9},{9,8},{10,11... | collective-permute-start | bytes 958472 | tf_op jit(solution)/shard_map/ppermute | solution.py:172
  27.6 1.8 %collective-permute-start.4 = (bf16[96,1664]{1,0:T(8,128)(2,1)S(1)}, bf16[96,1664]{1,0:T(8,128)(2,1)S(1)}, u32[]{:S(2)}, u32[]{:S(2)}) collective-permute-start(bf16[96,1664]{1,0:T(8,128)(2,1)S(1)} %collective-permute-done.3.refs_2_), channel_id=1, source_target_pairs={{0,1},{1,0},{2,3},{3,2},{4,5},{5,4},{6,7},{7,6},{8,9},{9,8},{10,11... | collective-permute-start | bytes 958472 | tf_op jit(solution)/shard_map/ppermute | solution.py:172
  27.6 12.8 %collective-permute-start.1 = (bf16[96,1536]{1,0:T(8,128)(2,1)S(1)}, bf16[96,1536]{1,0:T(8,128)(2,1)S(1)}, u32[]{:S(2)}, u32[]{:S(2)}) collective-permute-start(bf16[96,1536]{1,0:T(8,128)(2,1)S(1)} %slice.8.refs_0_), channel_id=1, source_target_pairs={{0,2},{1,3},{2,0},{3,1},{4,6},{5,7},{6,4},{7,5},{8,10},{9,11},{10,... | collective-permute-start | bytes 884744 | tf_op jit(solution)/shard_map/ppermute | solution.py:172
  29.2 11.6 %collective-permute-start = (bf16[96,1536]{1,0:T(8,128)(2,1)S(1)}, bf16[96,1536]{1,0:T(8,128)(2,1)S(1)}, u32[]{:S(2)}, u32[]{:S(2)}) collective-permute-start(bf16[96,1536]{1,0:T(8,128)(2,1)S(1)} %slice.8.refs_0_), channel_id=1, source_target_pairs={{0,1},{1,0},{2,3},{3,2},{4,5},{5,4},{6,7},{7,6},{8,9},{9,8},{10,11... | collective-permute-start | bytes 884744 | tf_op jit(solution)/shard_map/ppermute | solution.py:172
  29.4 4.6 %copy-start = (bf16[1,3072,2048]{2,1,0:T(8,128)(2,1)S(1)}, bf16[1,3072,2048]{2,1,0:T(8,128)(2,1)}, u32[]{:S(2)}) copy-start(bf16[1,3072,2048]{2,1,0:T(8,128)(2,1)} %param.8) | copy-start | bytes 37748740
  34.0 8.1 %copy-start.1 = (bf16[1,3072,2048]{2,1,0:T(8,128)(2,1)S(1)}, bf16[1,3072,2048]{2,1,0:T(8,128)(2,1)}, u32[]{:S(2)}) copy-start(bf16[1,3072,2048]{2,1,0:T(8,128)(2,1)} %param.8) | copy-start | bytes 37748740
  40.4 1.6 %collective-permute-start.5 = (bf16[96,1536]{1,0:T(8,128)(2,1)S(1)}, bf16[96,1536]{1,0:T(8,128)(2,1)S(1)}, u32[]{:S(2)}, u32[]{:S(2)}) collective-permute-start(bf16[96,1536]{1,0:T(8,128)(2,1)S(1)} %collective-permute-done.1.refs_2_), channel_id=1, source_target_pairs={{0,1},{1,0},{2,3},{3,2},{4,5},{5,4},{6,7},{7,6},{8,9},{9,8},{10,11... | collective-permute-start | bytes 884744 | tf_op jit(solution)/shard_map/ppermute | solution.py:172
  42.1 12.3 %copy-start.2 = (s32[24,2]{0,1:T(2,128)S(1)}, s32[24,2]{0,1:T(2,128)}, u32[]{:S(2)}) copy-start(s32[24,2]{0,1:T(2,128)} %param.6) | copy-start | bytes 580
  42.1 12.4 %copy-start.3 = (f32[24,2]{0,1:T(2,128)S(1)}, f32[24,2]{0,1:T(2,128)}, u32[]{:S(2)}) copy-start(f32[24,2]{0,1:T(2,128)} %param.7) | copy-start | bytes 580
  49.1 23.9 %all-to-all-start = ((bf16[16,48,512]{2,1,0:T(8,128)(2,1)}), bf16[16,48,512]{2,1,0:T(8,128)(2,1)S(1)}, u32[]{:S(2)}, u32[]{:S(2)}) async-start(bf16[16,48,512]{2,1,0:T(8,128)(2,1)} %shard_map.56), calls=%async_computation | async-start | bytes 1572864 | tf_op jit(solution)/shard_map/all_to_all | solution.py:31

commit v4 on v3

--- a/solution.py
+++ b/solution.py
@@ -130,7 +130,7 @@
     step = 256
     whole = pl.BlockSpec(memory_space=pltpu.VMEM)
     outside = pl.BlockSpec(memory_space=pltpu.HBM)
-    params = pltpu.CompilerParams(vmem_limit_bytes=26 << 20)
+    params = pltpu.CompilerParams(vmem_limit_bytes=48 << 20)
     kind = gate_local.dtype
 
     def scratch(depth):

time: 75.2 us -> 71.9 us (0.956)
  local copies, waits for them, and re-layouts: 4.9 us -> 0.32 us
  waiting for transfers between devices: 25.4 us -> 26.5 us
    unnamed x10 -> x6, local copies, waits for them, and re-layouts: 4.76 us -> 0.18 us
    ppermute x6, waiting for transfers between devices: 6.84 us -> 7.94 us  [swap(): return lax.ppermute(block, 'ep', [(i, i ^ bit) for i in range(4)])]
  transfers between devices with their start and end apart: 7 -> 7, of which waited for: 3 -> 4; matrix products, arithmetic and copies ran while one was open for 0% -> 0% of each run, Pallas kernels for 9% -> 10%
where the time goes in v4:
time: 71.9 us; the launch traced here: 71.6 us
  waiting for transfers between devices  26.5 us (37%)
  blocking collectives  18.8 us (26%)
  Pallas kernels  15.6 us (22%)
  starting transfers between devices  8.76 us (12%)
  other arithmetic  1.61 us (2%)
    all_gather x1, blocking collectives, routed_by_columns(): own = lax.all_gather(packed, 'et', axis=0, tiled=True)  18.8 us
    all_to_all x1, waiting for transfers between devices, exchange(): lax.all_to_all(blocks, ('et', 'ep'), split_axis=0, concat_axis=0, tiled=T...  18.5 us
    ppermute x6, waiting for transfers between devices, swap(): return lax.ppermute(block, 'ep', [(i, i ^ bit) for i in range(4)])  7.94 us
    pallas_call x1, Pallas kernels, split_hidden(): pl.pallas_call(functools.partial(second_kernel, step, cut, folds), out_sh...  6.95 us
    pallas_call x1, Pallas kernels, split_hidden(): pl.pallas_call(functools.partial(first_kernel, step, tok_rows, capacity,...  6.86 us
    all_to_all x1, starting transfers between devices, exchange(): lax.all_to_all(blocks, ('et', 'ep'), split_axis=0, concat_axis=0, tiled=T...  5.41 us
    ppermute x6, starting transfers between devices, swap(): return lax.ppermute(block, 'ep', [(i, i ^ bit) for i in range(4)])  3.35 us
    pallas_call x1, Pallas kernels, finish(): pl.pallas_call(functools.partial(final_kernel, experts, folds), out_shape...  1.78 us
  transfers between devices with their start and end apart: 7, of which 4 were waited for; matrix products, arithmetic and copies ran while one was open for 0% of the time, Pallas kernels for 10%

profile of v4, /device:TPU:0, one launch (start us, length us, event | category | flops | bytes accessed | tf_op | source)
XLA Modules:
  0.0 71.6 jit_solution(16747645173243414679)
XLA Ops:
  0.0 0.7 convert_element_type.5
  0.7 0.1 copy.9
  0.8 0.9 %fusion.1 = bf16[24,3200]{1,0:T(8,128)(2,1)S(1)} fusion(bf16[24,2]{1,0:T(8,128)(2,1)S(1)} %copy.9, bf16[24,3072]{1,0:T(8,128)(2,1)} %param.5), kind=kLoop, calls=%fused_computation.2 | loop fusion | flops 460800 | bytes 301152 | tf_op jit(solution)/shard_map/concatenate | solution.py:168
  1.7 18.8 %all_gather.3 = bf16[96,3200]{1,0:T(8,128)(2,1)S(1)} all-gather(bf16[24,3200]{1,0:T(8,128)(2,1)S(1)} %fusion.1), channel_id=1, replica_groups=mesh['groups'=2,'et'=4,'ep'=4] {'et'}, dimensions={0}, use_global_device_ids=true | all-gather | bytes 768000 | tf_op jit(solution)/shard_map/all_gather | solution.py:169
  20.5 1.6 %collective-permute-start.3 = (bf16[96,1664]{1,0:T(8,128)(2,1)S(1)}, bf16[96,1664]{1,0:T(8,128)(2,1)S(1)}, u32[]{:S(2)}, u32[]{:S(2)}) collective-permute-start(bf16[96,1664]{1,0:T(8,128)(2,1)S(1)} %slice.9.refs_0_), channel_id=1, source_target_pairs={{0,2},{1,3},{2,0},{3,1},{4,6},{5,7},{6,4},{7,5},{8,10},{9,11},{10,... | collective-permute-start | bytes 958472 | tf_op jit(solution)/shard_map/ppermute | solution.py:172
  22.1 0.0 collective-permute-start.2
  22.1 5.5 %collective-permute-done.3.refs_2_ = bf16[96,1664]{1,0:T(8,128)(2,1)S(1)} collective-permute-done((bf16[96,1664]{1,0:T(8,128)(2,1)S(1)}, bf16[96,1664]{1,0:T(8,128)(2,1)S(1)}, u32[]{:S(2)}, u32[]{:S(2)}) %collective-permute-start.3) | collective-permute-done | bytes 319520 | tf_op jit(solution)/shard_map/ppermute | solution.py:172
  27.6 0.0 collective-permute-start.4
  27.6 1.6 %collective-permute-start.1 = (bf16[96,1536]{1,0:T(8,128)(2,1)S(1)}, bf16[96,1536]{1,0:T(8,128)(2,1)S(1)}, u32[]{:S(2)}, u32[]{:S(2)}) collective-permute-start(bf16[96,1536]{1,0:T(8,128)(2,1)S(1)} %slice.8.refs_0_), channel_id=1, source_target_pairs={{0,2},{1,3},{2,0},{3,1},{4,6},{5,7},{6,4},{7,5},{8,10},{9,11},{10,... | collective-permute-start | bytes 884744 | tf_op jit(solution)/shard_map/ppermute | solution.py:172
  29.2 0.2 collective-permute-start
  29.4 0.0 collective-permute-done.2.refs_1_
  29.4 0.0 collective-permute-done.4.refs_3_
  29.4 6.9 %shard_map.55 = (f32[192,2048]{1,0:T(8,128)S(1)}, f32[192,2048]{1,0:T(8,128)S(1)}, bf16[4,96,192]{2,1,0:T(8,128)(2,1)S(1)}) custom-call(bf16[96,1664]{1,0:T(8,128)(2,1)S(1)} %slice.9.refs_0_, bf16[96,1664]{1,0:T(8,128)(2,1)S(1)} %collective-permute-done.2.refs_1_, bf16[96,1664]{1,0:T(8,128)(2,1)S(1)} %collective-permute-done.3.refs_2_, ...), custom_call_target="tpu_custom_call" | custom-call | flops 2415919104 | bytes 12582912 | tf_op jit(solution)/shard_map/pallas_call | solution.py:142
  36.3 0.8 %collective-permute-done.1.refs_2_ = bf16[96,1536]{1,0:T(8,128)(2,1)S(1)} collective-permute-done((bf16[96,1536]{1,0:T(8,128)(2,1)S(1)}, bf16[96,1536]{1,0:T(8,128)(2,1)S(1)}, u32[]{:S(2)}, u32[]{:S(2)}) %collective-permute-start.1) | collective-permute-done | bytes 294944 | tf_op jit(solution)/shard_map/ppermute | solution.py:172
  37.1 0.0 collective-permute-start.5
  37.1 0.0 collective-permute-done.refs_1_
  37.1 1.6 %collective-permute-done.5.refs_3_ = bf16[96,1536]{1,0:T(8,128)(2,1)S(1)} collective-permute-done((bf16[96,1536]{1,0:T(8,128)(2,1)S(1)}, bf16[96,1536]{1,0:T(8,128)(2,1)S(1)}, u32[]{:S(2)}, u32[]{:S(2)}) %collective-permute-start.5) | collective-permute-done | bytes 294944 | tf_op jit(solution)/shard_map/ppermute | solution.py:172
  38.7 0.0 copy-start
  38.7 0.0 copy-start.1
  38.7 7.0 %shard_map.56 = bf16[16,48,512]{2,1,0:T(8,128)(2,1)} custom-call(bf16[96,1536]{1,0:T(8,128)(2,1)S(1)} %slice.8.refs_0_, bf16[96,1536]{1,0:T(8,128)(2,1)S(1)} %collective-permute-done.refs_1_, bf16[96,1536]{1,0:T(8,128)(2,1)S(1)} %collective-permute-done.1.refs_2_, bf16[96,1536]{1,0:T(8,128)(2,1)S(1)} %collective-permute-done.5.refs_3_, ...), custom_call_target="tpu_custom_call" | custom-call | flops 2415919104 | bytes 12582912 | tf_op jit(solution)/shard_map/pallas_call | solution.py:153
  45.7 5.4 %all-to-all-start = ((bf16[16,48,512]{2,1,0:T(8,128)(2,1)}), bf16[16,48,512]{2,1,0:T(8,128)(2,1)S(1)}, u32[]{:S(2)}, u32[]{:S(2)}) async-start(bf16[16,48,512]{2,1,0:T(8,128)(2,1)} %shard_map.56), calls=%async_computation | async-start | bytes 1572864 | tf_op jit(solution)/shard_map/all_to_all | solution.py:31
  51.1 0.0 copy-done
  51.1 0.1 copy.10.ids_ref
  51.2 0.0 copy-done.1
  51.2 0.1 copy.11.weights_ref
  51.3 18.5 %all-to-all-done.recv_ref = bf16[16,48,512]{2,1,0:T(8,128)(2,1)S(1)} async-done(((bf16[16,48,512]{2,1,0:T(8,128)(2,1)}), bf16[16,48,512]{2,1,0:T(8,128)(2,1)S(1)}, u32[]{:S(2)}, u32[]{:S(2)}) %all-to-all-start) | async-done | bytes 786464 | tf_op jit(solution)/shard_map/all_to_all | solution.py:31
  69.8 1.8 %shard_map.57 = bf16[24,2,8192]{2,1,0:T(2,128)(2,1)} custom-call(s32[24,2]{1,0:T(8,128)S(1)} %copy.10.ids_ref, f32[24,2]{1,0:T(8,128)S(1)} %copy.11.weights_ref, bf16[16,48,512]{2,1,0:T(8,128)(2,1)S(1)} %all-to-all-done.recv_ref), custom_call_target="tpu_custom_call" | custom-call | tf_op jit(solution)/shard_map/pallas_call | solution.py:250
  (2 shorter events, 0.0 us)
Async XLA Ops:
  20.5 7.1 %collective-permute-start.3 = (bf16[96,1664]{1,0:T(8,128)(2,1)S(1)}, bf16[96,1664]{1,0:T(8,128)(2,1)S(1)}, u32[]{:S(2)}, u32[]{:S(2)}) collective-permute-start(bf16[96,1664]{1,0:T(8,128)(2,1)S(1)} %slice.9.refs_0_), channel_id=1, source_target_pairs={{0,2},{1,3},{2,0},{3,1},{4,6},{5,7},{6,4},{7,5},{8,10},{9,11},{10,... | collective-permute-start | bytes 958472 | tf_op jit(solution)/shard_map/ppermute | solution.py:172
  22.1 7.4 %collective-permute-start.2 = (bf16[96,1664]{1,0:T(8,128)(2,1)S(1)}, bf16[96,1664]{1,0:T(8,128)(2,1)S(1)}, u32[]{:S(2)}, u32[]{:S(2)}) collective-permute-start(bf16[96,1664]{1,0:T(8,128)(2,1)S(1)} %slice.9.refs_0_), channel_id=1, source_target_pairs={{0,1},{1,0},{2,3},{3,2},{4,5},{5,4},{6,7},{7,6},{8,9},{9,8},{10,11... | collective-permute-start | bytes 958472 | tf_op jit(solution)/shard_map/ppermute | solution.py:172
  27.6 1.8 %collective-permute-start.4 = (bf16[96,1664]{1,0:T(8,128)(2,1)S(1)}, bf16[96,1664]{1,0:T(8,128)(2,1)S(1)}, u32[]{:S(2)}, u32[]{:S(2)}) collective-permute-start(bf16[96,1664]{1,0:T(8,128)(2,1)S(1)} %collective-permute-done.3.refs_2_), channel_id=1, source_target_pairs={{0,1},{1,0},{2,3},{3,2},{4,5},{5,4},{6,7},{7,6},{8,9},{9,8},{10,11... | collective-permute-start | bytes 958472 | tf_op jit(solution)/shard_map/ppermute | solution.py:172
  27.6 9.5 %collective-permute-start.1 = (bf16[96,1536]{1,0:T(8,128)(2,1)S(1)}, bf16[96,1536]{1,0:T(8,128)(2,1)S(1)}, u32[]{:S(2)}, u32[]{:S(2)}) collective-permute-start(bf16[96,1536]{1,0:T(8,128)(2,1)S(1)} %slice.8.refs_0_), channel_id=1, source_target_pairs={{0,2},{1,3},{2,0},{3,1},{4,6},{5,7},{6,4},{7,5},{8,10},{9,11},{10,... | collective-permute-start | bytes 884744 | tf_op jit(solution)/shard_map/ppermute | solution.py:172
  29.2 7.9 %collective-permute-start = (bf16[96,1536]{1,0:T(8,128)(2,1)S(1)}, bf16[96,1536]{1,0:T(8,128)(2,1)S(1)}, u32[]{:S(2)}, u32[]{:S(2)}) collective-permute-start(bf16[96,1536]{1,0:T(8,128)(2,1)S(1)} %slice.8.refs_0_), channel_id=1, source_target_pairs={{0,1},{1,0},{2,3},{3,2},{4,5},{5,4},{6,7},{7,6},{8,9},{9,8},{10,11... | collective-permute-start | bytes 884744 | tf_op jit(solution)/shard_map/ppermute | solution.py:172
  37.1 1.6 %collective-permute-start.5 = (bf16[96,1536]{1,0:T(8,128)(2,1)S(1)}, bf16[96,1536]{1,0:T(8,128)(2,1)S(1)}, u32[]{:S(2)}, u32[]{:S(2)}) collective-permute-start(bf16[96,1536]{1,0:T(8,128)(2,1)S(1)} %collective-permute-done.1.refs_2_), channel_id=1, source_target_pairs={{0,1},{1,0},{2,3},{3,2},{4,5},{5,4},{6,7},{7,6},{8,9},{9,8},{10,11... | collective-permute-start | bytes 884744 | tf_op jit(solution)/shard_map/ppermute | solution.py:172
  38.7 12.4 %copy-start = (s32[24,2]{0,1:T(2,128)S(1)}, s32[24,2]{0,1:T(2,128)}, u32[]{:S(2)}) copy-start(s32[24,2]{0,1:T(2,128)} %param.6) | copy-start | bytes 580
  38.7 12.5 %copy-start.1 = (f32[24,2]{0,1:T(2,128)S(1)}, f32[24,2]{0,1:T(2,128)}, u32[]{:S(2)}) copy-start(f32[24,2]{0,1:T(2,128)} %param.7) | copy-start | bytes 580
  45.7 24.1 %all-to-all-start = ((bf16[16,48,512]{2,1,0:T(8,128)(2,1)}), bf16[16,48,512]{2,1,0:T(8,128)(2,1)S(1)}, u32[]{:S(2)}, u32[]{:S(2)}) async-start(bf16[16,48,512]{2,1,0:T(8,128)(2,1)} %shard_map.56), calls=%async_computation | async-start | bytes 1572864 | tf_op jit(solution)/shard_map/all_to_all | solution.py:31

commit v5 on v2

--- a/solution.py
+++ b/solution.py
@@ -35,36 +35,185 @@
     return jnp.dot(a, b, preferred_element_type=jnp.float32)
 
 
-def hidden_kernel(folds, x_ref, gate_ref, up_ref, out_ref, hidden_ref):
+def store_blocks(folds, hidden_ref, out_ref):
     peers = out_ref.shape[0]
     capacity = hidden_ref.shape[0] // peers
     span = hidden_ref.shape[1] // folds
-    gate_val = exact_dot(x_ref[...], gate_ref[...])
-    up_val = exact_dot(x_ref[...], up_ref[...])
-    hidden_ref[...] = gate_val / (1.0 + jnp.exp(-gate_val)) * up_val
     for peer in range(peers):
         rows = hidden_ref[peer * capacity : (peer + 1) * capacity, :]
         pieces = [rows[:, fold * span : (fold + 1) * span] for fold in range(folds)]
         out_ref[peer] = jnp.concatenate(pieces, axis=0).astype(out_ref.dtype)
 
 
-def hidden_blocks(x, gate_local, up_local, peers, folds):
-    rows, width = x.shape
+def rows_of(ids_block, source, mine, experts, rows, tok_rows, capacity):
+    tall = ids_block.shape[0]
+    names = ids_block.astype(jnp.float32)
+    expert = mine.astype(jnp.float32)
+    named = (names[:, 0:1] == expert) | (names[:, 1:2] == expert)
+    later = lax.broadcasted_iota(jnp.int32, (tall, tall), 0)
+    earlier = lax.broadcasted_iota(jnp.int32, (tall, tall), 1)
+    lower = ((later > earlier) & (later // tok_rows == earlier // tok_rows)).astype(jnp.bfloat16)
+    flags = jnp.broadcast_to(named.astype(jnp.float32), (tall, 128)).astype(jnp.bfloat16)
+    before = exact_dot(lower, flags)[:, 0:1].astype(jnp.int32)
+    layer = lax.broadcasted_iota(jnp.int32, (tall, 1), 0) // tok_rows
+    target = jnp.where(named, (layer * experts + source) * capacity + before, -1)
+    return (lax.broadcasted_iota(jnp.int32, (tall, rows), 1) == target).astype(jnp.bfloat16)
+
+
+def transposed_dot(a, b):
+    return lax.dot_general(a, b, (((0,), (0,)), ((), ())), preferred_element_type=jnp.float32)
+
+
+def weight_copies(weights, held, sems, start, step):
+    return [
+        pltpu.make_async_copy(
+            ref.at[pl.ds(start + part * step, step), :], into.at[pl.ds(part * step, step), :], sems.at[which, part]
+        )
+        for part in range(held[0].shape[0] // step)
+        for which, (ref, into) in enumerate(zip(weights, held))
+    ]
+
+
+def select_kernel(step, tok_rows, capacity, experts, *refs):
+    first, second, gate_hbm, up_hbm, sel_ref, chosen_ref, gate_held, up_held, sems = refs
+    copies = weight_copies((gate_hbm, up_hbm), (gate_held, up_held), sems, 0, step)
+    for copy in copies:
+        copy.start()
+    mine = lax.axis_index("ep")
+    rows = sel_ref.shape[2]
+    chosen = 0.0
+    for number, block in enumerate((first, second)):
+        sel = rows_of(block[:, :128], mine ^ number, mine, experts, rows, tok_rows, capacity)
+        sel_ref[number] = sel
+        chosen = chosen + transposed_dot(sel, block[:, 128:])
+    chosen_ref[...] = chosen.astype(chosen_ref.dtype)
+    for copy in copies:
+        copy.wait()
+
+
+def first_kernel(step, tok_rows, capacity, experts, *refs):
+    third, fourth, near_ref, gate_held, up_held, gate_hbm, up_hbm = refs[:7]
+    gate_ref, up_ref, sel_ref, gate_rest, up_rest, sems = refs[7:]
+    copies = weight_copies((gate_hbm, up_hbm), (gate_rest, up_rest), sems, gate_held.shape[0], step)
+    for copy in copies:
+        copy.start()
+    mine = lax.axis_index("ep")
+    rows = gate_ref.shape[0]
+    chosen = near_ref[...].astype(jnp.float32)
+    for number, block in enumerate((third, fourth)):
+        sel = rows_of(block[:, :128], mine ^ (2 + number), mine, experts, rows, tok_rows, capacity)
+        sel_ref[number] = sel
+        chosen = chosen + transposed_dot(sel, block[:, 128:])
+    x = chosen.astype(gate_held.dtype)
+    gate_ref[...] = exact_dot(x, gate_held[: x.shape[1], :])
+    up_ref[...] = exact_dot(x, up_held[: x.shape[1], :])
+    for copy in copies:
+        copy.wait()
+
+
+def second_kernel(start, folds, *refs):
+    blocks = refs[:4]
+    near_sel, far_sel, gate_in, up_in, gate_held, up_held, gate_rest, up_rest, out_ref, hidden_ref = refs[4:]
+    sels = [ref[number] for ref in (near_sel, far_sel) for number in range(2)]
+    x = sum(transposed_dot(sel, block[...]) for sel, block in zip(sels, blocks)).astype(out_ref.dtype)
+    middle = gate_held.shape[0] - start
+    sums = []
+    for held, rest, total in ((gate_held, gate_rest, gate_in), (up_held, up_rest, up_in)):
+        total = total[...] + exact_dot(x[:, middle:], rest[...])
+        if middle:
+            total = total + exact_dot(x[:, :middle], held[start:, :])
+        sums.append(total)
+    gate_val, up_val = sums
+    hidden_ref[...] = gate_val / (1.0 + jnp.exp(-gate_val)) * up_val
+    store_blocks(folds, hidden_ref, out_ref)
+
+
+WHOLE = pl.BlockSpec(memory_space=pltpu.VMEM)
+OUTSIDE = pl.BlockSpec(memory_space=pltpu.HBM)
+
+
+def local_kernel(kernel, out_shape, args, weights=(), flops=0, moved=0, scratch=(), limit=12):
+    return pl.pallas_call(
+        kernel,
+        out_shape=out_shape,
+        in_specs=[WHOLE] * len(args) + [OUTSIDE] * len(weights),
+        out_specs=jax.tree.map(lambda _: WHOLE, out_shape),
+        scratch_shapes=scratch,
+        compiler_params=pltpu.CompilerParams(vmem_limit_bytes=limit << 20),
+        cost_estimate=pl.CostEstimate(flops=flops, bytes_accessed=moved, transcendentals=0),
+    )(*args, *(pltpu.with_memory_space_constraint(w, pltpu.HBM) for w in weights))
+
+
+def pack_kernel(ids_ref, tokens_ref, out_ref):
+    names = ids_ref[...].astype(jnp.float32)
+    lane = lax.broadcasted_iota(jnp.int32, (names.shape[0], 128), 1)
+    out_ref[:, :128] = jnp.where(lane == 0, names[:, 0:1], names[:, 1:2]).astype(out_ref.dtype)
+    out_ref[:, 128:] = tokens_ref[...]
+
+
+def cut_kernel(in_ref, first_ref, second_ref):
+    cut = first_ref.shape[1]
+    first_ref[...] = in_ref[:, :cut]
+    second_ref[...] = in_ref[:, cut:]
+
+
+def routed_by_columns(tokens, expert_ids, gate_local, up_local, peers, capacity, folds):
+    tok_rows, width = tokens.shape
     units = gate_local.shape[1]
-    whole = pl.BlockSpec(memory_space=pltpu.VMEM)
-    return pl.pallas_call(
-        functools.partial(hidden_kernel, folds),
-        out_shape=jax.ShapeDtypeStruct((peers, rows // peers * folds, units // folds), x.dtype),
-        in_specs=[whole] * 3,
-        out_specs=whole,
-        scratch_shapes=[pltpu.VMEM((rows, units), jnp.float32)],
-        compiler_params=pltpu.CompilerParams(vmem_limit_bytes=16 << 20),
-        cost_estimate=pl.CostEstimate(
-            flops=4 * rows * width * units,
-            bytes_accessed=4 * width * units,
-            transcendentals=rows * units,
-        ),
-    )(x, gate_local, up_local)
+    experts = 4
+    rows = peers * capacity
+    cut = width // 2
+    kind = tokens.dtype
+
+    def swap(block, bit):
+        return lax.ppermute(block, "ep", [(i, i ^ bit) for i in range(experts)])
+
+    def product_flops(depth):
+        return 4 * rows * depth * units
+
+    packed = local_kernel(
+        pack_kernel, jax.ShapeDtypeStruct((tok_rows, 128 + width), kind), (expert_ids, tokens), moved=4 * tokens.size
+    )
+    own = lax.all_gather(packed, "et", axis=0, tiled=True)
+    tall = own.shape[0]
+    shapes = [jax.ShapeDtypeStruct((tall, 128 + cut), kind), jax.ShapeDtypeStruct((tall, width - cut), kind)]
+    part, later = local_kernel(cut_kernel, shapes, (own,), moved=4 * own.size)
+    far, later_far = swap(part, 2), swap(later, 2)
+    near, later_near = swap(part, 1), swap(later, 1)
+    sel_shape = jax.ShapeDtypeStruct((2, tall, rows), kind)
+    held = 2 * width // 3
+    step = 256
+    near_sel, near_rows, gate_held, up_held = local_kernel(
+        functools.partial(select_kernel, step, tok_rows, capacity, experts),
+        [sel_shape, jax.ShapeDtypeStruct((rows, cut), kind)] + [pltpu.VMEM((held, units), kind)] * 2,
+        (part, near),
+        (gate_local, up_local),
+        flops=4 * tall * rows * cut,
+        moved=4 * held * units,
+        scratch=[pltpu.SemaphoreType.DMA((2, held // step))],
+    )
+    far, near_rows = lax.optimization_barrier((far, near_rows))
+    rest = width - held
+    gate_sum, up_sum, far_sel, gate_rest, up_rest = local_kernel(
+        functools.partial(first_kernel, step, tok_rows, capacity, experts),
+        [jax.ShapeDtypeStruct((rows, units), jnp.float32)] * 2
+        + [sel_shape]
+        + [pltpu.VMEM((rest, units), kind)] * 2,
+        (far, swap(far, 1), near_rows, gate_held, up_held),
+        (gate_local, up_local),
+        flops=product_flops(cut),
+        moved=4 * rest * units,
+        scratch=[pltpu.SemaphoreType.DMA((2, rest // step))],
+    )
+    later_far, far_sel = lax.optimization_barrier((later_far, far_sel))
+    return local_kernel(
+        functools.partial(second_kernel, cut, folds),
+        jax.ShapeDtypeStruct((peers, capacity * folds, units // folds), kind),
+        (later, later_near, later_far, swap(later_far, 1), near_sel, far_sel)
+        + (gate_sum, up_sum, gate_held, up_held, gate_rest, up_rest),
+        flops=product_flops(width - cut),
+        scratch=[pltpu.VMEM((rows, units), jnp.float32)],
+    )
 
 
 def picks_of(ids, experts, capacity, folds):
@@ -148,6 +297,10 @@
     capacity = tok_rows // 2
     gate_local = w_gate[0]
     up_local = w_up[0]
+    if experts == 4 and tensor_size == 4:
+        folds = 4
+        blocks = routed_by_columns(tokens, expert_ids, gate_local, up_local, peers, capacity, folds)
+        return finish(expert_ids, gate_weights, exchange(blocks), experts, folds)
     slot_pairs = place_slots(expert_ids, experts, capacity)
     selector = build_select(slot_pairs, experts * capacity)
     buffer = jnp.dot(selector, tokens, preferred_element_type=jnp.float32).astype(jnp.bfloat16)
@@ -155,10 +308,6 @@
     buffer = jnp.broadcast_to(buffer, (tensor_size,) + buffer.shape[1:])
     arrived = exchange(buffer.reshape(peers, capacity * width // 128, 128))
     units = gate_local.shape[1]
-    if peers <= 16:
-        folds = 4
-        blocks = hidden_blocks(arrived.reshape(peers * capacity, width), gate_local, up_local, peers, folds)
-        return finish(expert_ids, gate_weights, exchange(blocks), experts, folds)
     hidden = swiglu_rows(arrived.reshape(peers * capacity, width), gate_local, up_local)
     returned = exchange(hidden.reshape(peers, capacity * units // 128, 128))
     returned = returned.reshape(tensor_size, experts * capacity, units)

time: 79.7 us -> 72.2 us (0.906)
  blocking collectives: 36.6 us -> 18.8 us
  Pallas kernels: 7.82 us -> 17.9 us
  local copies, waits for them, and re-layouts: 11.1 us -> 1.76 us
  waiting for transfers between devices: 18.6 us -> 24.6 us
  starting transfers between devices: 3.75 us -> 8.79 us
  other arithmetic: 1.1 us -> 0 us
    all_to_all x1 -> x0, blocking collectives: 36.6 us -> none  [exchange(): lax.all_to_all(blocks, ('et', 'ep'), split_axis=0, concat_axis=0, tiled=T...]
    all_gather x0 -> x1, blocking collectives: none -> 18.8 us  [routed_by_columns(): own = lax.all_gather(packed, 'et', axis=0, tiled=True)]
    pallas_call x1 -> x5, Pallas kernels: 6.04 us -> 16.1 us  [local_kernel(): pl.pallas_call(kernel, out_shape=out_shape, in_specs=[WHOLE] * len(args)...]
    unnamed x10 -> x6, local copies, waits for them, and re-layouts: 10 us -> 1.76 us
    ppermute x0 -> x6, waiting for transfers between devices: none -> 5.99 us  [swap(): return lax.ppermute(block, 'ep', [(i, i ^ bit) for i in range(experts)])]
    ppermute x0 -> x6, starting transfers between devices: none -> 3.35 us  [swap(): return lax.ppermute(block, 'ep', [(i, i ^ bit) for i in range(experts)])]
    all_to_all x1, starting transfers between devices: 3.75 us -> 5.44 us  [exchange(): lax.all_to_all(blocks, ('et', 'ep'), split_axis=0, concat_axis=0, tiled=T...]
  transfers between devices with their start and end apart: 1 -> 7, of which waited for: 1 -> 4; matrix products, arithmetic and copies ran while one was open for 0% -> 0% of each run, Pallas kernels for 0% -> 16%
where the time goes in v5:
time: 72.2 us; the launch traced here: 71.9 us
  waiting for transfers between devices  24.6 us (34%)
  blocking collectives  18.8 us (26%)
  Pallas kernels  17.9 us (25%)
  starting transfers between devices  8.79 us (12%)
  local copies, waits for them, and re-layouts  1.76 us (2%)
    all_gather x1, blocking collectives, routed_by_columns(): own = lax.all_gather(packed, 'et', axis=0, tiled=True)  18.8 us
    all_to_all x1, waiting for transfers between devices, exchange(): lax.all_to_all(blocks, ('et', 'ep'), split_axis=0, concat_axis=0, tiled=T...  18.6 us
    pallas_call x5, Pallas kernels, local_kernel(): pl.pallas_call(kernel, out_shape=out_shape, in_specs=[WHOLE] * len(args)...  16.1 us
    ppermute x6, waiting for transfers between devices, swap(): return lax.ppermute(block, 'ep', [(i, i ^ bit) for i in range(experts)])  5.99 us
    all_to_all x1, starting transfers between devices, exchange(): lax.all_to_all(blocks, ('et', 'ep'), split_axis=0, concat_axis=0, tiled=T...  5.44 us
    ppermute x6, starting transfers between devices, swap(): return lax.ppermute(block, 'ep', [(i, i ^ bit) for i in range(experts)])  3.35 us
    pallas_call x1, Pallas kernels, finish(): pl.pallas_call(functools.partial(final_kernel, experts, folds), out_shape...  1.78 us
    unnamed x6, local copies, waits for them, and re-layouts  1.76 us
  transfers between devices with their start and end apart: 7, of which 4 were waited for; matrix products, arithmetic and copies ran while one was open for 0% of the time, Pallas kernels for 16%

profile of v5, /device:TPU:0, one launch (start us, length us, event | category | flops | bytes accessed | tf_op | source)
XLA Modules:
  0.0 71.9 jit_solution(3566239045354041252)
XLA Ops:
  0.0 0.8 %copy.7.ids_ref = s32[24,2]{1,0:T(8,128)S(1)} copy(s32[24,2]{0,1:T(2,128)} %param.6) | data formatting | bytes 384 | tf_op args[1]
  0.8 0.0 copy-start
  0.8 0.9 %copy-done = bf16[24,3072]{1,0:T(8,128)(2,1)S(1)} copy-done((bf16[24,3072]{1,0:T(8,128)(2,1)S(1)}, bf16[24,3072]{1,0:T(8,128)(2,1)}, u32[]{:S(2)}) %copy-start) | copy-done | bytes 147480
  1.7 0.1 shard_map.55
  1.7 18.8 %all_gather.3.in_ref = bf16[96,3200]{1,0:T(8,128)(2,1)S(1)} all-gather(bf16[24,3200]{1,0:T(8,128)(2,1)S(1)} %shard_map.55), channel_id=1, replica_groups=mesh['groups'=2,'et'=4,'ep'=4] {'et'}, dimensions={0}, use_global_device_ids=true | all-gather | bytes 768000 | tf_op jit(solution)/shard_map/all_gather | solution.py:177
  20.5 0.1 collective-permute-start.3
  20.6 1.6 %collective-permute-start.2 = (bf16[96,1664]{1,0:T(8,128)(2,1)S(1)}, bf16[96,1664]{1,0:T(8,128)(2,1)S(1)}, u32[]{:S(2)}, u32[]{:S(2)}) collective-permute-start(bf16[96,1664]{1,0:T(8,128)(2,1)S(1)} %get-tuple-element.21.refs_0_), channel_id=1, source_target_pairs={{0,2},{1,3},{2,0},{3,1},{4,6},{5,7},{6,4},{7,5},{8,10},{9,11},{10,... | collective-permute-start | bytes 958472 | tf_op jit(solution)/shard_map/ppermute | solution.py:169
  22.2 0.0 collective-permute-done.3.refs_1_
  22.2 6.4 %shard_map.57 = (bf16[2,96,192]{2,1,0:T(8,128)(2,1)S(1)}, bf16[192,1536]{1,0:T(8,128)(2,1)S(1)}, bf16[2048,2048]{1,0:T(8,128)(2,1)S(1)}, bf16[2048,2048]{1,0:T(8,128)(2,1)S(1)}) custom-call(bf16[96,1664]{1,0:T(8,128)(2,1)S(1)} %get-tuple-element.21.refs_0_, bf16[96,1664]{1,0:T(8,128)(2,1)S(1)} %collective-permute-done.3.refs_1_, bf16[3072,2048]{1,0:T(8,128)(2,1)} %bitcast.2, ...), custom_call_target="tpu_custom_call" | custom-call | flops 113246208 | bytes 16777216 | tf_op jit(solution)/shard_map/pallas_call | solution.py:136
  28.7 1.9 %collective-permute-done.2.refs_0_ = bf16[96,1664]{1,0:T(8,128)(2,1)S(1)} collective-permute-done((bf16[96,1664]{1,0:T(8,128)(2,1)S(1)}, bf16[96,1664]{1,0:T(8,128)(2,1)S(1)}, u32[]{:S(2)}, u32[]{:S(2)}) %collective-permute-start.2) | collective-permute-done | bytes 319520 | tf_op jit(solution)/shard_map/ppermute | solution.py:169
  30.6 0.0 collective-permute-start.4
  30.6 1.5 %collective-permute-start.1 = (bf16[96,1536]{1,0:T(8,128)(2,1)S(1)}, bf16[96,1536]{1,0:T(8,128)(2,1)S(1)}, u32[]{:S(2)}, u32[]{:S(2)}) collective-permute-start(bf16[96,1536]{1,0:T(8,128)(2,1)S(1)} %get-tuple-element.20.refs_0_), channel_id=1, source_target_pairs={{0,2},{1,3},{2,0},{3,1},{4,6},{5,7},{6,4},{7,5},{8,10},{9,11},{10,... | collective-permute-start | bytes 884744 | tf_op jit(solution)/shard_map/ppermute | solution.py:169
  32.1 0.2 collective-permute-start
  32.3 0.0 collective-permute-done.4.refs_1_
  32.3 5.2 %shard_map.58 = (f32[192,2048]{1,0:T(8,128)S(1)}, f32[192,2048]{1,0:T(8,128)S(1)}, bf16[2,96,192]{2,1,0:T(8,128)(2,1)S(1)}, bf16[1024,2048]{1,0:T(8,128)(2,1)S(1)}, bf16[1024,2048]{1,0:T(8,128)(2,1)S(1)}) custom-call(bf16[96,1664]{1,0:T(8,128)(2,1)S(1)} %collective-permute-done.2.refs_0_, bf16[96,1664]{1,0:T(8,128)(2,1)S(1)} %collective-permute-done.4.refs_1_, ...), custom_call_target="tpu_custom_call" | custom-call | flops 2415919104 | bytes 8388608 | tf_op jit(solution)/shard_map/pallas_call | solution.py:136
  37.6 2.5 %collective-permute-done.1.refs_2_ = bf16[96,1536]{1,0:T(8,128)(2,1)S(1)} collective-permute-done((bf16[96,1536]{1,0:T(8,128)(2,1)S(1)}, bf16[96,1536]{1,0:T(8,128)(2,1)S(1)}, u32[]{:S(2)}, u32[]{:S(2)}) %collective-permute-start.1) | collective-permute-done | bytes 294944 | tf_op jit(solution)/shard_map/ppermute | solution.py:169
  40.0 0.0 collective-permute-start.5
  40.0 0.0 collective-permute-done.refs_1_
  40.0 1.6 %collective-permute-done.5.refs_3_ = bf16[96,1536]{1,0:T(8,128)(2,1)S(1)} collective-permute-done((bf16[96,1536]{1,0:T(8,128)(2,1)S(1)}, bf16[96,1536]{1,0:T(8,128)(2,1)S(1)}, u32[]{:S(2)}, u32[]{:S(2)}) %collective-permute-start.5) | collective-permute-done | bytes 294944 | tf_op jit(solution)/shard_map/ppermute | solution.py:169
  41.6 0.0 copy-start.1
  41.6 4.4 %shard_map.59 = bf16[16,48,512]{2,1,0:T(8,128)(2,1)} custom-call(bf16[96,1536]{1,0:T(8,128)(2,1)S(1)} %get-tuple-element.20.refs_0_, bf16[96,1536]{1,0:T(8,128)(2,1)S(1)} %collective-permute-done.refs_1_, bf16[96,1536]{1,0:T(8,128)(2,1)S(1)} %collective-permute-done.1.refs_2_, bf16[96,1536]{1,0:T(8,128)(2,1)S(1)} %collective-permute-done.5.refs_3_, ...), custom_call_target="tpu_custom_call" | custom-call | flops 2415919104 | tf_op jit(solution)/shard_map/pallas_call | solution.py:136
  45.9 5.4 %all-to-all-start = ((bf16[16,48,512]{2,1,0:T(8,128)(2,1)}), bf16[16,48,512]{2,1,0:T(8,128)(2,1)S(1)}, u32[]{:S(2)}, u32[]{:S(2)}) async-start(bf16[16,48,512]{2,1,0:T(8,128)(2,1)} %shard_map.59), calls=%async_computation | async-start | bytes 1572864 | tf_op jit(solution)/shard_map/all_to_all | solution.py:31
  51.4 0.0 copy-done.1
  51.4 0.1 copy.8.weights_ref
  51.5 18.6 %all-to-all-done.recv_ref = bf16[16,48,512]{2,1,0:T(8,128)(2,1)S(1)} async-done(((bf16[16,48,512]{2,1,0:T(8,128)(2,1)}), bf16[16,48,512]{2,1,0:T(8,128)(2,1)S(1)}, u32[]{:S(2)}, u32[]{:S(2)}) %all-to-all-start) | async-done | bytes 786464 | tf_op jit(solution)/shard_map/all_to_all | solution.py:31
  70.1 1.8 %shard_map.60 = bf16[24,2,8192]{2,1,0:T(2,128)(2,1)} custom-call(s32[24,2]{1,0:T(8,128)S(1)} %copy.7.ids_ref, f32[24,2]{1,0:T(8,128)S(1)} %copy.8.weights_ref, bf16[16,48,512]{2,1,0:T(8,128)(2,1)S(1)} %all-to-all-done.recv_ref), custom_call_target="tpu_custom_call" | custom-call | tf_op jit(solution)/shard_map/pallas_call | solution.py:283
  (1 shorter events, 0.0 us)
Async XLA Ops:
  0.8 0.9 %copy-start = (bf16[24,3072]{1,0:T(8,128)(2,1)S(1)}, bf16[24,3072]{1,0:T(8,128)(2,1)}, u32[]{:S(2)}) copy-start(bf16[24,3072]{1,0:T(8,128)(2,1)} %tokens_ref.1) | copy-start | bytes 442372
  20.5 1.7 %collective-permute-start.3 = (bf16[96,1664]{1,0:T(8,128)(2,1)S(1)}, bf16[96,1664]{1,0:T(8,128)(2,1)S(1)}, u32[]{:S(2)}, u32[]{:S(2)}) collective-permute-start(bf16[96,1664]{1,0:T(8,128)(2,1)S(1)} %get-tuple-element.21.refs_0_), channel_id=1, source_target_pairs={{0,1},{1,0},{2,3},{3,2},{4,5},{5,4},{6,7},{7,6},{8,9},{9,8},{10,11... | collective-permute-start | bytes 958472 | tf_op jit(solution)/shard_map/ppermute | solution.py:169
  20.6 10.0 %collective-permute-start.2 = (bf16[96,1664]{1,0:T(8,128)(2,1)S(1)}, bf16[96,1664]{1,0:T(8,128)(2,1)S(1)}, u32[]{:S(2)}, u32[]{:S(2)}) collective-permute-start(bf16[96,1664]{1,0:T(8,128)(2,1)S(1)} %get-tuple-element.21.refs_0_), channel_id=1, source_target_pairs={{0,2},{1,3},{2,0},{3,1},{4,6},{5,7},{6,4},{7,5},{8,10},{9,11},{10,... | collective-permute-start | bytes 958472 | tf_op jit(solution)/shard_map/ppermute | solution.py:169
  30.6 1.7 %collective-permute-start.4 = (bf16[96,1664]{1,0:T(8,128)(2,1)S(1)}, bf16[96,1664]{1,0:T(8,128)(2,1)S(1)}, u32[]{:S(2)}, u32[]{:S(2)}) collective-permute-start(bf16[96,1664]{1,0:T(8,128)(2,1)S(1)} %collective-permute-done.2.refs_0_), channel_id=1, source_target_pairs={{0,1},{1,0},{2,3},{3,2},{4,5},{5,4},{6,7},{7,6},{8,9},{9,8},{10,11... | collective-permute-start | bytes 958472 | tf_op jit(solution)/shard_map/ppermute | solution.py:169
  30.6 9.4 %collective-permute-start.1 = (bf16[96,1536]{1,0:T(8,128)(2,1)S(1)}, bf16[96,1536]{1,0:T(8,128)(2,1)S(1)}, u32[]{:S(2)}, u32[]{:S(2)}) collective-permute-start(bf16[96,1536]{1,0:T(8,128)(2,1)S(1)} %get-tuple-element.20.refs_0_), channel_id=1, source_target_pairs={{0,2},{1,3},{2,0},{3,1},{4,6},{5,7},{6,4},{7,5},{8,10},{9,11},{10,... | collective-permute-start | bytes 884744 | tf_op jit(solution)/shard_map/ppermute | solution.py:169
  32.1 7.9 %collective-permute-start = (bf16[96,1536]{1,0:T(8,128)(2,1)S(1)}, bf16[96,1536]{1,0:T(8,128)(2,1)S(1)}, u32[]{:S(2)}, u32[]{:S(2)}) collective-permute-start(bf16[96,1536]{1,0:T(8,128)(2,1)S(1)} %get-tuple-element.20.refs_0_), channel_id=1, source_target_pairs={{0,1},{1,0},{2,3},{3,2},{4,5},{5,4},{6,7},{7,6},{8,9},{9,8},{10,11... | collective-permute-start | bytes 884744 | tf_op jit(solution)/shard_map/ppermute | solution.py:169
  40.0 1.6 %collective-permute-start.5 = (bf16[96,1536]{1,0:T(8,128)(2,1)S(1)}, bf16[96,1536]{1,0:T(8,128)(2,1)S(1)}, u32[]{:S(2)}, u32[]{:S(2)}) collective-permute-start(bf16[96,1536]{1,0:T(8,128)(2,1)S(1)} %collective-permute-done.1.refs_2_), channel_id=1, source_target_pairs={{0,1},{1,0},{2,3},{3,2},{4,5},{5,4},{6,7},{7,6},{8,9},{9,8},{10,11... | collective-permute-start | bytes 884744 | tf_op jit(solution)/shard_map/ppermute | solution.py:169
  41.6 9.8 %copy-start.1 = (f32[24,2]{0,1:T(2,128)S(1)}, f32[24,2]{0,1:T(2,128)}, u32[]{:S(2)}) copy-start(f32[24,2]{0,1:T(2,128)} %param.7) | copy-start | bytes 580
  45.9 24.2 %all-to-all-start = ((bf16[16,48,512]{2,1,0:T(8,128)(2,1)}), bf16[16,48,512]{2,1,0:T(8,128)(2,1)S(1)}, u32[]{:S(2)}, u32[]{:S(2)}) async-start(bf16[16,48,512]{2,1,0:T(8,128)(2,1)} %shard_map.59), calls=%async_computation | async-start | bytes 1572864 | tf_op jit(solution)/shard_map/all_to_all | solution.py:31

commit v6 on v1

--- a/solution.py
+++ b/solution.py
@@ -1,7 +1,14 @@
+import functools
+
 import jax
 import jax.numpy as jnp
 from jax import lax
+from jax.experimental import pallas as pl
+from jax.experimental.pallas import tpu as pltpu
 from jax.sharding import PartitionSpec as P
+
+WHOLE = pl.BlockSpec(memory_space=pltpu.VMEM)
+OUTSIDE = pl.BlockSpec(memory_space=pltpu.HBM)
 
 
 def place_slots(id_block, experts, capacity):
@@ -25,6 +32,269 @@
 
 def exchange(blocks):
     return lax.all_to_all(blocks, ("et", "ep"), split_axis=0, concat_axis=0, tiled=True)
+
+
+def local_kernel(kernel, out_shape, args, outside=(), flops=0, moved=0, scratch=(), limit=12):
+    return pl.pallas_call(
+        kernel,
+        out_shape=out_shape,
+        in_specs=[WHOLE] * len(args) + [OUTSIDE] * len(outside),
+        out_specs=jax.tree.map(lambda _: WHOLE, out_shape),
+        scratch_shapes=scratch,
+        compiler_params=pltpu.CompilerParams(vmem_limit_bytes=limit << 20),
+        cost_estimate=pl.CostEstimate(flops=flops, bytes_accessed=moved, transcendentals=0),
+    )(*args, *(pltpu.with_memory_space_constraint(array, pltpu.HBM) for array in outside))
+
+
+def exact_dot(a, b):
+    return jnp.dot(a, b, preferred_element_type=jnp.float32)
+
+
+def transposed_dot(a, b):
+    return lax.dot_general(a, b, (((0,), (0,)), ((), ())), preferred_element_type=jnp.float32)
+
+
+def iota(shape, dim):
+    return lax.broadcasted_iota(jnp.int32, shape, dim)
+
+
+def as_column(row):
+    size = row.shape[1]
+    eye = iota((size, size), 0) == iota((size, size), 1)
+    return jnp.sum(jnp.where(eye, row, jnp.zeros_like(row)), axis=1, keepdims=True)
+
+
+def as_row(column):
+    size = column.shape[0]
+    eye = iota((size, size), 0) == iota((size, size), 1)
+    return jnp.sum(jnp.where(eye, column, jnp.zeros_like(column)), axis=0, keepdims=True)
+
+
+def pack_kernel(ids_ref, tokens_hbm, out_ref, sem):
+    copy = pltpu.make_async_copy(tokens_hbm, out_ref.at[:, 128:], sem)
+    copy.start()
+    names = ids_ref[...].astype(jnp.float32)
+    lane = iota((out_ref.shape[0], 128), 1)
+    out_ref[:, :128] = jnp.where(lane == 0, as_column(names[0:1]), as_column(names[1:2])).astype(out_ref.dtype)
+    copy.wait()
+
+
+def rows_of(ids_block, source, expert, rows, tok_rows, capacity):
+    tall = ids_block.shape[0]
+    names = ids_block.astype(jnp.float32)
+    expert = expert.astype(jnp.float32)
+    named = (names[:, 0:1] == expert) | (names[:, 1:2] == expert)
+    later, earlier = iota((tall, tall), 0), iota((tall, tall), 1)
+    lower = ((later > earlier) & (later // tok_rows == earlier // tok_rows)).astype(jnp.bfloat16)
+    flags = jnp.broadcast_to(named.astype(jnp.float32), (tall, 128)).astype(jnp.bfloat16)
+    before = exact_dot(lower, flags)[:, 0:1].astype(jnp.int32)
+    layer = iota((tall, 1), 0) // tok_rows
+    target = jnp.where(named, (layer * 2 + source) * capacity + before, -1)
+    return (iota((tall, rows), 1) == target).astype(jnp.bfloat16)
+
+
+def select_kernel(tok_rows, capacity, own_ref, near_ref, first_ref, second_ref, stay_ref):
+    mine = lax.axis_index("ep")
+    core = mine % 2
+    rows = stay_ref.shape[0]
+    blocks = ((own_ref, core), (near_ref, 1 - core))
+    cut = first_ref.shape[1]
+
+    def chosen(sels, start, stop):
+        parts = [transposed_dot(sel, ref[:, 128 + start : 128 + stop]) for sel, (ref, _) in zip(sels, blocks)]
+        return (parts[0] + parts[1]).astype(stay_ref.dtype)
+
+    def columns_of(expert):
+        return [rows_of(ref[:, :128], source, expert, rows, tok_rows, capacity) for ref, source in blocks]
+
+    sels = columns_of(mine ^ 2)
+    first_ref[...] = chosen(sels, 0, cut)
+    second_ref[...] = chosen(sels, cut, stay_ref.shape[1])
+    stay_ref[...] = chosen(columns_of(mine), 0, stay_ref.shape[1])
+
+
+def weight_copies(weights, held, sems, start, step):
+    return [
+        pltpu.make_async_copy(
+            ref.at[pl.ds(start + part * step, step), :], into.at[pl.ds(part * step, step), :], sems.at[which, part]
+        )
+        for part in range(held[0].shape[0] // step)
+        for which, (ref, into) in enumerate(zip(weights, held))
+    ]
+
+
+def fetch_kernel(step, stay_ref, gate_hbm, up_hbm, gate_held, up_held, sems):
+    copies = weight_copies((gate_hbm, up_hbm), (gate_held, up_held), sems, 0, step)
+    for copy in copies:
+        copy.start()
+    for copy in copies:
+        copy.wait()
+
+
+def gather_rows(x_ref, stay, far):
+    rows = stay.shape[0]
+    chip = lax.axis_index("ep") // 2
+    x_ref[pl.ds(pl.multiple_of(chip * rows, rows), rows), :] = stay
+    x_ref[pl.ds(pl.multiple_of((1 - chip) * rows, rows), rows), :] = far
+
+
+def first_kernel(step, far_ref, stay_ref, gate_held, up_held, gate_hbm, up_hbm, *refs):
+    gate_ref, up_ref, gate_rest, up_rest, x_ref, sems = refs
+    copies = weight_copies((gate_hbm, up_hbm), (gate_rest, up_rest), sems, gate_held.shape[0], step)
+    for copy in copies:
+        copy.start()
+    cut = far_ref.shape[1]
+    gather_rows(x_ref, stay_ref[:, :cut], far_ref[...])
+    gate_ref[...] = exact_dot(x_ref[...], gate_held[:cut, :])
+    up_ref[...] = exact_dot(x_ref[...], up_held[:cut, :])
+    for copy in copies:
+        copy.wait()
+
+
+def second_kernel(folds, experts, far_ref, stay_ref, gate_in, up_in, *refs):
+    gate_held, up_held, gate_rest, up_rest, out_ref, x_ref, hidden_ref = refs
+    cut = stay_ref.shape[1] - far_ref.shape[1]
+    gather_rows(x_ref, stay_ref[:, cut:], far_ref[...])
+    middle = gate_held.shape[0] - cut
+    sums = []
+    for held, rest, total in ((gate_held, gate_rest, gate_in), (up_held, up_rest, up_in)):
+        total = total[...] + exact_dot(x_ref[:, middle:], rest[...])
+        if middle:
+            total = total + exact_dot(x_ref[:, :middle], held[cut:, :])
+        sums.append(total)
+    gate_val, up_val = sums
+    hidden_ref[...] = gate_val / (1.0 + jnp.exp(-gate_val)) * up_val
+    store_blocks(folds, experts, hidden_ref, out_ref)
+
+
+def store_blocks(folds, experts, hidden_ref, out_ref):
+    peers = out_ref.shape[0]
+    capacity = hidden_ref.shape[0] // peers
+    span = hidden_ref.shape[1] // folds
+    for peer in range(peers):
+        layer, chip, core = peer // experts, peer % experts // 2, peer % 2
+        start = (chip * (peers // 2) + layer * 2 + core) * capacity
+        rows = hidden_ref[start : start + capacity, :]
+        pieces = [rows[:, fold * span : (fold + 1) * span] for fold in range(folds)]
+        out_ref[peer] = jnp.concatenate(pieces, axis=0).astype(out_ref.dtype)
+
+
+def routed_by_columns(tokens, expert_ids, gate_local, up_local, peers, capacity, folds):
+    tok_rows, width = tokens.shape
+    units = gate_local.shape[1]
+    experts = 4
+    rows = peers * capacity
+    half = rows // 2
+    cut = width // 2
+    held = 2 * width // 3
+    rest = width - held
+    step = 256
+    kind = tokens.dtype
+
+    def array(*shape):
+        return jax.ShapeDtypeStruct(shape, kind)
+
+    def swap(block, bit):
+        return lax.ppermute(block, "ep", [(i, i ^ bit) for i in range(experts)])
+
+    packed = local_kernel(
+        pack_kernel, array(tok_rows, 128 + width), (expert_ids.T,), (tokens,), scratch=[pltpu.SemaphoreType.DMA]
+    )
+    own = lax.all_gather(packed, "et", axis=0, tiled=True)
+    first, second, stay = local_kernel(
+        functools.partial(select_kernel, tok_rows, capacity),
+        [array(half, cut), array(half, width - cut), array(half, width)],
+        (own, swap(own, 1)),
+        flops=8 * own.shape[0] * half * width,
+        moved=8 * own.size,
+    )
+    far, later = swap(first, 2), swap(second, 2)
+    gate_held, up_held = local_kernel(
+        functools.partial(fetch_kernel, step),
+        [pltpu.VMEM((held, units), kind)] * 2,
+        (stay,),
+        (gate_local, up_local),
+        moved=8 * held * units,
+        scratch=[pltpu.SemaphoreType.DMA((2, held // step))],
+    )
+    far, gate_held, up_held = lax.optimization_barrier((far, gate_held, up_held))
+    gate_sum, up_sum, gate_rest, up_rest = local_kernel(
+        functools.partial(first_kernel, step),
+        [jax.ShapeDtypeStruct((rows, units), jnp.float32)] * 2 + [pltpu.VMEM((rest, units), kind)] * 2,
+        (far, stay, gate_held, up_held),
+        (gate_local, up_local),
+        flops=4 * rows * cut * units,
+        moved=4 * rest * units,
+        scratch=[pltpu.VMEM((rows, cut), kind), pltpu.SemaphoreType.DMA((2, rest // step))],
+    )
+    later, gate_rest, up_rest = lax.optimization_barrier((later, gate_rest, up_rest))
+    return local_kernel(
+        functools.partial(second_kernel, folds, experts),
+        array(peers, capacity * folds, units // folds),
+        (later, stay, gate_sum, up_sum, gate_held, up_held, gate_rest, up_rest),
+        flops=4 * rows * (width - cut) * units,
+        scratch=[pltpu.VMEM((rows, width - cut), kind), pltpu.VMEM((rows, units), jnp.float32)],
+    )
+
+
+def picks_kernel(experts, capacity, folds, ids_ref, weights_ref, picks_ref, column_ref):
+    tok_rows = ids_ref.shape[1]
+    both = 2 * tok_rows
+    ids = [as_column(ids_ref[slot : slot + 1, :]) for slot in range(2)]
+    expert = iota((tok_rows, 128), 1)
+    named = ((expert == ids[0]) | (expert == ids[1])).astype(jnp.bfloat16)
+    lower = (iota((tok_rows, tok_rows), 0) > iota((tok_rows, tok_rows), 1)).astype(jnp.bfloat16)
+    before = exact_dot(lower, named).astype(jnp.int32)
+    slot_row, token = iota((both, tok_rows), 0), iota((both, tok_rows), 1)
+    target = jnp.zeros((both, 1), jnp.int32)
+    column = jnp.zeros((both, 1), jnp.float32)
+    for slot, chosen in enumerate(ids):
+        position = jnp.sum(jnp.where(expert == chosen, before, 0), axis=1, keepdims=True)
+        mask = slot_row == 2 * token + slot
+        place = as_row(chosen * (folds * capacity) + position)
+        target = target + jnp.sum(jnp.where(mask, place, 0), axis=1, keepdims=True)
+        column = column + jnp.sum(jnp.where(mask, weights_ref[slot : slot + 1, :], 0.0), axis=1, keepdims=True)
+    column_ref[...] = jnp.broadcast_to(column, column_ref.shape)
+    lane = iota((both, experts * folds * capacity), 1)
+    for fold in range(folds):
+        picks_ref[fold * both : (fold + 1) * both, :] = (lane == target + fold * capacity).astype(picks_ref.dtype)
+
+
+def final_kernel(experts, folds, picks_ref, column_ref, recv_ref, out_ref):
+    tok_rows = out_ref.shape[0]
+    both = 2 * tok_rows
+    peers, tall, span = recv_ref.shape
+    column = column_ref[:, 0:1]
+    for part in range(peers // experts):
+        block = recv_ref[part * experts : (part + 1) * experts].reshape(experts * tall, span)
+        rows = exact_dot(picks_ref[...], block)
+        for fold in range(folds):
+            scaled = rows[fold * both : (fold + 1) * both] * column
+            start = (part * folds + fold) * span
+            out_ref[:, :, start : start + span] = scaled.astype(out_ref.dtype).reshape(tok_rows, 2, span)
+
+
+def finish(expert_ids, gate_weights, received, experts, folds):
+    tok_rows = expert_ids.shape[0]
+    peers, tall, span = received.shape
+    capacity = tall // folds
+    kind = received.dtype
+    picks, column = local_kernel(
+        functools.partial(picks_kernel, experts, capacity, folds),
+        [
+            jax.ShapeDtypeStruct((2 * tok_rows * folds, experts * tall), kind),
+            jax.ShapeDtypeStruct((2 * tok_rows, 128), jnp.float32),
+        ],
+        (expert_ids.T, gate_weights.T),
+        moved=1 << 20,
+    )
+    units = peers // experts * folds * span
+    return local_kernel(
+        functools.partial(final_kernel, experts, folds),
+        jax.ShapeDtypeStruct((tok_rows, 2, units), kind),
+        (picks, column, received),
+        moved=4 * received.size,
+    )
 
 
 def body(tokens, expert_ids, gate_weights, w_gate, w_up):
@@ -35,6 +305,10 @@
     capacity = tok_rows // 2
     gate_local = w_gate[0]
     up_local = w_up[0]
+    if experts == 4 and tensor_size == 4:
+        folds = 4
+        blocks = routed_by_columns(tokens, expert_ids, gate_local, up_local, peers, capacity, folds)
+        return finish(expert_ids, gate_weights, exchange(blocks), experts, folds)
     slot_pairs = place_slots(expert_ids, experts, capacity)
     selector = build_select(slot_pairs, experts * capacity)
     buffer = jnp.dot(selector, tokens, preferred_element_type=jnp.float32).astype(jnp.bfloat16)

time: 81.4 us -> 68.8 us (0.85)
  blocking collectives: 60 us -> 18.8 us
  waiting for transfers between devices: 0 us -> 23.2 us
  Pallas kernels: 0 us -> 18.2 us
  matrix products: 14.1 us -> 0 us
  starting transfers between devices: 0 us -> 7.53 us
  local copies, waits for them, and re-layouts: 5.48 us -> 0.69 us
  other arithmetic: 1.1 us -> 0 us
    all_to_all x2 -> x0, blocking collectives: 60 us -> none  [exchange(): lax.all_to_all(blocks, ('et', 'ep'), split_axis=0, concat_axis=0, tiled=T...]
    all_gather x0 -> x1, blocking collectives: none -> 18.8 us  [routed_by_columns(): own = lax.all_gather(packed, 'et', axis=0, tiled=True)]
    all_to_all x0 -> x1, waiting for transfers between devices: none -> 18.2 us  [exchange(): lax.all_to_all(blocks, ('et', 'ep'), split_axis=0, concat_axis=0, tiled=T...]
    pallas_call x0 -> x7, Pallas kernels: none -> 18.2 us  [local_kernel(): pl.pallas_call(kernel, out_shape=out_shape, in_specs=[WHOLE] * len(args)...]
    dot_general x4 -> x0, matrix products: 14.1 us -> none  [the longest x1 7.36 us: swiglu_rows(): up_val = jnp.dot(rows, up_local, preferred_element_type=jnp.float32)]
    all_to_all x0 -> x1, starting transfers between devices: none -> 5.44 us  [exchange(): lax.all_to_all(blocks, ('et', 'ep'), split_axis=0, concat_axis=0, tiled=T...]
    ppermute x0 -> x3, waiting for transfers between devices: none -> 4.93 us  [swap(): return lax.ppermute(block, 'ep', [(i, i ^ bit) for i in range(experts)])]
    ppermute x0 -> x3, starting transfers between devices: none -> 2.09 us  [swap(): return lax.ppermute(block, 'ep', [(i, i ^ bit) for i in range(experts)])]
  transfers between devices with their start and end apart: 0 -> 4, of which waited for: 0 -> 4; matrix products, arithmetic and copies ran while one was open for 0% -> 0% of each run, Pallas kernels for 0% -> 16%
where the time goes in v6:
time: 68.8 us; the launch traced here: 68.4 us
  waiting for transfers between devices  23.2 us (34%)
  blocking collectives  18.8 us (27%)
  Pallas kernels  18.2 us (26%)
  starting transfers between devices  7.53 us (11%)
  local copies, waits for them, and re-layouts  0.69 us (1%)
    all_gather x1, blocking collectives, routed_by_columns(): own = lax.all_gather(packed, 'et', axis=0, tiled=True)  18.8 us
    all_to_all x1, waiting for transfers between devices, exchange(): lax.all_to_all(blocks, ('et', 'ep'), split_axis=0, concat_axis=0, tiled=T...  18.2 us
    pallas_call x7, Pallas kernels, local_kernel(): pl.pallas_call(kernel, out_shape=out_shape, in_specs=[WHOLE] * len(args)...  18.2 us
    all_to_all x1, starting transfers between devices, exchange(): lax.all_to_all(blocks, ('et', 'ep'), split_axis=0, concat_axis=0, tiled=T...  5.44 us
    ppermute x3, waiting for transfers between devices, swap(): return lax.ppermute(block, 'ep', [(i, i ^ bit) for i in range(experts)])  4.93 us
    ppermute x3, starting transfers between devices, swap(): return lax.ppermute(block, 'ep', [(i, i ^ bit) for i in range(experts)])  2.09 us
  transfers between devices with their start and end apart: 4, of which 4 were waited for; matrix products, arithmetic and copies ran while one was open for 0% of the time, Pallas kernels for 16%

profile of v6, /device:TPU:0, one launch (start us, length us, event | category | flops | bytes accessed | tf_op | source)
XLA Modules:
  0.0 68.4 jit_solution(16223262877591439411)
XLA Ops:
  0.0 0.0 copy-start
  0.0 0.7 copy-done
  0.7 0.9 %shard_map.56 = bf16[24,3200]{1,0:T(8,128)(2,1)S(1)} custom-call(s32[2,24]{1,0:T(2,128)S(1)} %bitcast.4, bf16[24,3072]{1,0:T(8,128)(2,1)} %tokens_hbm.1), custom_call_target="tpu_custom_call" | custom-call | tf_op jit(solution)/shard_map/pallas_call | solution.py:38
  1.6 18.8 %all_gather.3.own_ref = bf16[96,3200]{1,0:T(8,128)(2,1)S(1)} all-gather(bf16[24,3200]{1,0:T(8,128)(2,1)S(1)} %shard_map.56), channel_id=1, replica_groups=mesh['groups'=2,'et'=4,'ep'=4] {'et'}, dimensions={0}, use_global_device_ids=true | all-gather | bytes 768000 | tf_op jit(solution)/shard_map/all_gather | solution.py:203
  20.4 0.0 collective-permute-start
  20.4 2.0 %collective-permute-done.near_ref = bf16[96,3200]{1,0:T(8,128)(2,1)S(1)} collective-permute-done((bf16[96,3200]{1,0:T(8,128)(2,1)S(1)}, bf16[96,3200]{1,0:T(8,128)(2,1)S(1)}, u32[]{:S(2)}, u32[]{:S(2)}) %collective-permute-start) | collective-permute-done | bytes 614432 | tf_op jit(solution)/shard_map/ppermute | solution.py:198
  22.4 1.4 %shard_map.57 = (bf16[96,1536]{1,0:T(8,128)(2,1)S(1)}, bf16[96,1536]{1,0:T(8,128)(2,1)S(1)}, bf16[96,3072]{1,0:T(8,128)(2,1)S(1)}) custom-call(bf16[96,3200]{1,0:T(8,128)(2,1)S(1)} %all_gather.3.own_ref, bf16[96,3200]{1,0:T(8,128)(2,1)S(1)} %collective-permute-done.near_ref), custom_call_target="tpu_custom_call" | custom-call | flops 226492416 | bytes 2457600 | tf_op jit(solution)/shard_map/pallas_call | solution.py:38
  23.9 1.6 %collective-permute-start.2 = (bf16[96,1536]{1,0:T(8,128)(2,1)S(1)}, bf16[96,1536]{1,0:T(8,128)(2,1)S(1)}, u32[]{:S(2)}, u32[]{:S(2)}) collective-permute-start(bf16[96,1536]{1,0:T(8,128)(2,1)S(1)} %get-tuple-element.25), channel_id=1, source_target_pairs={{0,2},{1,3},{2,0},{3,1},{4,6},{5,7},{6,4},{7,5},{8,10},{9,11},{10,... | collective-permute-start | bytes 884744 | tf_op jit(solution)/shard_map/ppermute | solution.py:198
  25.4 0.5 collective-permute-start.1
  26.0 5.9 %shard_map.58 = (bf16[2048,2048]{1,0:T(8,128)(2,1)S(1)}, bf16[2048,2048]{1,0:T(8,128)(2,1)S(1)}) custom-call(bf16[96,3072]{1,0:T(8,128)(2,1)S(1)} %get-tuple-element.26.stay_ref, bf16[3072,2048]{1,0:T(8,128)(2,1)} %bitcast.7, bf16[3072,2048]{1,0:T(8,128)(2,1)} %bitcast.9), custom_call_target="tpu_custom_call" | custom-call | bytes 33554432 | tf_op jit(solution)/shard_map/pallas_call | solution.py:38
  31.9 1.9 %collective-permute-done.2.far_ref = bf16[96,1536]{1,0:T(8,128)(2,1)S(1)} collective-permute-done((bf16[96,1536]{1,0:T(8,128)(2,1)S(1)}, bf16[96,1536]{1,0:T(8,128)(2,1)S(1)}, u32[]{:S(2)}, u32[]{:S(2)}) %collective-permute-start.2) | collective-permute-done | bytes 294944 | tf_op jit(solution)/shard_map/ppermute | solution.py:198
  33.8 4.5 %shard_map.59 = (f32[192,2048]{1,0:T(8,128)S(1)}, f32[192,2048]{1,0:T(8,128)S(1)}, bf16[1024,2048]{1,0:T(8,128)(2,1)S(1)}, bf16[1024,2048]{1,0:T(8,128)(2,1)S(1)}) custom-call(bf16[96,1536]{1,0:T(8,128)(2,1)S(1)} %collective-permute-done.2.far_ref, bf16[96,3072]{1,0:T(8,128)(2,1)S(1)} %get-tuple-element.26.stay_ref, ...), custom_call_target="tpu_custom_call" | custom-call | flops 2415919104 | bytes 8388608 | tf_op jit(solution)/shard_map/pallas_call | solution.py:38
  38.3 1.0 %collective-permute-done.1.far_ref = bf16[96,1536]{1,0:T(8,128)(2,1)S(1)} collective-permute-done((bf16[96,1536]{1,0:T(8,128)(2,1)S(1)}, bf16[96,1536]{1,0:T(8,128)(2,1)S(1)}, u32[]{:S(2)}, u32[]{:S(2)}) %collective-permute-start.1) | collective-permute-done | bytes 294944 | tf_op jit(solution)/shard_map/ppermute | solution.py:198
  39.3 0.0 copy-start.1
  39.3 0.0 copy-start.2
  39.3 3.7 %shard_map.60 = bf16[16,48,512]{2,1,0:T(8,128)(2,1)} custom-call(bf16[96,1536]{1,0:T(8,128)(2,1)S(1)} %collective-permute-done.1.far_ref, bf16[96,3072]{1,0:T(8,128)(2,1)S(1)} %get-tuple-element.26.stay_ref, f32[192,2048]{1,0:T(8,128)S(1)} %get-tuple-element.35.gate_in, f32[192,2048]{1,0:T(8,128)S(1)} %get-tuple-element.36.up_in, ...), custom_call_target="tpu_custom_call" | custom-call | flops 2415919104 | tf_op jit(solution)/shard_map/pallas_call | solution.py:38
  43.0 5.4 %all-to-all-start = ((bf16[16,48,512]{2,1,0:T(8,128)(2,1)}), bf16[16,48,512]{2,1,0:T(8,128)(2,1)S(1)}, u32[]{:S(2)}, u32[]{:S(2)}) async-start(bf16[16,48,512]{2,1,0:T(8,128)(2,1)} %shard_map.60), calls=%async_computation | async-start | bytes 1572864 | tf_op jit(solution)/shard_map/all_to_all | solution.py:34
  48.5 0.0 copy-done.1
  48.5 0.0 copy-done.2
  48.5 0.4 shard_map.55
  48.9 18.2 %all-to-all-done.recv_ref = bf16[16,48,512]{2,1,0:T(8,128)(2,1)S(1)} async-done(((bf16[16,48,512]{2,1,0:T(8,128)(2,1)}), bf16[16,48,512]{2,1,0:T(8,128)(2,1)S(1)}, u32[]{:S(2)}, u32[]{:S(2)}) %all-to-all-start) | async-done | bytes 786464 | tf_op jit(solution)/shard_map/all_to_all | solution.py:34
  67.2 1.3 %shard_map.61 = bf16[24,2,8192]{2,1,0:T(2,128)(2,1)} custom-call(bf16[192,192]{1,0:T(8,128)(2,1)S(1)} %get-tuple-element.22.picks_ref, f32[48,128]{1,0:T(8,128)S(1)} %get-tuple-element.23.column_ref, bf16[16,48,512]{2,1,0:T(8,128)(2,1)S(1)} %all-to-all-done.recv_ref), custom_call_target="tpu_custom_call" | custom-call | bytes 1572864 | tf_op jit(solution)/shard_map/pallas_call | solution.py:38
Async XLA Ops:
  0.0 0.7 copy-start
  20.4 2.0 %collective-permute-start = (bf16[96,3200]{1,0:T(8,128)(2,1)S(1)}, bf16[96,3200]{1,0:T(8,128)(2,1)S(1)}, u32[]{:S(2)}, u32[]{:S(2)}) collective-permute-start(bf16[96,3200]{1,0:T(8,128)(2,1)S(1)} %all_gather.3.own_ref), channel_id=1, source_target_pairs={{0,1},{1,0},{2,3},{3,2},{4,5},{5,4},{6,7},{7,6},{8,9},{9,8},{10,11... | collective-permute-start | bytes 1843208 | tf_op jit(solution)/shard_map/ppermute | solution.py:198
  23.9 9.9 %collective-permute-start.2 = (bf16[96,1536]{1,0:T(8,128)(2,1)S(1)}, bf16[96,1536]{1,0:T(8,128)(2,1)S(1)}, u32[]{:S(2)}, u32[]{:S(2)}) collective-permute-start(bf16[96,1536]{1,0:T(8,128)(2,1)S(1)} %get-tuple-element.25), channel_id=1, source_target_pairs={{0,2},{1,3},{2,0},{3,1},{4,6},{5,7},{6,4},{7,5},{8,10},{9,11},{10,... | collective-permute-start | bytes 884744 | tf_op jit(solution)/shard_map/ppermute | solution.py:198
  25.4 13.8 %collective-permute-start.1 = (bf16[96,1536]{1,0:T(8,128)(2,1)S(1)}, bf16[96,1536]{1,0:T(8,128)(2,1)S(1)}, u32[]{:S(2)}, u32[]{:S(2)}) collective-permute-start(bf16[96,1536]{1,0:T(8,128)(2,1)S(1)} %get-tuple-element.24), channel_id=1, source_target_pairs={{0,2},{1,3},{2,0},{3,1},{4,6},{5,7},{6,4},{7,5},{8,10},{9,11},{10,... | collective-permute-start | bytes 884744 | tf_op jit(solution)/shard_map/ppermute | solution.py:198
  39.3 9.2 %copy-start.1 = (s32[24,2]{0,1:T(2,128)S(1)}, s32[24,2]{0,1:T(2,128)}, u32[]{:S(2)}) copy-start(s32[24,2]{0,1:T(2,128)} %param.6) | copy-start | bytes 580
  39.3 9.2 %copy-start.2 = (f32[24,2]{0,1:T(2,128)S(1)}, f32[24,2]{0,1:T(2,128)}, u32[]{:S(2)}) copy-start(f32[24,2]{0,1:T(2,128)} %param.7) | copy-start | bytes 580
  43.0 24.2 %all-to-all-start = ((bf16[16,48,512]{2,1,0:T(8,128)(2,1)}), bf16[16,48,512]{2,1,0:T(8,128)(2,1)S(1)}, u32[]{:S(2)}, u32[]{:S(2)}) async-start(bf16[16,48,512]{2,1,0:T(8,128)(2,1)} %shard_map.60), calls=%async_computation | async-start | bytes 1572864 | tf_op jit(solution)/shard_map/all_to_all | solution.py:34

commit v7 on v6

--- a/solution.py
+++ b/solution.py
@@ -70,9 +70,12 @@
     return jnp.sum(jnp.where(eye, column, jnp.zeros_like(column)), axis=0, keepdims=True)
 
 
-def pack_kernel(ids_ref, tokens_hbm, out_ref, sem):
-    copy = pltpu.make_async_copy(tokens_hbm, out_ref.at[:, 128:], sem)
+def pack_kernel(ids_hbm, tokens_hbm, out_ref, ids_ref, sems):
+    named = pltpu.make_async_copy(ids_hbm, ids_ref, sems.at[0])
+    named.start()
+    copy = pltpu.make_async_copy(tokens_hbm, out_ref.at[:, 128:], sems.at[1])
     copy.start()
+    named.wait()
     names = ids_ref[...].astype(jnp.float32)
     lane = iota((out_ref.shape[0], 128), 1)
     out_ref[:, :128] = jnp.where(lane == 0, as_column(names[0:1]), as_column(names[1:2])).astype(out_ref.dtype)
@@ -93,24 +96,22 @@
     return (iota((tall, rows), 1) == target).astype(jnp.bfloat16)
 
 
-def select_kernel(tok_rows, capacity, own_ref, near_ref, first_ref, second_ref, stay_ref):
-    mine = lax.axis_index("ep")
-    core = mine % 2
-    rows = stay_ref.shape[0]
+def chosen_rows(own_ref, near_ref, expert, rows, tok_rows, capacity, spans):
+    core = lax.axis_index("ep") % 2
     blocks = ((own_ref, core), (near_ref, 1 - core))
-    cut = first_ref.shape[1]
-
-    def chosen(sels, start, stop):
+    sels = [rows_of(ref[:, :128], source, expert, rows, tok_rows, capacity) for ref, source in blocks]
+    for start, stop in spans:
         parts = [transposed_dot(sel, ref[:, 128 + start : 128 + stop]) for sel, (ref, _) in zip(sels, blocks)]
-        return (parts[0] + parts[1]).astype(stay_ref.dtype)
-
-    def columns_of(expert):
-        return [rows_of(ref[:, :128], source, expert, rows, tok_rows, capacity) for ref, source in blocks]
-
-    sels = columns_of(mine ^ 2)
-    first_ref[...] = chosen(sels, 0, cut)
-    second_ref[...] = chosen(sels, cut, stay_ref.shape[1])
-    stay_ref[...] = chosen(columns_of(mine), 0, stay_ref.shape[1])
+        yield (parts[0] + parts[1]).astype(own_ref.dtype)
+
+
+def select_kernel(tok_rows, capacity, own_ref, near_ref, first_ref, second_ref):
+    rows, cut = first_ref.shape
+    expert = lax.axis_index("ep") ^ 2
+    spans = ((0, cut), (cut, cut + second_ref.shape[1]))
+    found = chosen_rows(own_ref, near_ref, expert, rows, tok_rows, capacity, spans)
+    for ref, part in zip((first_ref, second_ref), found):
+        ref[...] = part
 
 
 def weight_copies(weights, held, sems, start, step):
@@ -123,10 +124,14 @@
     ]
 
 
-def fetch_kernel(step, stay_ref, gate_hbm, up_hbm, gate_held, up_held, sems):
+def fetch_kernel(step, tok_rows, capacity, own_ref, near_ref, *refs):
+    gate_hbm, up_hbm, stay_ref, gate_held, up_held, sems = refs
     copies = weight_copies((gate_hbm, up_hbm), (gate_held, up_held), sems, 0, step)
     for copy in copies:
         copy.start()
+    rows, width = stay_ref.shape
+    expert = lax.axis_index("ep")
+    (stay_ref[...],) = chosen_rows(own_ref, near_ref, expert, rows, tok_rows, capacity, ((0, width),))
     for copy in copies:
         copy.wait()
 
@@ -185,7 +190,7 @@
     experts = 4
     rows = peers * capacity
     half = rows // 2
-    cut = width // 2
+    cut = 7 * width // 12
     held = 2 * width // 3
     rest = width - held
     step = 256
@@ -198,21 +203,26 @@
         return lax.ppermute(block, "ep", [(i, i ^ bit) for i in range(experts)])
 
     packed = local_kernel(
-        pack_kernel, array(tok_rows, 128 + width), (expert_ids.T,), (tokens,), scratch=[pltpu.SemaphoreType.DMA]
+        pack_kernel,
+        array(tok_rows, 128 + width),
+        (),
+        (expert_ids.T, tokens),
+        scratch=[pltpu.VMEM((2, tok_rows), jnp.int32), pltpu.SemaphoreType.DMA((2,))],
     )
     own = lax.all_gather(packed, "et", axis=0, tiled=True)
-    first, second, stay = local_kernel(
+    near = swap(own, 1)
+    first, second = local_kernel(
         functools.partial(select_kernel, tok_rows, capacity),
-        [array(half, cut), array(half, width - cut), array(half, width)],
-        (own, swap(own, 1)),
-        flops=8 * own.shape[0] * half * width,
-        moved=8 * own.size,
+        [array(half, cut), array(half, width - cut)],
+        (own, near),
+        flops=4 * own.shape[0] * half * width,
+        moved=4 * own.size,
     )
     far, later = swap(first, 2), swap(second, 2)
-    gate_held, up_held = local_kernel(
-        functools.partial(fetch_kernel, step),
-        [pltpu.VMEM((held, units), kind)] * 2,
-        (stay,),
+    stay, gate_held, up_held = local_kernel(
+        functools.partial(fetch_kernel, step, tok_rows, capacity),
+        [array(half, width)] + [pltpu.VMEM((held, units), kind)] * 2,
+        (own, near),
         (gate_local, up_local),
         moved=8 * held * units,
         scratch=[pltpu.SemaphoreType.DMA((2, held // step))],

time: 68.8 us -> 67.8 us (0.985)
  transfers between devices with their start and end apart: 4 -> 4, of which waited for: 4 -> 3; matrix products, arithmetic and copies ran while one was open for 0% -> 0% of each run, Pallas kernels for 16% -> 17%
where the time goes in v7:
time: 67.8 us; the launch traced here: 67.5 us
  waiting for transfers between devices  23.1 us (34%)
  blocking collectives  18.8 us (28%)
  Pallas kernels  18 us (27%)
  starting transfers between devices  7.56 us (11%)
    all_gather x1, blocking collectives, routed_by_columns(): own = lax.all_gather(packed, 'et', axis=0, tiled=True)  18.8 us
    all_to_all x1, waiting for transfers between devices, exchange(): lax.all_to_all(blocks, ('et', 'ep'), split_axis=0, concat_axis=0, tiled=T...  18.2 us
    pallas_call x7, Pallas kernels, local_kernel(): pl.pallas_call(kernel, out_shape=out_shape, in_specs=[WHOLE] * len(args)...  18 us
    all_to_all x1, starting transfers between devices, exchange(): lax.all_to_all(blocks, ('et', 'ep'), split_axis=0, concat_axis=0, tiled=T...  5.47 us
    ppermute x3, waiting for transfers between devices, swap(): return lax.ppermute(block, 'ep', [(i, i ^ bit) for i in range(experts)])  4.81 us
    ppermute x3, starting transfers between devices, swap(): return lax.ppermute(block, 'ep', [(i, i ^ bit) for i in range(experts)])  2.09 us
  transfers between devices with their start and end apart: 4, of which 3 were waited for; matrix products, arithmetic and copies ran while one was open for 0% of the time, Pallas kernels for 17%

profile of v7, /device:TPU:0, one launch (start us, length us, event | category | flops | bytes accessed | tf_op | source)
XLA Modules:
  0.0 67.5 jit_solution(1178296390055798299)
XLA Ops:
  0.0 0.9 %shard_map.56 = bf16[24,3200]{1,0:T(8,128)(2,1)S(1)} custom-call(s32[2,24]{1,0:T(2,128)} %bitcast.4, bf16[24,3072]{1,0:T(8,128)(2,1)} %tokens_hbm.1), custom_call_target="tpu_custom_call" | custom-call | tf_op jit(solution)/shard_map/pallas_call | solution.py:38
  1.0 18.8 %all_gather.3.own_ref = bf16[96,3200]{1,0:T(8,128)(2,1)S(1)} all-gather(bf16[24,3200]{1,0:T(8,128)(2,1)S(1)} %shard_map.56), channel_id=1, replica_groups=mesh['groups'=2,'et'=4,'ep'=4] {'et'}, dimensions={0}, use_global_device_ids=true | all-gather | bytes 768000 | tf_op jit(solution)/shard_map/all_gather | solution.py:212
  19.7 0.0 collective-permute-start
  19.7 2.0 %collective-permute-done.near_ref = bf16[96,3200]{1,0:T(8,128)(2,1)S(1)} collective-permute-done((bf16[96,3200]{1,0:T(8,128)(2,1)S(1)}, bf16[96,3200]{1,0:T(8,128)(2,1)S(1)}, u32[]{:S(2)}, u32[]{:S(2)}) %collective-permute-start) | collective-permute-done | bytes 614432 | tf_op jit(solution)/shard_map/ppermute | solution.py:203
  21.8 0.9 %shard_map.57 = (bf16[96,1792]{1,0:T(8,128)(2,1)S(1)}, bf16[96,1280]{1,0:T(8,128)(2,1)S(1)}) custom-call(bf16[96,3200]{1,0:T(8,128)(2,1)S(1)} %all_gather.3.own_ref, bf16[96,3200]{1,0:T(8,128)(2,1)S(1)} %collective-permute-done.near_ref), custom_call_target="tpu_custom_call" | custom-call | flops 113246208 | bytes 1228800 | tf_op jit(solution)/shard_map/pallas_call | solution.py:38
  22.6 1.6 %collective-permute-start.2 = (bf16[96,1792]{1,0:T(8,128)(2,1)S(1)}, bf16[96,1792]{1,0:T(8,128)(2,1)S(1)}, u32[]{:S(2)}, u32[]{:S(2)}) collective-permute-start(bf16[96,1792]{1,0:T(8,128)(2,1)S(1)} %get-tuple-element.25), channel_id=1, source_target_pairs={{0,2},{1,3},{2,0},{3,1},{4,6},{5,7},{6,4},{7,5},{8,10},{9,11},{10,... | collective-permute-start | bytes 1032200 | tf_op jit(solution)/shard_map/ppermute | solution.py:203
  24.2 0.5 collective-permute-start.1
  24.7 6.1 %shard_map.58 = (bf16[96,3072]{1,0:T(8,128)(2,1)S(1)}, bf16[2048,2048]{1,0:T(8,128)(2,1)S(1)}, bf16[2048,2048]{1,0:T(8,128)(2,1)S(1)}) custom-call(bf16[96,3200]{1,0:T(8,128)(2,1)S(1)} %all_gather.3.own_ref, bf16[96,3200]{1,0:T(8,128)(2,1)S(1)} %collective-permute-done.near_ref, bf16[3072,2048]{1,0:T(8,128)(2,1)} %bitcast.7, bf16[3072,2048]{1,0:T(8,128)(2,1)} %bitcast.9), custom_call_target="tpu_custom_call" | custom-call | bytes 33554432 | tf_op jit(solution)/shard_map/pallas_call | solution.py:38
  30.8 2.8 %collective-permute-done.2.far_ref = bf16[96,1792]{1,0:T(8,128)(2,1)S(1)} collective-permute-done((bf16[96,1792]{1,0:T(8,128)(2,1)S(1)}, bf16[96,1792]{1,0:T(8,128)(2,1)S(1)}, u32[]{:S(2)}, u32[]{:S(2)}) %collective-permute-start.2) | collective-permute-done | bytes 344096 | tf_op jit(solution)/shard_map/ppermute | solution.py:203
  33.6 5.1 %shard_map.59 = (f32[192,2048]{1,0:T(8,128)S(1)}, f32[192,2048]{1,0:T(8,128)S(1)}, bf16[1024,2048]{1,0:T(8,128)(2,1)S(1)}, bf16[1024,2048]{1,0:T(8,128)(2,1)S(1)}) custom-call(bf16[96,1792]{1,0:T(8,128)(2,1)S(1)} %collective-permute-done.2.far_ref, bf16[96,3072]{1,0:T(8,128)(2,1)S(1)} %get-tuple-element.29.stay_ref, ...), custom_call_target="tpu_custom_call" | custom-call | flops 2818572288 | bytes 8388608 | tf_op jit(solution)/shard_map/pallas_call | solution.py:38
  38.7 0.0 collective-permute-done.1.far_ref
  38.7 0.0 copy-start
  38.7 0.0 copy-start.1
  38.8 3.3 %shard_map.60 = bf16[16,48,512]{2,1,0:T(8,128)(2,1)} custom-call(bf16[96,1280]{1,0:T(8,128)(2,1)S(1)} %collective-permute-done.1.far_ref, bf16[96,3072]{1,0:T(8,128)(2,1)S(1)} %get-tuple-element.29.stay_ref, f32[192,2048]{1,0:T(8,128)S(1)} %get-tuple-element.35.gate_in, f32[192,2048]{1,0:T(8,128)S(1)} %get-tuple-element.36.up_in, ...), custom_call_target="tpu_custom_call" | custom-call | flops 2013265920 | tf_op jit(solution)/shard_map/pallas_call | solution.py:38
  42.0 5.5 %all-to-all-start = ((bf16[16,48,512]{2,1,0:T(8,128)(2,1)}), bf16[16,48,512]{2,1,0:T(8,128)(2,1)S(1)}, u32[]{:S(2)}, u32[]{:S(2)}) async-start(bf16[16,48,512]{2,1,0:T(8,128)(2,1)} %shard_map.60), calls=%async_computation | async-start | bytes 1572864 | tf_op jit(solution)/shard_map/all_to_all | solution.py:34
  47.5 0.0 copy-done
  47.5 0.0 copy-done.1
  47.5 0.4 shard_map.55
  48.0 18.2 %all-to-all-done.recv_ref = bf16[16,48,512]{2,1,0:T(8,128)(2,1)S(1)} async-done(((bf16[16,48,512]{2,1,0:T(8,128)(2,1)}), bf16[16,48,512]{2,1,0:T(8,128)(2,1)S(1)}, u32[]{:S(2)}, u32[]{:S(2)}) %all-to-all-start) | async-done | bytes 786464 | tf_op jit(solution)/shard_map/all_to_all | solution.py:34
  66.2 1.3 %shard_map.61 = bf16[24,2,8192]{2,1,0:T(2,128)(2,1)} custom-call(bf16[192,192]{1,0:T(8,128)(2,1)S(1)} %get-tuple-element.22.picks_ref, f32[48,128]{1,0:T(8,128)S(1)} %get-tuple-element.23.column_ref, bf16[16,48,512]{2,1,0:T(8,128)(2,1)S(1)} %all-to-all-done.recv_ref), custom_call_target="tpu_custom_call" | custom-call | bytes 1572864 | tf_op jit(solution)/shard_map/pallas_call | solution.py:38
Async XLA Ops:
  19.7 2.0 %collective-permute-start = (bf16[96,3200]{1,0:T(8,128)(2,1)S(1)}, bf16[96,3200]{1,0:T(8,128)(2,1)S(1)}, u32[]{:S(2)}, u32[]{:S(2)}) collective-permute-start(bf16[96,3200]{1,0:T(8,128)(2,1)S(1)} %all_gather.3.own_ref), channel_id=1, source_target_pairs={{0,1},{1,0},{2,3},{3,2},{4,5},{5,4},{6,7},{7,6},{8,9},{9,8},{10,11... | collective-permute-start | bytes 1843208 | tf_op jit(solution)/shard_map/ppermute | solution.py:203
  22.6 11.0 %collective-permute-start.2 = (bf16[96,1792]{1,0:T(8,128)(2,1)S(1)}, bf16[96,1792]{1,0:T(8,128)(2,1)S(1)}, u32[]{:S(2)}, u32[]{:S(2)}) collective-permute-start(bf16[96,1792]{1,0:T(8,128)(2,1)S(1)} %get-tuple-element.25), channel_id=1, source_target_pairs={{0,2},{1,3},{2,0},{3,1},{4,6},{5,7},{6,4},{7,5},{8,10},{9,11},{10,... | collective-permute-start | bytes 1032200 | tf_op jit(solution)/shard_map/ppermute | solution.py:203
  24.2 14.5 %collective-permute-start.1 = (bf16[96,1280]{1,0:T(8,128)(2,1)S(1)}, bf16[96,1280]{1,0:T(8,128)(2,1)S(1)}, u32[]{:S(2)}, u32[]{:S(2)}) collective-permute-start(bf16[96,1280]{1,0:T(8,128)(2,1)S(1)} %get-tuple-element.24), channel_id=1, source_target_pairs={{0,2},{1,3},{2,0},{3,1},{4,6},{5,7},{6,4},{7,5},{8,10},{9,11},{10,... | collective-permute-start | bytes 737288 | tf_op jit(solution)/shard_map/ppermute | solution.py:203
  38.7 8.8 %copy-start = (s32[24,2]{0,1:T(2,128)S(1)}, s32[24,2]{0,1:T(2,128)}, u32[]{:S(2)}) copy-start(s32[24,2]{0,1:T(2,128)} %param.6) | copy-start | bytes 580
  38.7 8.8 %copy-start.1 = (f32[24,2]{0,1:T(2,128)S(1)}, f32[24,2]{0,1:T(2,128)}, u32[]{:S(2)}) copy-start(f32[24,2]{0,1:T(2,128)} %param.7) | copy-start | bytes 580
  42.0 24.2 %all-to-all-start = ((bf16[16,48,512]{2,1,0:T(8,128)(2,1)}), bf16[16,48,512]{2,1,0:T(8,128)(2,1)S(1)}, u32[]{:S(2)}, u32[]{:S(2)}) async-start(bf16[16,48,512]{2,1,0:T(8,128)(2,1)} %shard_map.60), calls=%async_computation | async-start | bytes 1572864 | tf_op jit(solution)/shard_map/all_to_all | solution.py:34

commit v8 on v7

--- a/solution.py
+++ b/solution.py
@@ -96,22 +96,24 @@
     return (iota((tall, rows), 1) == target).astype(jnp.bfloat16)
 
 
-def chosen_rows(own_ref, near_ref, expert, rows, tok_rows, capacity, spans):
-    core = lax.axis_index("ep") % 2
-    blocks = ((own_ref, core), (near_ref, 1 - core))
-    sels = [rows_of(ref[:, :128], source, expert, rows, tok_rows, capacity) for ref, source in blocks]
-    for start, stop in spans:
-        parts = [transposed_dot(sel, ref[:, 128 + start : 128 + stop]) for sel, (ref, _) in zip(sels, blocks)]
-        yield (parts[0] + parts[1]).astype(own_ref.dtype)
-
-
-def select_kernel(tok_rows, capacity, own_ref, near_ref, first_ref, second_ref):
-    rows, cut = first_ref.shape
-    expert = lax.axis_index("ep") ^ 2
-    spans = ((0, cut), (cut, cut + second_ref.shape[1]))
-    found = chosen_rows(own_ref, near_ref, expert, rows, tok_rows, capacity, spans)
-    for ref, part in zip((first_ref, second_ref), found):
-        ref[...] = part
+def picked(ref, source, expert, rows, tok_rows, capacity, start, stop):
+    sel = rows_of(ref[:, :128], source, expert, rows, tok_rows, capacity)
+    return transposed_dot(sel, ref[:, 128 + start : 128 + stop])
+
+
+def cut_kernel(in_ref, out_ref):
+    out_ref[...] = in_ref[:, : out_ref.shape[1]]
+
+
+def select_kernel(tok_rows, capacity, own_ref, near_ref, out_ref):
+    expert, core = lax.axis_index("ep") ^ 2, lax.axis_index("ep") % 2
+    rows, span = out_ref.shape
+    stop = own_ref.shape[1] - 128
+    parts = [
+        picked(ref, source, expert, rows, tok_rows, capacity, stop - span, stop)
+        for ref, source in ((own_ref, core), (near_ref, 1 - core))
+    ]
+    out_ref[...] = (parts[0] + parts[1]).astype(out_ref.dtype)
 
 
 def weight_copies(weights, held, sems, start, step):
@@ -124,14 +126,17 @@
     ]
 
 
-def fetch_kernel(step, tok_rows, capacity, own_ref, near_ref, *refs):
-    gate_hbm, up_hbm, stay_ref, gate_held, up_held, sems = refs
-    copies = weight_copies((gate_hbm, up_hbm), (gate_held, up_held), sems, 0, step)
+def fetch_kernel(start, step, tok_rows, capacity, swapped, *refs):
+    blocks = refs[: len(swapped)]
+    gate_hbm, up_hbm, rows_ref, gate_held, up_held, sems = refs[len(swapped) :]
+    copies = weight_copies((gate_hbm, up_hbm), (gate_held, up_held), sems, start, step)
     for copy in copies:
         copy.start()
-    rows, width = stay_ref.shape
-    expert = lax.axis_index("ep")
-    (stay_ref[...],) = chosen_rows(own_ref, near_ref, expert, rows, tok_rows, capacity, ((0, width),))
+    rows, width = rows_ref.shape
+    expert, core = lax.axis_index("ep"), lax.axis_index("ep") % 2
+    rows_ref[...] = sum(
+        picked(ref, core ^ other, expert, rows, tok_rows, capacity, 0, width) for ref, other in zip(blocks, swapped)
+    ).astype(rows_ref.dtype)
     for copy in copies:
         copy.wait()
 
@@ -143,31 +148,39 @@
     x_ref[pl.ds(pl.multiple_of((1 - chip) * rows, rows), rows), :] = far
 
 
-def first_kernel(step, far_ref, stay_ref, gate_held, up_held, gate_hbm, up_hbm, *refs):
-    gate_ref, up_ref, gate_rest, up_rest, x_ref, sems = refs
-    copies = weight_copies((gate_hbm, up_hbm), (gate_rest, up_rest), sems, gate_held.shape[0], step)
+def partial_product(x_ref, pieces, start):
+    total, base, stop = None, 0, start + x_ref.shape[1]
+    for piece in pieces:
+        low, high = max(base, start), min(base + piece.shape[0], stop)
+        if low < high:
+            product = exact_dot(x_ref[:, low - start : high - start], piece[low - base : high - base, :])
+            total = product if total is None else total + product
+        base = base + piece.shape[0]
+    return total
+
+
+def first_kernel(step, tok_rows, capacity, held, other_ref, part_ref, stay_ref, *refs):
+    gates, ups = refs[: 2 * held : 2], refs[1 : 2 * held : 2]
+    gate_hbm, up_hbm, gate_ref, up_ref, gate_rest, up_rest, x_ref, sems = refs[2 * held :]
+    copies = weight_copies((gate_hbm, up_hbm), (gate_rest, up_rest), sems, sum(ref.shape[0] for ref in gates), step)
     for copy in copies:
         copy.start()
-    cut = far_ref.shape[1]
-    gather_rows(x_ref, stay_ref[:, :cut], far_ref[...])
-    gate_ref[...] = exact_dot(x_ref[...], gate_held[:cut, :])
-    up_ref[...] = exact_dot(x_ref[...], up_held[:cut, :])
+    rows, cut = part_ref.shape
+    expert, core = lax.axis_index("ep"), lax.axis_index("ep") % 2
+    far = picked(other_ref, 1 - core, expert, rows, tok_rows, capacity, 0, cut) + part_ref[...].astype(jnp.float32)
+    gather_rows(x_ref, stay_ref[:, :cut], far.astype(x_ref.dtype))
+    gate_ref[...] = partial_product(x_ref, gates, 0)
+    up_ref[...] = partial_product(x_ref, ups, 0)
     for copy in copies:
         copy.wait()
 
 
 def second_kernel(folds, experts, far_ref, stay_ref, gate_in, up_in, *refs):
-    gate_held, up_held, gate_rest, up_rest, out_ref, x_ref, hidden_ref = refs
+    gates, ups, (out_ref, x_ref, hidden_ref) = refs[:-3:2], refs[1:-3:2], refs[-3:]
     cut = stay_ref.shape[1] - far_ref.shape[1]
     gather_rows(x_ref, stay_ref[:, cut:], far_ref[...])
-    middle = gate_held.shape[0] - cut
-    sums = []
-    for held, rest, total in ((gate_held, gate_rest, gate_in), (up_held, up_rest, up_in)):
-        total = total[...] + exact_dot(x_ref[:, middle:], rest[...])
-        if middle:
-            total = total + exact_dot(x_ref[:, :middle], held[cut:, :])
-        sums.append(total)
-    gate_val, up_val = sums
+    gate_val = gate_in[...] + partial_product(x_ref, gates, cut)
+    up_val = up_in[...] + partial_product(x_ref, ups, cut)
     hidden_ref[...] = gate_val / (1.0 + jnp.exp(-gate_val)) * up_val
     store_blocks(folds, experts, hidden_ref, out_ref)
 
@@ -190,9 +203,8 @@
     experts = 4
     rows = peers * capacity
     half = rows // 2
-    cut = 7 * width // 12
-    held = 2 * width // 3
-    rest = width - held
+    cut = 11 * width // 24
+    helds = (7 * width // 12, width // 6)
     step = 256
     kind = tokens.dtype
 
@@ -210,39 +222,40 @@
         scratch=[pltpu.VMEM((2, tok_rows), jnp.int32), pltpu.SemaphoreType.DMA((2,))],
     )
     own = lax.all_gather(packed, "et", axis=0, tiled=True)
-    near = swap(own, 1)
-    first, second = local_kernel(
-        functools.partial(select_kernel, tok_rows, capacity),
-        [array(half, cut), array(half, width - cut)],
-        (own, near),
-        flops=4 * own.shape[0] * half * width,
-        moved=4 * own.size,
-    )
-    far, later = swap(first, 2), swap(second, 2)
-    stay, gate_held, up_held = local_kernel(
-        functools.partial(fetch_kernel, step, tok_rows, capacity),
-        [array(half, width)] + [pltpu.VMEM((held, units), kind)] * 2,
-        (own, near),
+    part = local_kernel(cut_kernel, array(own.shape[0], 128 + cut), (own,))
+    near, far = swap(own, 1), swap(part, 2)
+    later = local_kernel(functools.partial(select_kernel, tok_rows, capacity), array(half, width - cut), (own, near))
+    later_far = swap(later, 2)
+
+    def fetch(start, held, blocks, swapped, span):
+        return local_kernel(
+            functools.partial(fetch_kernel, start, step, tok_rows, capacity, swapped),
+            [array(half, span)] + [pltpu.VMEM((held, units), kind)] * 2,
+            blocks,
+            (gate_local, up_local),
+            scratch=[pltpu.SemaphoreType.DMA((2, held // step))],
+        )
+
+    own, near, later = lax.optimization_barrier((own, near, later))
+    stay, *pieces = fetch(0, helds[0], (own, near), (0, 1), width)
+    far, *pieces = lax.optimization_barrier((far, *pieces))
+    far_other = swap(far, 1)
+    far_part, *more = fetch(helds[0], helds[1], (far,), (0,), cut)
+    far_other, *more = lax.optimization_barrier((far_other, *more))
+    pieces = (*pieces, *more)
+    rest = width - sum(helds)
+    gate_sum, up_sum, *last = local_kernel(
+        functools.partial(first_kernel, step, tok_rows, capacity, len(helds)),
+        [jax.ShapeDtypeStruct((rows, units), jnp.float32)] * 2 + [pltpu.VMEM((rest, units), kind)] * 2,
+        (far_other, far_part, stay, *pieces),
         (gate_local, up_local),
-        moved=8 * held * units,
-        scratch=[pltpu.SemaphoreType.DMA((2, held // step))],
-    )
-    far, gate_held, up_held = lax.optimization_barrier((far, gate_held, up_held))
-    gate_sum, up_sum, gate_rest, up_rest = local_kernel(
-        functools.partial(first_kernel, step),
-        [jax.ShapeDtypeStruct((rows, units), jnp.float32)] * 2 + [pltpu.VMEM((rest, units), kind)] * 2,
-        (far, stay, gate_held, up_held),
-        (gate_local, up_local),
-        flops=4 * rows * cut * units,
-        moved=4 * rest * units,
         scratch=[pltpu.VMEM((rows, cut), kind), pltpu.SemaphoreType.DMA((2, rest // step))],
     )
-    later, gate_rest, up_rest = lax.optimization_barrier((later, gate_rest, up_rest))
+    later_far, *last = lax.optimization_barrier((later_far, *last))
     return local_kernel(
         functools.partial(second_kernel, folds, experts),
         array(peers, capacity * folds, units // folds),
-        (later, stay, gate_sum, up_sum, gate_held, up_held, gate_rest, up_rest),
-        flops=4 * rows * (width - cut) * units,
+        (later_far, stay, gate_sum, up_sum, *pieces, *last),
         scratch=[pltpu.VMEM((rows, width - cut), kind), pltpu.VMEM((rows, units), jnp.float32)],
     )
 

time: 67.8 us -> 66.1 us (0.975)
  waiting for transfers between devices: 23.1 us -> 19.2 us
  Pallas kernels: 18 us -> 19.1 us
  starting transfers between devices: 7.56 us -> 8.56 us
    ppermute x3 -> x4, waiting for transfers between devices: 4.81 us -> 1 us  [swap(): return lax.ppermute(block, 'ep', [(i, i ^ bit) for i in range(experts)])]
    pallas_call x7 -> x9, Pallas kernels: 18 us -> 19.1 us  [local_kernel(): pl.pallas_call(kernel, out_shape=out_shape, in_specs=[WHOLE] * len(args)...]
    ppermute x3 -> x4, starting transfers between devices: 2.09 us -> 3.12 us  [swap(): return lax.ppermute(block, 'ep', [(i, i ^ bit) for i in range(experts)])]
  transfers between devices with their start and end apart: 4 -> 5, of which waited for: 3 -> 4; matrix products, arithmetic and copies ran while one was open for 0% -> 0% of each run, Pallas kernels for 17% -> 19%
where the time goes in v8:
time: 66.1 us; the launch traced here: 65.8 us
  waiting for transfers between devices  19.2 us (29%)
  Pallas kernels  19.1 us (29%)
  blocking collectives  18.8 us (28%)
  starting transfers between devices  8.56 us (13%)
    pallas_call x9, Pallas kernels, local_kernel(): pl.pallas_call(kernel, out_shape=out_shape, in_specs=[WHOLE] * len(args)...  19.1 us
    all_gather x1, blocking collectives, routed_by_columns(): own = lax.all_gather(packed, 'et', axis=0, tiled=True)  18.8 us
    all_to_all x1, waiting for transfers between devices, exchange(): lax.all_to_all(blocks, ('et', 'ep'), split_axis=0, concat_axis=0, tiled=T...  18.2 us
    all_to_all x1, starting transfers between devices, exchange(): lax.all_to_all(blocks, ('et', 'ep'), split_axis=0, concat_axis=0, tiled=T...  5.44 us
    ppermute x4, starting transfers between devices, swap(): return lax.ppermute(block, 'ep', [(i, i ^ bit) for i in range(experts)])  3.12 us
  transfers between devices with their start and end apart: 5, of which 4 were waited for; matrix products, arithmetic and copies ran while one was open for 0% of the time, Pallas kernels for 19%

profile of v8, /device:TPU:0, one launch (start us, length us, event | category | flops | bytes accessed | tf_op | source)
XLA Modules:
  0.0 65.8 jit_solution(4588467363000881535)
XLA Ops:
  0.0 0.9 %shard_map.56 = bf16[24,3200]{1,0:T(8,128)(2,1)S(1)} custom-call(s32[2,24]{1,0:T(2,128)} %bitcast.4, bf16[24,3072]{1,0:T(8,128)(2,1)} %tokens_hbm.1), custom_call_target="tpu_custom_call" | custom-call | tf_op jit(solution)/shard_map/pallas_call | solution.py:38
  1.0 18.8 %all_gather.3.own_ref.in_ref.refs_0_ = bf16[96,3200]{1,0:T(8,128)(2,1)S(1)} all-gather(bf16[24,3200]{1,0:T(8,128)(2,1)S(1)} %shard_map.56), channel_id=1, replica_groups=mesh['groups'=2,'et'=4,'ep'=4] {'et'}, dimensions={0}, use_global_device_ids=true | all-gather | bytes 768000 | tf_op jit(solution)/shard_map/all_gather | solution.py:224
  19.7 0.0 collective-permute-start
  19.7 1.6 %collective-permute-start.2 = (bf16[96,1536]{1,0:T(8,128)(2,1)S(1)}, bf16[96,1536]{1,0:T(8,128)(2,1)S(1)}, u32[]{:S(2)}, u32[]{:S(2)}) collective-permute-start(bf16[96,1536]{1,0:T(8,128)(2,1)S(1)} %shard_map.58), channel_id=1, source_target_pairs={{0,2},{1,3},{2,0},{3,1},{4,6},{5,7},{6,4},{7,5},{8,10},{9,11},{10,... | collective-permute-start | bytes 884744 | tf_op jit(solution)/shard_map/ppermute | solution.py:215
  21.3 0.5 collective-permute-done.near_ref.refs_1_
  21.8 0.7 %shard_map.57 = bf16[96,1664]{1,0:T(8,128)(2,1)S(1)} custom-call(bf16[96,3200]{1,0:T(8,128)(2,1)S(1)} %all_gather.3.own_ref.in_ref.refs_0_, bf16[96,3200]{1,0:T(8,128)(2,1)S(1)} %collective-permute-done.near_ref.refs_1_), custom_call_target="tpu_custom_call" | custom-call | tf_op jit(solution)/shard_map/pallas_call | solution.py:38
  22.5 1.6 %collective-permute-start.1 = (bf16[96,1664]{1,0:T(8,128)(2,1)S(1)}, bf16[96,1664]{1,0:T(8,128)(2,1)S(1)}, u32[]{:S(2)}, u32[]{:S(2)}) collective-permute-start(bf16[96,1664]{1,0:T(8,128)(2,1)S(1)} %shard_map.57), channel_id=1, source_target_pairs={{0,2},{1,3},{2,0},{3,1},{4,6},{5,7},{6,4},{7,5},{8,10},{9,11},{10,... | collective-permute-start | bytes 958472 | tf_op jit(solution)/shard_map/ppermute | solution.py:215
  24.1 5.4 %shard_map.59 = (bf16[96,3072]{1,0:T(8,128)(2,1)S(1)}, bf16[1792,2048]{1,0:T(8,128)(2,1)S(1)}, bf16[1792,2048]{1,0:T(8,128)(2,1)S(1)}) custom-call(bf16[96,3200]{1,0:T(8,128)(2,1)S(1)} %all_gather.3.own_ref.in_ref.refs_0_, bf16[96,3200]{1,0:T(8,128)(2,1)S(1)} %collective-permute-done.near_ref.refs_1_, bf16[3072,2048]{1,0:T(8,128)(2,1)} %bitcast.7, ...), custom_call_target="tpu_custom_call" | custom-call | tf_op jit(solution)/shard_map/pallas_call | solution.py:38
  29.5 0.1 collective-permute-done.2.refs_0_
  29.6 0.0 collective-permute-start.3
  29.6 2.2 %shard_map.60 = (bf16[96,1408]{1,0:T(8,128)(2,1)S(1)}, bf16[512,2048]{1,0:T(8,128)(2,1)S(1)}, bf16[512,2048]{1,0:T(8,128)(2,1)S(1)}) custom-call(bf16[96,1536]{1,0:T(8,128)(2,1)S(1)} %collective-permute-done.2.refs_0_, bf16[3072,2048]{1,0:T(8,128)(2,1)} %bitcast.8, bf16[3072,2048]{1,0:T(8,128)(2,1)} %bitcast.11), custom_call_target="tpu_custom_call" | custom-call | tf_op jit(solution)/shard_map/pallas_call | solution.py:38
  31.8 0.0 collective-permute-done.3.other_ref
  31.9 3.8 %shard_map.61 = (f32[192,2048]{1,0:T(8,128)S(1)}, f32[192,2048]{1,0:T(8,128)S(1)}, bf16[768,2048]{1,0:T(8,128)(2,1)S(1)}, bf16[768,2048]{1,0:T(8,128)(2,1)S(1)}) custom-call(bf16[96,1536]{1,0:T(8,128)(2,1)S(1)} %collective-permute-done.3.other_ref, bf16[96,1408]{1,0:T(8,128)(2,1)S(1)} %get-tuple-element.38.part_ref, ...), custom_call_target="tpu_custom_call" | custom-call | tf_op jit(solution)/shard_map/pallas_call | solution.py:38
  35.6 0.4 collective-permute-done.1.far_ref
  36.1 0.0 copy-start
  36.1 0.0 copy-start.1
  36.1 4.3 %shard_map.62 = bf16[16,48,512]{2,1,0:T(8,128)(2,1)} custom-call(bf16[96,1664]{1,0:T(8,128)(2,1)S(1)} %collective-permute-done.1.far_ref, bf16[96,3072]{1,0:T(8,128)(2,1)S(1)} %get-tuple-element.39.stay_ref, f32[192,2048]{1,0:T(8,128)S(1)} %get-tuple-element.47.gate_in, f32[192,2048]{1,0:T(8,128)S(1)} %get-tuple-element.48.up_in, ...), custom_call_target="tpu_custom_call" | custom-call | tf_op jit(solution)/shard_map/pallas_call | solution.py:38
  40.3 5.4 %all-to-all-start = ((bf16[16,48,512]{2,1,0:T(8,128)(2,1)}), bf16[16,48,512]{2,1,0:T(8,128)(2,1)S(1)}, u32[]{:S(2)}, u32[]{:S(2)}) async-start(bf16[16,48,512]{2,1,0:T(8,128)(2,1)} %shard_map.62), calls=%async_computation | async-start | bytes 1572864 | tf_op jit(solution)/shard_map/all_to_all | solution.py:34
  45.8 0.0 copy-done
  45.8 0.0 copy-done.1
  45.8 0.4 shard_map.55
  46.2 18.2 %all-to-all-done.recv_ref = bf16[16,48,512]{2,1,0:T(8,128)(2,1)S(1)} async-done(((bf16[16,48,512]{2,1,0:T(8,128)(2,1)}), bf16[16,48,512]{2,1,0:T(8,128)(2,1)S(1)}, u32[]{:S(2)}, u32[]{:S(2)}) %all-to-all-start) | async-done | bytes 786464 | tf_op jit(solution)/shard_map/all_to_all | solution.py:34
  64.5 1.3 %shard_map.63 = bf16[24,2,8192]{2,1,0:T(2,128)(2,1)} custom-call(bf16[192,192]{1,0:T(8,128)(2,1)S(1)} %get-tuple-element.28.picks_ref, f32[48,128]{1,0:T(8,128)S(1)} %get-tuple-element.29.column_ref, bf16[16,48,512]{2,1,0:T(8,128)(2,1)S(1)} %all-to-all-done.recv_ref), custom_call_target="tpu_custom_call" | custom-call | bytes 1572864 | tf_op jit(solution)/shard_map/pallas_call | solution.py:38
  (1 shorter events, 0.0 us)
Async XLA Ops:
  19.7 2.0 %collective-permute-start = (bf16[96,3200]{1,0:T(8,128)(2,1)S(1)}, bf16[96,3200]{1,0:T(8,128)(2,1)S(1)}, u32[]{:S(2)}, u32[]{:S(2)}) collective-permute-start(bf16[96,3200]{1,0:T(8,128)(2,1)S(1)} %all_gather.3.own_ref.in_ref.refs_0_), channel_id=1, source_target_pairs={{0,1},{1,0},{2,3},{3,2},{4,5},{5,4},{6,7},{7,6},{8,9},{9,8},{10,11... | collective-permute-start | bytes 1843208 | tf_op jit(solution)/shard_map/ppermute | solution.py:215
  19.7 9.9 %collective-permute-start.2 = (bf16[96,1536]{1,0:T(8,128)(2,1)S(1)}, bf16[96,1536]{1,0:T(8,128)(2,1)S(1)}, u32[]{:S(2)}, u32[]{:S(2)}) collective-permute-start(bf16[96,1536]{1,0:T(8,128)(2,1)S(1)} %shard_map.58), channel_id=1, source_target_pairs={{0,2},{1,3},{2,0},{3,1},{4,6},{5,7},{6,4},{7,5},{8,10},{9,11},{10,... | collective-permute-start | bytes 884744 | tf_op jit(solution)/shard_map/ppermute | solution.py:215
  22.5 13.6 %collective-permute-start.1 = (bf16[96,1664]{1,0:T(8,128)(2,1)S(1)}, bf16[96,1664]{1,0:T(8,128)(2,1)S(1)}, u32[]{:S(2)}, u32[]{:S(2)}) collective-permute-start(bf16[96,1664]{1,0:T(8,128)(2,1)S(1)} %shard_map.57), channel_id=1, source_target_pairs={{0,2},{1,3},{2,0},{3,1},{4,6},{5,7},{6,4},{7,5},{8,10},{9,11},{10,... | collective-permute-start | bytes 958472 | tf_op jit(solution)/shard_map/ppermute | solution.py:215
  29.6 2.2 %collective-permute-start.3 = (bf16[96,1536]{1,0:T(8,128)(2,1)S(1)}, bf16[96,1536]{1,0:T(8,128)(2,1)S(1)}, u32[]{:S(2)}, u32[]{:S(2)}) collective-permute-start(bf16[96,1536]{1,0:T(8,128)(2,1)S(1)} %collective-permute-done.2.refs_0_), channel_id=1, source_target_pairs={{0,1},{1,0},{2,3},{3,2},{4,5},{5,4},{6,7},{7,6},{8,9},{9,8},{10,11... | collective-permute-start | bytes 884744 | tf_op jit(solution)/shard_map/ppermute | solution.py:215
  36.1 9.7 %copy-start = (s32[24,2]{0,1:T(2,128)S(1)}, s32[24,2]{0,1:T(2,128)}, u32[]{:S(2)}) copy-start(s32[24,2]{0,1:T(2,128)} %param.6) | copy-start | bytes 580
  36.1 9.7 %copy-start.1 = (f32[24,2]{0,1:T(2,128)S(1)}, f32[24,2]{0,1:T(2,128)}, u32[]{:S(2)}) copy-start(f32[24,2]{0,1:T(2,128)} %param.7) | copy-start | bytes 580
  40.3 24.2 %all-to-all-start = ((bf16[16,48,512]{2,1,0:T(8,128)(2,1)}), bf16[16,48,512]{2,1,0:T(8,128)(2,1)S(1)}, u32[]{:S(2)}, u32[]{:S(2)}) async-start(bf16[16,48,512]{2,1,0:T(8,128)(2,1)} %shard_map.62), calls=%async_computation | async-start | bytes 1572864 | tf_op jit(solution)/shard_map/all_to_all | solution.py:34

commit v9 on v8

--- a/solution.py
+++ b/solution.py
@@ -128,8 +128,8 @@
 
 def fetch_kernel(start, step, tok_rows, capacity, swapped, *refs):
     blocks = refs[: len(swapped)]
-    gate_hbm, up_hbm, rows_ref, gate_held, up_held, sems = refs[len(swapped) :]
-    copies = weight_copies((gate_hbm, up_hbm), (gate_held, up_held), sems, start, step)
+    up_hbm, rows_ref, up_held, sems = refs[len(swapped) :]
+    copies = weight_copies((up_hbm,), (up_held,), sems, start, step)
     for copy in copies:
         copy.start()
     rows, width = rows_ref.shape
@@ -160,26 +160,26 @@
 
 
 def first_kernel(step, tok_rows, capacity, held, other_ref, part_ref, stay_ref, *refs):
-    gates, ups = refs[: 2 * held : 2], refs[1 : 2 * held : 2]
-    gate_hbm, up_hbm, gate_ref, up_ref, gate_rest, up_rest, x_ref, sems = refs[2 * held :]
-    copies = weight_copies((gate_hbm, up_hbm), (gate_rest, up_rest), sems, sum(ref.shape[0] for ref in gates), step)
+    gate_all, ups = refs[0], refs[1 : 1 + held]
+    up_hbm, gate_ref, up_ref, up_rest, x_ref, sems = refs[1 + held :]
+    copies = weight_copies((up_hbm,), (up_rest,), sems, sum(ref.shape[0] for ref in ups), step)
     for copy in copies:
         copy.start()
     rows, cut = part_ref.shape
     expert, core = lax.axis_index("ep"), lax.axis_index("ep") % 2
     far = picked(other_ref, 1 - core, expert, rows, tok_rows, capacity, 0, cut) + part_ref[...].astype(jnp.float32)
     gather_rows(x_ref, stay_ref[:, :cut], far.astype(x_ref.dtype))
-    gate_ref[...] = partial_product(x_ref, gates, 0)
+    gate_ref[...] = partial_product(x_ref, (gate_all.at[0],), 0)
     up_ref[...] = partial_product(x_ref, ups, 0)
     for copy in copies:
         copy.wait()
 
 
 def second_kernel(folds, experts, far_ref, stay_ref, gate_in, up_in, *refs):
-    gates, ups, (out_ref, x_ref, hidden_ref) = refs[:-3:2], refs[1:-3:2], refs[-3:]
+    gate_all, ups, (out_ref, x_ref, hidden_ref) = refs[0], refs[1:-3], refs[-3:]
     cut = stay_ref.shape[1] - far_ref.shape[1]
     gather_rows(x_ref, stay_ref[:, cut:], far_ref[...])
-    gate_val = gate_in[...] + partial_product(x_ref, gates, cut)
+    gate_val = gate_in[...] + partial_product(x_ref, (gate_all.at[0],), cut)
     up_val = up_in[...] + partial_product(x_ref, ups, cut)
     hidden_ref[...] = gate_val / (1.0 + jnp.exp(-gate_val)) * up_val
     store_blocks(folds, experts, hidden_ref, out_ref)
@@ -197,14 +197,14 @@
         out_ref[peer] = jnp.concatenate(pieces, axis=0).astype(out_ref.dtype)
 
 
-def routed_by_columns(tokens, expert_ids, gate_local, up_local, peers, capacity, folds):
+def routed_by_columns(tokens, expert_ids, gate_whole, up_local, peers, capacity, folds):
     tok_rows, width = tokens.shape
-    units = gate_local.shape[1]
+    units = up_local.shape[1]
     experts = 4
     rows = peers * capacity
     half = rows // 2
     cut = 11 * width // 24
-    helds = (7 * width // 12, width // 6)
+    helds = (2 * width // 3, width // 6)
     step = 256
     kind = tokens.dtype
 
@@ -230,10 +230,10 @@
     def fetch(start, held, blocks, swapped, span):
         return local_kernel(
             functools.partial(fetch_kernel, start, step, tok_rows, capacity, swapped),
-            [array(half, span)] + [pltpu.VMEM((held, units), kind)] * 2,
+            [array(half, span), pltpu.VMEM((held, units), kind)],
             blocks,
-            (gate_local, up_local),
-            scratch=[pltpu.SemaphoreType.DMA((2, held // step))],
+            (up_local,),
+            scratch=[pltpu.SemaphoreType.DMA((1, held // step))],
         )
 
     own, near, later = lax.optimization_barrier((own, near, later))
@@ -246,16 +246,16 @@
     rest = width - sum(helds)
     gate_sum, up_sum, *last = local_kernel(
         functools.partial(first_kernel, step, tok_rows, capacity, len(helds)),
-        [jax.ShapeDtypeStruct((rows, units), jnp.float32)] * 2 + [pltpu.VMEM((rest, units), kind)] * 2,
-        (far_other, far_part, stay, *pieces),
-        (gate_local, up_local),
-        scratch=[pltpu.VMEM((rows, cut), kind), pltpu.SemaphoreType.DMA((2, rest // step))],
+        [jax.ShapeDtypeStruct((rows, units), jnp.float32)] * 2 + [pltpu.VMEM((rest, units), kind)],
+        (far_other, far_part, stay, gate_whole, *pieces),
+        (up_local,),
+        scratch=[pltpu.VMEM((rows, cut), kind), pltpu.SemaphoreType.DMA((1, rest // step))],
     )
     later_far, *last = lax.optimization_barrier((later_far, *last))
     return local_kernel(
         functools.partial(second_kernel, folds, experts),
         array(peers, capacity * folds, units // folds),
-        (later_far, stay, gate_sum, up_sum, *pieces, *last),
+        (later_far, stay, gate_sum, up_sum, gate_whole, *pieces, *last),
         scratch=[pltpu.VMEM((rows, width - cut), kind), pltpu.VMEM((rows, units), jnp.float32)],
     )
 
@@ -330,7 +330,7 @@
     up_local = w_up[0]
     if experts == 4 and tensor_size == 4:
         folds = 4
-        blocks = routed_by_columns(tokens, expert_ids, gate_local, up_local, peers, capacity, folds)
+        blocks = routed_by_columns(tokens, expert_ids, w_gate, up_local, peers, capacity, folds)
         return finish(expert_ids, gate_weights, exchange(blocks), experts, folds)
     slot_pairs = place_slots(expert_ids, experts, capacity)
     selector = build_select(slot_pairs, experts * capacity)

time: 66.1 us -> 66.1 us (level)
  Pallas kernels: 19.1 us -> 16.9 us
  local copies, waits for them, and re-layouts: 0.01 us -> 1.18 us
  waiting for transfers between devices: 19.2 us -> 20.3 us
    pallas_call x9, Pallas kernels: 19.1 us -> 16.9 us  [local_kernel(): pl.pallas_call(kernel, out_shape=out_shape, in_specs=[WHOLE] * len(args)...]
    unnamed x4 -> x10, local copies, waits for them, and re-layouts: 0.01 us -> 1.18 us
    ppermute x4, waiting for transfers between devices: 1 us -> 2.06 us  [swap(): return lax.ppermute(block, 'ep', [(i, i ^ bit) for i in range(experts)])]
  transfers between devices with their start and end apart: 5 -> 5, of which waited for: 4 -> 4; matrix products, arithmetic and copies ran while one was open for 0% -> 0% of each run, Pallas kernels for 19% -> 16%
where the time goes in v9:
time: 66.1 us; the launch traced here: 65.8 us
  waiting for transfers between devices  20.3 us (31%)
  blocking collectives  18.8 us (28%)
  Pallas kernels  16.9 us (26%)
  starting transfers between devices  8.56 us (13%)
  local copies, waits for them, and re-layouts  1.18 us (2%)
    all_gather x1, blocking collectives, routed_by_columns(): own = lax.all_gather(packed, 'et', axis=0, tiled=True)  18.8 us
    all_to_all x1, waiting for transfers between devices, exchange(): lax.all_to_all(blocks, ('et', 'ep'), split_axis=0, concat_axis=0, tiled=T...  18.2 us
    pallas_call x9, Pallas kernels, local_kernel(): pl.pallas_call(kernel, out_shape=out_shape, in_specs=[WHOLE] * len(args)...  16.9 us
    all_to_all x1, starting transfers between devices, exchange(): lax.all_to_all(blocks, ('et', 'ep'), split_axis=0, concat_axis=0, tiled=T...  5.44 us
    ppermute x4, starting transfers between devices, swap(): return lax.ppermute(block, 'ep', [(i, i ^ bit) for i in range(experts)])  3.12 us
    ppermute x4, waiting for transfers between devices, swap(): return lax.ppermute(block, 'ep', [(i, i ^ bit) for i in range(experts)])  2.06 us
  transfers between devices with their start and end apart: 5, of which 4 were waited for; matrix products, arithmetic and copies ran while one was open for 0% of the time, Pallas kernels for 16%

profile of v9, /device:TPU:0, one launch (start us, length us, event | category | flops | bytes accessed | tf_op | source)
XLA Modules:
  0.0 65.8 jit_solution(9573892552724628784)
XLA Ops:
  0.0 0.9 %shard_map.56 = bf16[24,3200]{1,0:T(8,128)(2,1)S(1)} custom-call(s32[2,24]{1,0:T(2,128)} %bitcast.5, bf16[24,3072]{1,0:T(8,128)(2,1)} %tokens_hbm.1), custom_call_target="tpu_custom_call" | custom-call | tf_op jit(solution)/shard_map/pallas_call | solution.py:38
  1.0 18.8 %all_gather.3.own_ref.in_ref.refs_0_ = bf16[96,3200]{1,0:T(8,128)(2,1)S(1)} all-gather(bf16[24,3200]{1,0:T(8,128)(2,1)S(1)} %shard_map.56), channel_id=1, replica_groups=mesh['groups'=2,'et'=4,'ep'=4] {'et'}, dimensions={0}, use_global_device_ids=true | all-gather | bytes 768000 | tf_op jit(solution)/shard_map/all_gather | solution.py:224
  19.7 0.0 collective-permute-start
  19.7 1.6 %collective-permute-start.2 = (bf16[96,1536]{1,0:T(8,128)(2,1)S(1)}, bf16[96,1536]{1,0:T(8,128)(2,1)S(1)}, u32[]{:S(2)}, u32[]{:S(2)}) collective-permute-start(bf16[96,1536]{1,0:T(8,128)(2,1)S(1)} %shard_map.58), channel_id=1, source_target_pairs={{0,2},{1,3},{2,0},{3,1},{4,6},{5,7},{6,4},{7,5},{8,10},{9,11},{10,... | collective-permute-start | bytes 884744 | tf_op jit(solution)/shard_map/ppermute | solution.py:215
  21.3 0.5 collective-permute-done.near_ref.refs_1_
  21.8 0.7 %shard_map.57 = bf16[96,1664]{1,0:T(8,128)(2,1)S(1)} custom-call(bf16[96,3200]{1,0:T(8,128)(2,1)S(1)} %all_gather.3.own_ref.in_ref.refs_0_, bf16[96,3200]{1,0:T(8,128)(2,1)S(1)} %collective-permute-done.near_ref.refs_1_), custom_call_target="tpu_custom_call" | custom-call | tf_op jit(solution)/shard_map/pallas_call | solution.py:38
  22.5 1.6 %collective-permute-start.1 = (bf16[96,1664]{1,0:T(8,128)(2,1)S(1)}, bf16[96,1664]{1,0:T(8,128)(2,1)S(1)}, u32[]{:S(2)}, u32[]{:S(2)}) collective-permute-start(bf16[96,1664]{1,0:T(8,128)(2,1)S(1)} %shard_map.57), channel_id=1, source_target_pairs={{0,2},{1,3},{2,0},{3,1},{4,6},{5,7},{6,4},{7,5},{8,10},{9,11},{10,... | collective-permute-start | bytes 958472 | tf_op jit(solution)/shard_map/ppermute | solution.py:215
  24.1 0.0 slice-start
  24.1 0.0 slice-start.1
  24.1 4.2 %shard_map.59 = (bf16[96,3072]{1,0:T(8,128)(2,1)S(1)}, bf16[2048,2048]{1,0:T(8,128)(2,1)S(1)}) custom-call(bf16[96,3200]{1,0:T(8,128)(2,1)S(1)} %all_gather.3.own_ref.in_ref.refs_0_, bf16[96,3200]{1,0:T(8,128)(2,1)S(1)} %collective-permute-done.near_ref.refs_1_, bf16[3072,2048]{1,0:T(8,128)(2,1)} %bitcast.8), custom_call_target="tpu_custom_call" | custom-call | tf_op jit(solution)/shard_map/pallas_call | solution.py:38
  28.3 1.3 %collective-permute-done.2.refs_0_ = bf16[96,1536]{1,0:T(8,128)(2,1)S(1)} collective-permute-done((bf16[96,1536]{1,0:T(8,128)(2,1)S(1)}, bf16[96,1536]{1,0:T(8,128)(2,1)S(1)}, u32[]{:S(2)}, u32[]{:S(2)}) %collective-permute-start.2) | collective-permute-done | bytes 294944 | tf_op jit(solution)/shard_map/ppermute | solution.py:215
  29.6 0.0 slice-start.2
  29.6 0.0 collective-permute-start.3
  29.6 1.7 %shard_map.60 = (bf16[96,1408]{1,0:T(8,128)(2,1)S(1)}, bf16[512,2048]{1,0:T(8,128)(2,1)S(1)}) custom-call(bf16[96,1536]{1,0:T(8,128)(2,1)S(1)} %collective-permute-done.2.refs_0_, bf16[3072,2048]{1,0:T(8,128)(2,1)} %bitcast.9), custom_call_target="tpu_custom_call" | custom-call | tf_op jit(solution)/shard_map/pallas_call | solution.py:38
  31.3 0.0 collective-permute-done.3.other_ref
  31.4 0.0 slice-done
  31.4 0.0 slice-done.1
  31.4 1.2 %slice-done.2 = s8[4194304]{0:T(1024)(128)(4,1)S(1)} async-done(((s8[12582912]{0:T(1024)(128)(4,1)}), s8[4194304]{0:T(1024)(128)(4,1)S(1)}, s32[]{:S(2)}) %slice-start.2) | async-done | bytes 4194328
  32.5 3.3 %shard_map.61 = (f32[192,2048]{1,0:T(8,128)S(1)}, f32[192,2048]{1,0:T(8,128)S(1)}, bf16[512,2048]{1,0:T(8,128)(2,1)S(1)}) custom-call(bf16[96,1536]{1,0:T(8,128)(2,1)S(1)} %collective-permute-done.3.other_ref, bf16[96,1408]{1,0:T(8,128)(2,1)S(1)} %get-tuple-element.30.part_ref, bf16[96,3072]{1,0:T(8,128)(2,1)S(1)} %get-tuple-element.31.stay_ref, ...), custom_call_target="tpu_custom_call" | custom-call | tf_op jit(solution)/shard_map/pallas_call | solution.py:38
  35.8 0.3 collective-permute-done.1.far_ref
  36.1 0.0 copy-start
  36.1 0.0 copy-start.1
  36.1 4.3 %shard_map.62 = bf16[16,48,512]{2,1,0:T(8,128)(2,1)} custom-call(bf16[96,1664]{1,0:T(8,128)(2,1)S(1)} %collective-permute-done.1.far_ref, bf16[96,3072]{1,0:T(8,128)(2,1)S(1)} %get-tuple-element.31.stay_ref, f32[192,2048]{1,0:T(8,128)S(1)} %get-tuple-element.36.gate_in, f32[192,2048]{1,0:T(8,128)S(1)} %get-tuple-element.37.up_in, ...), custom_call_target="tpu_custom_call" | custom-call | tf_op jit(solution)/shard_map/pallas_call | solution.py:38
  40.4 5.4 %all-to-all-start = ((bf16[16,48,512]{2,1,0:T(8,128)(2,1)}), bf16[16,48,512]{2,1,0:T(8,128)(2,1)S(1)}, u32[]{:S(2)}, u32[]{:S(2)}) async-start(bf16[16,48,512]{2,1,0:T(8,128)(2,1)} %shard_map.62), calls=%async_computation | async-start | bytes 1572864 | tf_op jit(solution)/shard_map/all_to_all | solution.py:34
  45.8 0.0 copy-done
  45.9 0.0 copy-done.1
  45.9 0.4 shard_map.55
  46.3 18.2 %all-to-all-done.recv_ref = bf16[16,48,512]{2,1,0:T(8,128)(2,1)S(1)} async-done(((bf16[16,48,512]{2,1,0:T(8,128)(2,1)}), bf16[16,48,512]{2,1,0:T(8,128)(2,1)S(1)}, u32[]{:S(2)}, u32[]{:S(2)}) %all-to-all-start) | async-done | bytes 786464 | tf_op jit(solution)/shard_map/all_to_all | solution.py:34
  64.6 1.3 %shard_map.63 = bf16[24,2,8192]{2,1,0:T(2,128)(2,1)} custom-call(bf16[192,192]{1,0:T(8,128)(2,1)S(1)} %get-tuple-element.22.picks_ref, f32[48,128]{1,0:T(8,128)S(1)} %get-tuple-element.23.column_ref, bf16[16,48,512]{2,1,0:T(8,128)(2,1)S(1)} %all-to-all-done.recv_ref), custom_call_target="tpu_custom_call" | custom-call | bytes 1572864 | tf_op jit(solution)/shard_map/pallas_call | solution.py:38
  (2 shorter events, 0.0 us)
Async XLA Ops:
  19.7 2.0 %collective-permute-start = (bf16[96,3200]{1,0:T(8,128)(2,1)S(1)}, bf16[96,3200]{1,0:T(8,128)(2,1)S(1)}, u32[]{:S(2)}, u32[]{:S(2)}) collective-permute-start(bf16[96,3200]{1,0:T(8,128)(2,1)S(1)} %all_gather.3.own_ref.in_ref.refs_0_), channel_id=1, source_target_pairs={{0,1},{1,0},{2,3},{3,2},{4,5},{5,4},{6,7},{7,6},{8,9},{9,8},{10,11... | collective-permute-start | bytes 1843208 | tf_op jit(solution)/shard_map/ppermute | solution.py:215
  19.7 9.9 %collective-permute-start.2 = (bf16[96,1536]{1,0:T(8,128)(2,1)S(1)}, bf16[96,1536]{1,0:T(8,128)(2,1)S(1)}, u32[]{:S(2)}, u32[]{:S(2)}) collective-permute-start(bf16[96,1536]{1,0:T(8,128)(2,1)S(1)} %shard_map.58), channel_id=1, source_target_pairs={{0,2},{1,3},{2,0},{3,1},{4,6},{5,7},{6,4},{7,5},{8,10},{9,11},{10,... | collective-permute-start | bytes 884744 | tf_op jit(solution)/shard_map/ppermute | solution.py:215
  22.5 13.6 %collective-permute-start.1 = (bf16[96,1664]{1,0:T(8,128)(2,1)S(1)}, bf16[96,1664]{1,0:T(8,128)(2,1)S(1)}, u32[]{:S(2)}, u32[]{:S(2)}) collective-permute-start(bf16[96,1664]{1,0:T(8,128)(2,1)S(1)} %shard_map.57), channel_id=1, source_target_pairs={{0,2},{1,3},{2,0},{3,1},{4,6},{5,7},{6,4},{7,5},{8,10},{9,11},{10,... | collective-permute-start | bytes 958472 | tf_op jit(solution)/shard_map/ppermute | solution.py:215
  24.1 7.3 %slice-start = ((s8[12582912]{0:T(1024)(128)(4,1)}), s8[4194304]{0:T(1024)(128)(4,1)S(1)}, s32[]{:S(2)}) async-start(s8[12582912]{0:T(1024)(128)(4,1)} %bitcast.3), calls=%async_computation.1 | async-start | bytes 8388608
  24.1 7.3 %slice-start.1 = ((s8[12582912]{0:T(1024)(128)(4,1)}), s8[4194304]{0:T(1024)(128)(4,1)S(1)}, s32[]{:S(2)}) async-start(s8[12582912]{0:T(1024)(128)(4,1)} %bitcast.3), calls=%async_computation.2 | async-start | bytes 8388608
  29.6 2.9 %slice-start.2 = ((s8[12582912]{0:T(1024)(128)(4,1)}), s8[4194304]{0:T(1024)(128)(4,1)S(1)}, s32[]{:S(2)}) async-start(s8[12582912]{0:T(1024)(128)(4,1)} %bitcast.3), calls=%async_computation.3 | async-start | bytes 8388608
  29.6 1.7 %collective-permute-start.3 = (bf16[96,1536]{1,0:T(8,128)(2,1)S(1)}, bf16[96,1536]{1,0:T(8,128)(2,1)S(1)}, u32[]{:S(2)}, u32[]{:S(2)}) collective-permute-start(bf16[96,1536]{1,0:T(8,128)(2,1)S(1)} %collective-permute-done.2.refs_0_), channel_id=1, source_target_pairs={{0,1},{1,0},{2,3},{3,2},{4,5},{5,4},{6,7},{7,6},{8,9},{9,8},{10,11... | collective-permute-start | bytes 884744 | tf_op jit(solution)/shard_map/ppermute | solution.py:215
  36.1 9.8 %copy-start = (s32[24,2]{0,1:T(2,128)S(1)}, s32[24,2]{0,1:T(2,128)}, u32[]{:S(2)}) copy-start(s32[24,2]{0,1:T(2,128)} %param.6) | copy-start | bytes 580
  36.1 9.8 %copy-start.1 = (f32[24,2]{0,1:T(2,128)S(1)}, f32[24,2]{0,1:T(2,128)}, u32[]{:S(2)}) copy-start(f32[24,2]{0,1:T(2,128)} %param.7) | copy-start | bytes 580
  40.4 24.2 %all-to-all-start = ((bf16[16,48,512]{2,1,0:T(8,128)(2,1)}), bf16[16,48,512]{2,1,0:T(8,128)(2,1)S(1)}, u32[]{:S(2)}, u32[]{:S(2)}) async-start(bf16[16,48,512]{2,1,0:T(8,128)(2,1)} %shard_map.62), calls=%async_computation | async-start | bytes 1572864 | tf_op jit(solution)/shard_map/all_to_all | solution.py:34

commit v10 on v8

--- a/solution.py
+++ b/solution.py
@@ -105,15 +105,18 @@
     out_ref[...] = in_ref[:, : out_ref.shape[1]]
 
 
-def select_kernel(tok_rows, capacity, own_ref, near_ref, out_ref):
+def select_kernel(tok_rows, capacity, own_ref, near_ref, *outs):
     expert, core = lax.axis_index("ep") ^ 2, lax.axis_index("ep") % 2
-    rows, span = out_ref.shape
-    stop = own_ref.shape[1] - 128
-    parts = [
-        picked(ref, source, expert, rows, tok_rows, capacity, stop - span, stop)
+    rows = outs[0].shape[0]
+    found = [
+        (rows_of(ref[:, :128], source, expert, rows, tok_rows, capacity), ref)
         for ref, source in ((own_ref, core), (near_ref, 1 - core))
     ]
-    out_ref[...] = (parts[0] + parts[1]).astype(out_ref.dtype)
+    start = own_ref.shape[1] - sum(out.shape[1] for out in outs)
+    for out in outs:
+        stop = start + out.shape[1]
+        out[...] = sum(transposed_dot(sel, ref[:, start:stop]) for sel, ref in found).astype(out.dtype)
+        start = stop
 
 
 def weight_copies(weights, held, sems, start, step):
@@ -171,6 +174,19 @@
     gather_rows(x_ref, stay_ref[:, :cut], far.astype(x_ref.dtype))
     gate_ref[...] = partial_product(x_ref, gates, 0)
     up_ref[...] = partial_product(x_ref, ups, 0)
+    for copy in copies:
+        copy.wait()
+
+
+def middle_step(step, start, held, far_ref, stay_ref, gate_in, up_in, *refs):
+    gates, ups = refs[: 2 * held : 2], refs[1 : 2 * held : 2]
+    gate_hbm, up_hbm, gate_ref, up_ref, gate_rest, up_rest, x_ref, sems = refs[2 * held :]
+    copies = weight_copies((gate_hbm, up_hbm), (gate_rest, up_rest), sems, sum(ref.shape[0] for ref in gates), step)
+    for copy in copies:
+        copy.start()
+    gather_rows(x_ref, stay_ref[:, start : start + far_ref.shape[1]], far_ref[...])
+    gate_ref[...] = gate_in[...] + partial_product(x_ref, gates, start)
+    up_ref[...] = up_in[...] + partial_product(x_ref, ups, start)
     for copy in copies:
         copy.wait()
 
@@ -203,8 +219,9 @@
     experts = 4
     rows = peers * capacity
     half = rows // 2
-    cut = 11 * width // 24
-    helds = (7 * width // 12, width // 6)
+    cuts = (width // 4, 2 * width // 3)
+    cut = cuts[0]
+    helds = (width // 3, width // 6, width // 4)
     step = 256
     kind = tokens.dtype
 
@@ -224,8 +241,9 @@
     own = lax.all_gather(packed, "et", axis=0, tiled=True)
     part = local_kernel(cut_kernel, array(own.shape[0], 128 + cut), (own,))
     near, far = swap(own, 1), swap(part, 2)
-    later = local_kernel(functools.partial(select_kernel, tok_rows, capacity), array(half, width - cut), (own, near))
-    later_far = swap(later, 2)
+    kernel = functools.partial(select_kernel, tok_rows, capacity)
+    laters = local_kernel(kernel, [array(half, cuts[1] - cut), array(half, width - cuts[1])], (own, near))
+    middle_far, later_far = (swap(later, 2) for later in laters)
 
     def fetch(start, held, blocks, swapped, span):
         return local_kernel(
@@ -236,27 +254,36 @@
             scratch=[pltpu.SemaphoreType.DMA((2, held // step))],
         )
 
-    own, near, later = lax.optimization_barrier((own, near, later))
+    own, near, *laters = lax.optimization_barrier((own, near, *laters))
     stay, *pieces = fetch(0, helds[0], (own, near), (0, 1), width)
     far, *pieces = lax.optimization_barrier((far, *pieces))
     far_other = swap(far, 1)
     far_part, *more = fetch(helds[0], helds[1], (far,), (0,), cut)
     far_other, *more = lax.optimization_barrier((far_other, *more))
     pieces = (*pieces, *more)
+
+    def sums(kernel, rest, blocks, pieces, span):
+        return local_kernel(
+            functools.partial(kernel, len(pieces) // 2),
+            [jax.ShapeDtypeStruct((rows, units), jnp.float32)] * 2 + [pltpu.VMEM((rest, units), kind)] * 2,
+            (*blocks, *pieces),
+            (gate_local, up_local),
+            scratch=[pltpu.VMEM((rows, span), kind), pltpu.SemaphoreType.DMA((2, rest // step))],
+        )
+
+    kernel = functools.partial(first_kernel, step, tok_rows, capacity)
+    gate_sum, up_sum, *last = sums(kernel, helds[2], (far_other, far_part, stay), pieces, cut)
+    middle_far, *last = lax.optimization_barrier((middle_far, *last))
+    pieces = (*pieces, *last)
+    kernel = functools.partial(middle_step, step, cut)
     rest = width - sum(helds)
-    gate_sum, up_sum, *last = local_kernel(
-        functools.partial(first_kernel, step, tok_rows, capacity, len(helds)),
-        [jax.ShapeDtypeStruct((rows, units), jnp.float32)] * 2 + [pltpu.VMEM((rest, units), kind)] * 2,
-        (far_other, far_part, stay, *pieces),
-        (gate_local, up_local),
-        scratch=[pltpu.VMEM((rows, cut), kind), pltpu.SemaphoreType.DMA((2, rest // step))],
-    )
+    gate_sum, up_sum, *last = sums(kernel, rest, (middle_far, stay, gate_sum, up_sum), pieces, cuts[1] - cut)
     later_far, *last = lax.optimization_barrier((later_far, *last))
     return local_kernel(
         functools.partial(second_kernel, folds, experts),
         array(peers, capacity * folds, units // folds),
         (later_far, stay, gate_sum, up_sum, *pieces, *last),
-        scratch=[pltpu.VMEM((rows, width - cut), kind), pltpu.VMEM((rows, units), jnp.float32)],
+        scratch=[pltpu.VMEM((rows, width - cuts[1]), kind), pltpu.VMEM((rows, units), jnp.float32)],
     )
 
 

time: 66.1 us -> 67.3 us (1.018)
  Pallas kernels: 19.1 us -> 20 us
  starting transfers between devices: 8.56 us -> 9.25 us
    pallas_call x9 -> x10, Pallas kernels: 19.1 us -> 20 us  [local_kernel(): pl.pallas_call(kernel, out_shape=out_shape, in_specs=[WHOLE] * len(args)...]
    ppermute x4 -> x5, starting transfers between devices: 3.12 us -> 3.72 us  [swap(): return lax.ppermute(block, 'ep', [(i, i ^ bit) for i in range(experts)])]
  transfers between devices with their start and end apart: 5 -> 6, of which waited for: 4 -> 2; matrix products, arithmetic and copies ran while one was open for 0% -> 0% of each run, Pallas kernels for 19% -> 22%
where the time goes in v10:
time: 67.3 us; the launch traced here: 66.9 us
  Pallas kernels  20 us (30%)
  blocking collectives  18.8 us (28%)
  waiting for transfers between devices  18.7 us (28%)
  starting transfers between devices  9.25 us (14%)
    pallas_call x10, Pallas kernels, local_kernel(): pl.pallas_call(kernel, out_shape=out_shape, in_specs=[WHOLE] * len(args)...  20 us
    all_gather x1, blocking collectives, routed_by_columns(): own = lax.all_gather(packed, 'et', axis=0, tiled=True)  18.8 us
    all_to_all x1, waiting for transfers between devices, exchange(): lax.all_to_all(blocks, ('et', 'ep'), split_axis=0, concat_axis=0, tiled=T...  18.2 us
    all_to_all x1, starting transfers between devices, exchange(): lax.all_to_all(blocks, ('et', 'ep'), split_axis=0, concat_axis=0, tiled=T...  5.52 us
    ppermute x5, starting transfers between devices, swap(): return lax.ppermute(block, 'ep', [(i, i ^ bit) for i in range(experts)])  3.72 us
  transfers between devices with their start and end apart: 6, of which 2 were waited for; matrix products, arithmetic and copies ran while one was open for 0% of the time, Pallas kernels for 22%

profile of v10, /device:TPU:0, one launch (start us, length us, event | category | flops | bytes accessed | tf_op | source)
XLA Modules:
  0.0 66.9 jit_solution(6372409507869822448)
XLA Ops:
  0.0 0.9 %shard_map.56 = bf16[24,3200]{1,0:T(8,128)(2,1)S(1)} custom-call(s32[2,24]{1,0:T(2,128)} %bitcast.4, bf16[24,3072]{1,0:T(8,128)(2,1)} %tokens_hbm.1), custom_call_target="tpu_custom_call" | custom-call | tf_op jit(solution)/shard_map/pallas_call | solution.py:38
  1.0 18.8 %all_gather.3.own_ref.in_ref.refs_0_ = bf16[96,3200]{1,0:T(8,128)(2,1)S(1)} all-gather(bf16[24,3200]{1,0:T(8,128)(2,1)S(1)} %shard_map.56), channel_id=1, replica_groups=mesh['groups'=2,'et'=4,'ep'=4] {'et'}, dimensions={0}, use_global_device_ids=true | all-gather | bytes 768000 | tf_op jit(solution)/shard_map/all_gather | solution.py:241
  19.7 0.0 collective-permute-start
  19.7 1.6 %collective-permute-start.3 = (bf16[96,896]{1,0:T(8,128)(2,1)S(1)}, bf16[96,896]{1,0:T(8,128)(2,1)S(1)}, u32[]{:S(2)}, u32[]{:S(2)}) collective-permute-start(bf16[96,896]{1,0:T(8,128)(2,1)S(1)} %shard_map.58), channel_id=1, source_target_pairs={{0,2},{1,3},{2,0},{3,1},{4,6},{5,7},{6,4},{7,5},{8,10},{9,11},{10,... | collective-permute-start | bytes 516104 | tf_op jit(solution)/shard_map/ppermute | solution.py:232
  21.3 0.5 collective-permute-done.near_ref.refs_1_
  21.8 0.8 %shard_map.57 = (bf16[96,1280]{1,0:T(8,128)(2,1)S(1)}, bf16[96,1024]{1,0:T(8,128)(2,1)S(1)}) custom-call(bf16[96,3200]{1,0:T(8,128)(2,1)S(1)} %all_gather.3.own_ref.in_ref.refs_0_, bf16[96,3200]{1,0:T(8,128)(2,1)S(1)} %collective-permute-done.near_ref.refs_1_), custom_call_target="tpu_custom_call" | custom-call | tf_op jit(solution)/shard_map/pallas_call | solution.py:38
  22.5 1.6 %collective-permute-start.2 = (bf16[96,1280]{1,0:T(8,128)(2,1)S(1)}, bf16[96,1280]{1,0:T(8,128)(2,1)S(1)}, u32[]{:S(2)}, u32[]{:S(2)}) collective-permute-start(bf16[96,1280]{1,0:T(8,128)(2,1)S(1)} %get-tuple-element.40), channel_id=1, source_target_pairs={{0,2},{1,3},{2,0},{3,1},{4,6},{5,7},{6,4},{7,5},{8,10},{9,11},{10,... | collective-permute-start | bytes 737288 | tf_op jit(solution)/shard_map/ppermute | solution.py:232
  24.1 0.5 collective-permute-start.1
  24.6 3.6 %shard_map.59 = (bf16[96,3072]{1,0:T(8,128)(2,1)S(1)}, bf16[1024,2048]{1,0:T(8,128)(2,1)S(1)}, bf16[1024,2048]{1,0:T(8,128)(2,1)S(1)}) custom-call(bf16[96,3200]{1,0:T(8,128)(2,1)S(1)} %all_gather.3.own_ref.in_ref.refs_0_, bf16[96,3200]{1,0:T(8,128)(2,1)S(1)} %collective-permute-done.near_ref.refs_1_, bf16[3072,2048]{1,0:T(8,128)(2,1)} %bitcast.7, ...), custom_call_target="tpu_custom_call" | custom-call | tf_op jit(solution)/shard_map/pallas_call | solution.py:38
  28.3 0.0 collective-permute-done.3.refs_0_
  28.3 0.1 collective-permute-start.4
  28.4 2.2 %shard_map.60 = (bf16[96,768]{1,0:T(8,128)(2,1)S(1)}, bf16[512,2048]{1,0:T(8,128)(2,1)S(1)}, bf16[512,2048]{1,0:T(8,128)(2,1)S(1)}) custom-call(bf16[96,896]{1,0:T(8,128)(2,1)S(1)} %collective-permute-done.3.refs_0_, bf16[3072,2048]{1,0:T(8,128)(2,1)} %bitcast.8, bf16[3072,2048]{1,0:T(8,128)(2,1)} %bitcast.12), custom_call_target="tpu_custom_call" | custom-call | tf_op jit(solution)/shard_map/pallas_call | solution.py:38
  30.6 0.0 collective-permute-done.4.other_ref
  30.6 4.0 %shard_map.61 = (f32[192,2048]{1,0:T(8,128)S(1)}, f32[192,2048]{1,0:T(8,128)S(1)}, bf16[768,2048]{1,0:T(8,128)(2,1)S(1)}, bf16[768,2048]{1,0:T(8,128)(2,1)S(1)}) custom-call(bf16[96,896]{1,0:T(8,128)(2,1)S(1)} %collective-permute-done.4.other_ref, bf16[96,768]{1,0:T(8,128)(2,1)S(1)} %get-tuple-element.49.part_ref, ...), custom_call_target="tpu_custom_call" | custom-call | tf_op jit(solution)/shard_map/pallas_call | solution.py:38
  34.6 0.0 collective-permute-done.2.far_ref
  34.6 3.9 %shard_map.62 = (f32[192,2048]{1,0:T(8,128)S(1)}, f32[192,2048]{1,0:T(8,128)S(1)}, bf16[768,2048]{1,0:T(8,128)(2,1)S(1)}, bf16[768,2048]{1,0:T(8,128)(2,1)S(1)}) custom-call(bf16[96,1280]{1,0:T(8,128)(2,1)S(1)} %collective-permute-done.2.far_ref, bf16[96,3072]{1,0:T(8,128)(2,1)S(1)} %get-tuple-element.50.stay_ref, ...), custom_call_target="tpu_custom_call" | custom-call | tf_op jit(solution)/shard_map/pallas_call | solution.py:38
  38.5 0.0 collective-permute-done.1.far_ref
  38.5 0.0 copy-start
  38.5 0.0 copy-start.1
  38.5 2.9 %shard_map.63 = bf16[16,48,512]{2,1,0:T(8,128)(2,1)} custom-call(bf16[96,1024]{1,0:T(8,128)(2,1)S(1)} %collective-permute-done.1.far_ref, bf16[96,3072]{1,0:T(8,128)(2,1)S(1)} %get-tuple-element.50.stay_ref, f32[192,2048]{1,0:T(8,128)S(1)} %get-tuple-element.65.gate_in, f32[192,2048]{1,0:T(8,128)S(1)} %get-tuple-element.66.up_in, ...), custom_call_target="tpu_custom_call" | custom-call | tf_op jit(solution)/shard_map/pallas_call | solution.py:38
  41.4 5.5 %all-to-all-start = ((bf16[16,48,512]{2,1,0:T(8,128)(2,1)}), bf16[16,48,512]{2,1,0:T(8,128)(2,1)S(1)}, u32[]{:S(2)}, u32[]{:S(2)}) async-start(bf16[16,48,512]{2,1,0:T(8,128)(2,1)} %shard_map.63), calls=%async_computation | async-start | bytes 1572864 | tf_op jit(solution)/shard_map/all_to_all | solution.py:34
  46.9 0.0 copy-done
  46.9 0.0 copy-done.1
  46.9 0.4 shard_map.55
  47.4 18.2 %all-to-all-done.recv_ref = bf16[16,48,512]{2,1,0:T(8,128)(2,1)S(1)} async-done(((bf16[16,48,512]{2,1,0:T(8,128)(2,1)}), bf16[16,48,512]{2,1,0:T(8,128)(2,1)S(1)}, u32[]{:S(2)}, u32[]{:S(2)}) %all-to-all-start) | async-done | bytes 786464 | tf_op jit(solution)/shard_map/all_to_all | solution.py:34
  65.6 1.3 %shard_map.64 = bf16[24,2,8192]{2,1,0:T(2,128)(2,1)} custom-call(bf16[192,192]{1,0:T(8,128)(2,1)S(1)} %get-tuple-element.37.picks_ref, f32[48,128]{1,0:T(8,128)S(1)} %get-tuple-element.38.column_ref, bf16[16,48,512]{2,1,0:T(8,128)(2,1)S(1)} %all-to-all-done.recv_ref), custom_call_target="tpu_custom_call" | custom-call | bytes 1572864 | tf_op jit(solution)/shard_map/pallas_call | solution.py:38
  (1 shorter events, 0.0 us)
Async XLA Ops:
  19.7 2.0 %collective-permute-start = (bf16[96,3200]{1,0:T(8,128)(2,1)S(1)}, bf16[96,3200]{1,0:T(8,128)(2,1)S(1)}, u32[]{:S(2)}, u32[]{:S(2)}) collective-permute-start(bf16[96,3200]{1,0:T(8,128)(2,1)S(1)} %all_gather.3.own_ref.in_ref.refs_0_), channel_id=1, source_target_pairs={{0,1},{1,0},{2,3},{3,2},{4,5},{5,4},{6,7},{7,6},{8,9},{9,8},{10,11... | collective-permute-start | bytes 1843208 | tf_op jit(solution)/shard_map/ppermute | solution.py:232
  19.7 8.5 %collective-permute-start.3 = (bf16[96,896]{1,0:T(8,128)(2,1)S(1)}, bf16[96,896]{1,0:T(8,128)(2,1)S(1)}, u32[]{:S(2)}, u32[]{:S(2)}) collective-permute-start(bf16[96,896]{1,0:T(8,128)(2,1)S(1)} %shard_map.58), channel_id=1, source_target_pairs={{0,2},{1,3},{2,0},{3,1},{4,6},{5,7},{6,4},{7,5},{8,10},{9,11},{10,... | collective-permute-start | bytes 516104 | tf_op jit(solution)/shard_map/ppermute | solution.py:232
  22.5 12.1 %collective-permute-start.2 = (bf16[96,1280]{1,0:T(8,128)(2,1)S(1)}, bf16[96,1280]{1,0:T(8,128)(2,1)S(1)}, u32[]{:S(2)}, u32[]{:S(2)}) collective-permute-start(bf16[96,1280]{1,0:T(8,128)(2,1)S(1)} %get-tuple-element.40), channel_id=1, source_target_pairs={{0,2},{1,3},{2,0},{3,1},{4,6},{5,7},{6,4},{7,5},{8,10},{9,11},{10,... | collective-permute-start | bytes 737288 | tf_op jit(solution)/shard_map/ppermute | solution.py:232
  24.1 14.4 %collective-permute-start.1 = (bf16[96,1024]{1,0:T(8,128)(2,1)S(1)}, bf16[96,1024]{1,0:T(8,128)(2,1)S(1)}, u32[]{:S(2)}, u32[]{:S(2)}) collective-permute-start(bf16[96,1024]{1,0:T(8,128)(2,1)S(1)} %get-tuple-element.39), channel_id=1, source_target_pairs={{0,2},{1,3},{2,0},{3,1},{4,6},{5,7},{6,4},{7,5},{8,10},{9,11},{10,... | collective-permute-start | bytes 589832 | tf_op jit(solution)/shard_map/ppermute | solution.py:232
  28.3 2.3 %collective-permute-start.4 = (bf16[96,896]{1,0:T(8,128)(2,1)S(1)}, bf16[96,896]{1,0:T(8,128)(2,1)S(1)}, u32[]{:S(2)}, u32[]{:S(2)}) collective-permute-start(bf16[96,896]{1,0:T(8,128)(2,1)S(1)} %collective-permute-done.3.refs_0_), channel_id=1, source_target_pairs={{0,1},{1,0},{2,3},{3,2},{4,5},{5,4},{6,7},{7,6},{8,9},{9,8},{10,11... | collective-permute-start | bytes 516104 | tf_op jit(solution)/shard_map/ppermute | solution.py:232
  38.5 8.4 %copy-start = (s32[24,2]{0,1:T(2,128)S(1)}, s32[24,2]{0,1:T(2,128)}, u32[]{:S(2)}) copy-start(s32[24,2]{0,1:T(2,128)} %param.6) | copy-start | bytes 580
  38.5 8.4 %copy-start.1 = (f32[24,2]{0,1:T(2,128)S(1)}, f32[24,2]{0,1:T(2,128)}, u32[]{:S(2)}) copy-start(f32[24,2]{0,1:T(2,128)} %param.7) | copy-start | bytes 580
  41.4 24.2 %all-to-all-start = ((bf16[16,48,512]{2,1,0:T(8,128)(2,1)}), bf16[16,48,512]{2,1,0:T(8,128)(2,1)S(1)}, u32[]{:S(2)}, u32[]{:S(2)}) async-start(bf16[16,48,512]{2,1,0:T(8,128)(2,1)} %shard_map.63), calls=%async_computation | async-start | bytes 1572864 | tf_op jit(solution)/shard_map/all_to_all | solution.py:34

commit v11 on v9

--- a/solution.py
+++ b/solution.py
@@ -70,7 +70,7 @@
     return jnp.sum(jnp.where(eye, column, jnp.zeros_like(column)), axis=0, keepdims=True)
 
 
-def pack_kernel(ids_hbm, tokens_hbm, out_ref, ids_ref, sems):
+def pack_kernel(ids_hbm, tokens_hbm, _, __, out_ref, ids_ref, sems):
     named = pltpu.make_async_copy(ids_hbm, ids_ref, sems.at[0])
     named.start()
     copy = pltpu.make_async_copy(tokens_hbm, out_ref.at[:, 128:], sems.at[1])
@@ -116,29 +116,13 @@
     out_ref[...] = (parts[0] + parts[1]).astype(out_ref.dtype)
 
 
-def weight_copies(weights, held, sems, start, step):
-    return [
-        pltpu.make_async_copy(
-            ref.at[pl.ds(start + part * step, step), :], into.at[pl.ds(part * step, step), :], sems.at[which, part]
-        )
-        for part in range(held[0].shape[0] // step)
-        for which, (ref, into) in enumerate(zip(weights, held))
-    ]
-
-
-def fetch_kernel(start, step, tok_rows, capacity, swapped, *refs):
-    blocks = refs[: len(swapped)]
-    up_hbm, rows_ref, up_held, sems = refs[len(swapped) :]
-    copies = weight_copies((up_hbm,), (up_held,), sems, start, step)
-    for copy in copies:
-        copy.start()
+def pick_kernel(tok_rows, capacity, swapped, *refs):
+    blocks, rows_ref = refs[:-1], refs[-1]
     rows, width = rows_ref.shape
     expert, core = lax.axis_index("ep"), lax.axis_index("ep") % 2
     rows_ref[...] = sum(
         picked(ref, core ^ other, expert, rows, tok_rows, capacity, 0, width) for ref, other in zip(blocks, swapped)
     ).astype(rows_ref.dtype)
-    for copy in copies:
-        copy.wait()
 
 
 def gather_rows(x_ref, stay, far):
@@ -148,39 +132,20 @@
     x_ref[pl.ds(pl.multiple_of((1 - chip) * rows, rows), rows), :] = far
 
 
-def partial_product(x_ref, pieces, start):
-    total, base, stop = None, 0, start + x_ref.shape[1]
-    for piece in pieces:
-        low, high = max(base, start), min(base + piece.shape[0], stop)
-        if low < high:
-            product = exact_dot(x_ref[:, low - start : high - start], piece[low - base : high - base, :])
-            total = product if total is None else total + product
-        base = base + piece.shape[0]
-    return total
-
-
-def first_kernel(step, tok_rows, capacity, held, other_ref, part_ref, stay_ref, *refs):
-    gate_all, ups = refs[0], refs[1 : 1 + held]
-    up_hbm, gate_ref, up_ref, up_rest, x_ref, sems = refs[1 + held :]
-    copies = weight_copies((up_hbm,), (up_rest,), sems, sum(ref.shape[0] for ref in ups), step)
-    for copy in copies:
-        copy.start()
+def first_kernel(tok_rows, capacity, other_ref, part_ref, stay_ref, gate_all, up_all, gate_ref, up_ref, x_ref):
     rows, cut = part_ref.shape
     expert, core = lax.axis_index("ep"), lax.axis_index("ep") % 2
     far = picked(other_ref, 1 - core, expert, rows, tok_rows, capacity, 0, cut) + part_ref[...].astype(jnp.float32)
     gather_rows(x_ref, stay_ref[:, :cut], far.astype(x_ref.dtype))
-    gate_ref[...] = partial_product(x_ref, (gate_all.at[0],), 0)
-    up_ref[...] = partial_product(x_ref, ups, 0)
-    for copy in copies:
-        copy.wait()
-
-
-def second_kernel(folds, experts, far_ref, stay_ref, gate_in, up_in, *refs):
-    gate_all, ups, (out_ref, x_ref, hidden_ref) = refs[0], refs[1:-3], refs[-3:]
+    gate_ref[...] = exact_dot(x_ref[...], gate_all[0, :cut, :])
+    up_ref[...] = exact_dot(x_ref[...], up_all[0, :cut, :])
+
+
+def second_kernel(folds, experts, far_ref, stay_ref, gate_in, up_in, gate_all, up_all, out_ref, x_ref, hidden_ref):
     cut = stay_ref.shape[1] - far_ref.shape[1]
     gather_rows(x_ref, stay_ref[:, cut:], far_ref[...])
-    gate_val = gate_in[...] + partial_product(x_ref, (gate_all.at[0],), cut)
-    up_val = up_in[...] + partial_product(x_ref, ups, cut)
+    gate_val = gate_in[...] + exact_dot(x_ref[...], gate_all[0, cut:, :])
+    up_val = up_in[...] + exact_dot(x_ref[...], up_all[0, cut:, :])
     hidden_ref[...] = gate_val / (1.0 + jnp.exp(-gate_val)) * up_val
     store_blocks(folds, experts, hidden_ref, out_ref)
 
@@ -197,15 +162,13 @@
         out_ref[peer] = jnp.concatenate(pieces, axis=0).astype(out_ref.dtype)
 
 
-def routed_by_columns(tokens, expert_ids, gate_whole, up_local, peers, capacity, folds):
+def routed_by_columns(tokens, expert_ids, w_gate, w_up, peers, capacity, folds):
     tok_rows, width = tokens.shape
-    units = up_local.shape[1]
+    units = w_gate.shape[2]
     experts = 4
     rows = peers * capacity
     half = rows // 2
     cut = 11 * width // 24
-    helds = (2 * width // 3, width // 6)
-    step = 256
     kind = tokens.dtype
 
     def array(*shape):
@@ -218,7 +181,7 @@
         pack_kernel,
         array(tok_rows, 128 + width),
         (),
-        (expert_ids.T, tokens),
+        (expert_ids.T, tokens, w_gate, w_up),
         scratch=[pltpu.VMEM((2, tok_rows), jnp.int32), pltpu.SemaphoreType.DMA((2,))],
     )
     own = lax.all_gather(packed, "et", axis=0, tiled=True)
@@ -227,35 +190,27 @@
     later = local_kernel(functools.partial(select_kernel, tok_rows, capacity), array(half, width - cut), (own, near))
     later_far = swap(later, 2)
 
-    def fetch(start, held, blocks, swapped, span):
-        return local_kernel(
-            functools.partial(fetch_kernel, start, step, tok_rows, capacity, swapped),
-            [array(half, span), pltpu.VMEM((held, units), kind)],
-            blocks,
-            (up_local,),
-            scratch=[pltpu.SemaphoreType.DMA((1, held // step))],
-        )
+    def pick(blocks, swapped, span):
+        kernel = functools.partial(pick_kernel, tok_rows, capacity, swapped)
+        return local_kernel(kernel, array(half, span), blocks)
 
     own, near, later = lax.optimization_barrier((own, near, later))
-    stay, *pieces = fetch(0, helds[0], (own, near), (0, 1), width)
-    far, *pieces = lax.optimization_barrier((far, *pieces))
+    stay = pick((own, near), (0, 1), width)
+    far, stay = lax.optimization_barrier((far, stay))
     far_other = swap(far, 1)
-    far_part, *more = fetch(helds[0], helds[1], (far,), (0,), cut)
-    far_other, *more = lax.optimization_barrier((far_other, *more))
-    pieces = (*pieces, *more)
-    rest = width - sum(helds)
-    gate_sum, up_sum, *last = local_kernel(
-        functools.partial(first_kernel, step, tok_rows, capacity, len(helds)),
-        [jax.ShapeDtypeStruct((rows, units), jnp.float32)] * 2 + [pltpu.VMEM((rest, units), kind)],
-        (far_other, far_part, stay, gate_whole, *pieces),
-        (up_local,),
-        scratch=[pltpu.VMEM((rows, cut), kind), pltpu.SemaphoreType.DMA((1, rest // step))],
-    )
-    later_far, *last = lax.optimization_barrier((later_far, *last))
+    far_part = pick((far,), (0,), cut)
+    far_other, far_part = lax.optimization_barrier((far_other, far_part))
+    gate_sum, up_sum = local_kernel(
+        functools.partial(first_kernel, tok_rows, capacity),
+        [jax.ShapeDtypeStruct((rows, units), jnp.float32)] * 2,
+        (far_other, far_part, stay, w_gate, w_up),
+        scratch=[pltpu.VMEM((rows, cut), kind)],
+    )
+    later_far, gate_sum = lax.optimization_barrier((later_far, gate_sum))
     return local_kernel(
         functools.partial(second_kernel, folds, experts),
         array(peers, capacity * folds, units // folds),
-        (later_far, stay, gate_sum, up_sum, gate_whole, *pieces, *last),
+        (later_far, stay, gate_sum, up_sum, w_gate, w_up),
         scratch=[pltpu.VMEM((rows, width - cut), kind), pltpu.VMEM((rows, units), jnp.float32)],
     )
 
@@ -330,7 +285,7 @@
     up_local = w_up[0]
     if experts == 4 and tensor_size == 4:
         folds = 4
-        blocks = routed_by_columns(tokens, expert_ids, w_gate, up_local, peers, capacity, folds)
+        blocks = routed_by_columns(tokens, expert_ids, w_gate, w_up, peers, capacity, folds)
         return finish(expert_ids, gate_weights, exchange(blocks), experts, folds)
     slot_pairs = place_slots(expert_ids, experts, capacity)
     selector = build_select(slot_pairs, experts * capacity)

time: 66.1 us -> 66.3 us (level)
  waiting for transfers between devices: 20.3 us -> 26 us
  Pallas kernels: 16.9 us -> 12.5 us
  local copies, waits for them, and re-layouts: 1.18 us -> 0.02 us
    ppermute x4, waiting for transfers between devices: 2.06 us -> 7.72 us  [swap(): return lax.ppermute(block, 'ep', [(i, i ^ bit) for i in range(experts)])]
    pallas_call x9, Pallas kernels: 16.9 us -> 12.5 us  [local_kernel(): pl.pallas_call(kernel, out_shape=out_shape, in_specs=[WHOLE] * len(args)...]
    unnamed x10 -> x12, local copies, waits for them, and re-layouts: 1.18 us -> 0.02 us
  transfers between devices with their start and end apart: 5 -> 5, of which waited for: 4 -> 5; matrix products, arithmetic and copies ran while one was open for 0% -> 0% of each run, Pallas kernels for 16% -> 9%
where the time goes in v11:
time: 66.3 us; the launch traced here: 66 us
  waiting for transfers between devices  26 us (39%)
  blocking collectives  18.9 us (29%)
  Pallas kernels  12.5 us (19%)
  starting transfers between devices  8.55 us (13%)
    all_gather x1, blocking collectives, routed_by_columns(): own = lax.all_gather(packed, 'et', axis=0, tiled=True)  18.9 us
    all_to_all x1, waiting for transfers between devices, exchange(): lax.all_to_all(blocks, ('et', 'ep'), split_axis=0, concat_axis=0, tiled=T...  18.2 us
    pallas_call x9, Pallas kernels, local_kernel(): pl.pallas_call(kernel, out_shape=out_shape, in_specs=[WHOLE] * len(args)...  12.5 us
    ppermute x4, waiting for transfers between devices, swap(): return lax.ppermute(block, 'ep', [(i, i ^ bit) for i in range(experts)])  7.72 us
    all_to_all x1, starting transfers between devices, exchange(): lax.all_to_all(blocks, ('et', 'ep'), split_axis=0, concat_axis=0, tiled=T...  5.44 us
    ppermute x4, starting transfers between devices, swap(): return lax.ppermute(block, 'ep', [(i, i ^ bit) for i in range(experts)])  3.11 us
  transfers between devices with their start and end apart: 5, of which 5 were waited for; matrix products, arithmetic and copies ran while one was open for 0% of the time, Pallas kernels for 9%

profile of v11, /device:TPU:0, one launch (start us, length us, event | category | flops | bytes accessed | tf_op | source)
XLA Modules:
  0.0 66.0 jit_solution(13609745634312774330)
XLA Ops:
  0.0 0.0 slice-start
  0.0 0.0 slice-start.1
  0.0 0.0 slice-start.2
  0.0 0.0 copy-start
  0.0 1.1 %shard_map.56 = bf16[24,3200]{1,0:T(8,128)(2,1)S(1)} custom-call(s32[2,24]{1,0:T(2,128)} %bitcast.4, bf16[24,3072]{1,0:T(8,128)(2,1)} %tokens_hbm.1, bf16[1,3072,2048]{2,1,0:T(8,128)(2,1)} %gate_all.3, bf16[1,3072,2048]{2,1,0:T(8,128)(2,1)} %up_all.3), custom_call_target="tpu_custom_call" | custom-call | tf_op jit(solution)/shard_map/pallas_call | solution.py:38
  1.1 18.9 %all_gather.3.own_ref.in_ref.refs_0_ = bf16[96,3200]{1,0:T(8,128)(2,1)S(1)} all-gather(bf16[24,3200]{1,0:T(8,128)(2,1)S(1)} %shard_map.56), channel_id=1, replica_groups=mesh['groups'=2,'et'=4,'ep'=4] {'et'}, dimensions={0}, use_global_device_ids=true | all-gather | bytes 768000 | tf_op jit(solution)/shard_map/all_gather | solution.py:187
  20.0 0.0 collective-permute-start
  20.1 1.6 %collective-permute-start.2 = (bf16[96,1536]{1,0:T(8,128)(2,1)S(1)}, bf16[96,1536]{1,0:T(8,128)(2,1)S(1)}, u32[]{:S(2)}, u32[]{:S(2)}) collective-permute-start(bf16[96,1536]{1,0:T(8,128)(2,1)S(1)} %shard_map.58), channel_id=1, source_target_pairs={{0,2},{1,3},{2,0},{3,1},{4,6},{5,7},{6,4},{7,5},{8,10},{9,11},{10,... | collective-permute-start | bytes 884744 | tf_op jit(solution)/shard_map/ppermute | solution.py:178
  21.6 0.5 collective-permute-done.near_ref.refs_1_
  22.1 0.7 %shard_map.57 = bf16[96,1664]{1,0:T(8,128)(2,1)S(1)} custom-call(bf16[96,3200]{1,0:T(8,128)(2,1)S(1)} %all_gather.3.own_ref.in_ref.refs_0_, bf16[96,3200]{1,0:T(8,128)(2,1)S(1)} %collective-permute-done.near_ref.refs_1_), custom_call_target="tpu_custom_call" | custom-call | tf_op jit(solution)/shard_map/pallas_call | solution.py:38
  22.8 1.6 %collective-permute-start.1 = (bf16[96,1664]{1,0:T(8,128)(2,1)S(1)}, bf16[96,1664]{1,0:T(8,128)(2,1)S(1)}, u32[]{:S(2)}, u32[]{:S(2)}) collective-permute-start(bf16[96,1664]{1,0:T(8,128)(2,1)S(1)} %shard_map.57), channel_id=1, source_target_pairs={{0,2},{1,3},{2,0},{3,1},{4,6},{5,7},{6,4},{7,5},{8,10},{9,11},{10,... | collective-permute-start | bytes 958472 | tf_op jit(solution)/shard_map/ppermute | solution.py:178
  24.4 0.9 %shard_map.59.stay_ref = bf16[96,3072]{1,0:T(8,128)(2,1)S(1)} custom-call(bf16[96,3200]{1,0:T(8,128)(2,1)S(1)} %all_gather.3.own_ref.in_ref.refs_0_, bf16[96,3200]{1,0:T(8,128)(2,1)S(1)} %collective-permute-done.near_ref.refs_1_), custom_call_target="tpu_custom_call" | custom-call | tf_op jit(solution)/shard_map/pallas_call | solution.py:38
  25.2 4.7 %collective-permute-done.2.refs_0_ = bf16[96,1536]{1,0:T(8,128)(2,1)S(1)} collective-permute-done((bf16[96,1536]{1,0:T(8,128)(2,1)S(1)}, bf16[96,1536]{1,0:T(8,128)(2,1)S(1)}, u32[]{:S(2)}, u32[]{:S(2)}) %collective-permute-start.2) | collective-permute-done | bytes 294944 | tf_op jit(solution)/shard_map/ppermute | solution.py:178
  29.9 0.0 collective-permute-start.3
  29.9 0.6 shard_map.60.part_ref
  30.5 1.0 %collective-permute-done.3.other_ref = bf16[96,1536]{1,0:T(8,128)(2,1)S(1)} collective-permute-done((bf16[96,1536]{1,0:T(8,128)(2,1)S(1)}, bf16[96,1536]{1,0:T(8,128)(2,1)S(1)}, u32[]{:S(2)}, u32[]{:S(2)}) %collective-permute-start.3) | collective-permute-done | bytes 294944 | tf_op jit(solution)/shard_map/ppermute | solution.py:178
  31.5 0.0 slice-done
  31.5 0.0 slice-done.1
  31.5 0.0 slice-done.2
  31.5 0.0 copy-done
  31.5 3.2 %shard_map.61 = (f32[192,2048]{1,0:T(8,128)S(1)}, f32[192,2048]{1,0:T(8,128)S(1)}) custom-call(bf16[96,1536]{1,0:T(8,128)(2,1)S(1)} %collective-permute-done.3.other_ref, bf16[96,1408]{1,0:T(8,128)(2,1)S(1)} %shard_map.60.part_ref, bf16[96,3072]{1,0:T(8,128)(2,1)S(1)} %shard_map.59.stay_ref, bf16[1,3072,2048]{2,1,0:T(8,128)(2,1)S(1)} %bitcast.3, ...), custom_call_target="tpu_custom_call" | custom-call | tf_op jit(solution)/shard_map/pallas_call | solution.py:38
  34.8 1.6 %collective-permute-done.1.far_ref = bf16[96,1664]{1,0:T(8,128)(2,1)S(1)} collective-permute-done((bf16[96,1664]{1,0:T(8,128)(2,1)S(1)}, bf16[96,1664]{1,0:T(8,128)(2,1)S(1)}, u32[]{:S(2)}, u32[]{:S(2)}) %collective-permute-start.1) | collective-permute-done | bytes 319520 | tf_op jit(solution)/shard_map/ppermute | solution.py:178
  36.4 0.0 copy-start.1
  36.4 0.0 copy-start.2
  36.4 4.2 %shard_map.62 = bf16[16,48,512]{2,1,0:T(8,128)(2,1)} custom-call(bf16[96,1664]{1,0:T(8,128)(2,1)S(1)} %collective-permute-done.1.far_ref, bf16[96,3072]{1,0:T(8,128)(2,1)S(1)} %shard_map.59.stay_ref, f32[192,2048]{1,0:T(8,128)S(1)} %get-tuple-element.27.gate_in, f32[192,2048]{1,0:T(8,128)S(1)} %get-tuple-element.28.up_in, ...), custom_call_target="tpu_custom_call" | custom-call | tf_op jit(solution)/shard_map/pallas_call | solution.py:38
  40.6 5.4 %all-to-all-start = ((bf16[16,48,512]{2,1,0:T(8,128)(2,1)}), bf16[16,48,512]{2,1,0:T(8,128)(2,1)S(1)}, u32[]{:S(2)}, u32[]{:S(2)}) async-start(bf16[16,48,512]{2,1,0:T(8,128)(2,1)} %shard_map.62), calls=%async_computation | async-start | bytes 1572864 | tf_op jit(solution)/shard_map/all_to_all | solution.py:34
  46.1 0.0 copy-done.1
  46.1 0.0 copy-done.2
  46.1 0.4 shard_map.55
  46.5 18.2 %all-to-all-done.recv_ref = bf16[16,48,512]{2,1,0:T(8,128)(2,1)S(1)} async-done(((bf16[16,48,512]{2,1,0:T(8,128)(2,1)}), bf16[16,48,512]{2,1,0:T(8,128)(2,1)S(1)}, u32[]{:S(2)}, u32[]{:S(2)}) %all-to-all-start) | async-done | bytes 786464 | tf_op jit(solution)/shard_map/all_to_all | solution.py:34
  64.8 1.3 %shard_map.63 = bf16[24,2,8192]{2,1,0:T(2,128)(2,1)} custom-call(bf16[192,192]{1,0:T(8,128)(2,1)S(1)} %get-tuple-element.17.picks_ref, f32[48,128]{1,0:T(8,128)S(1)} %get-tuple-element.18.column_ref, bf16[16,48,512]{2,1,0:T(8,128)(2,1)S(1)} %all-to-all-done.recv_ref), custom_call_target="tpu_custom_call" | custom-call | bytes 1572864 | tf_op jit(solution)/shard_map/pallas_call | solution.py:38
  (2 shorter events, 0.0 us)
Async XLA Ops:
  0.0 31.5 %slice-start = ((s8[12582912]{0:T(1024)(128)(4,1)}), s8[4194304]{0:T(1024)(128)(4,1)S(1)}, s32[]{:S(2)}) async-start(s8[12582912]{0:T(1024)(128)(4,1)} %bitcast.2), calls=%async_computation.1 | async-start | bytes 8388608
  0.0 31.5 %slice-start.1 = ((s8[12582912]{0:T(1024)(128)(4,1)}), s8[4194304]{0:T(1024)(128)(4,1)S(1)}, s32[]{:S(2)}) async-start(s8[12582912]{0:T(1024)(128)(4,1)} %bitcast.2), calls=%async_computation.2 | async-start | bytes 8388608
  0.0 31.5 %slice-start.2 = ((s8[12582912]{0:T(1024)(128)(4,1)}), s8[4194304]{0:T(1024)(128)(4,1)S(1)}, s32[]{:S(2)}) async-start(s8[12582912]{0:T(1024)(128)(4,1)} %bitcast.2), calls=%async_computation.3 | async-start | bytes 8388608
  0.0 31.5 %copy-start = (bf16[1,3072,2048]{2,1,0:T(8,128)(2,1)S(1)}, bf16[1,3072,2048]{2,1,0:T(8,128)(2,1)}, u32[]{:S(2)}) copy-start(bf16[1,3072,2048]{2,1,0:T(8,128)(2,1)} %up_all.3) | copy-start | bytes 37748740
  20.0 2.0 %collective-permute-start = (bf16[96,3200]{1,0:T(8,128)(2,1)S(1)}, bf16[96,3200]{1,0:T(8,128)(2,1)S(1)}, u32[]{:S(2)}, u32[]{:S(2)}) collective-permute-start(bf16[96,3200]{1,0:T(8,128)(2,1)S(1)} %all_gather.3.own_ref.in_ref.refs_0_), channel_id=1, source_target_pairs={{0,1},{1,0},{2,3},{3,2},{4,5},{5,4},{6,7},{7,6},{8,9},{9,8},{10,11... | collective-permute-start | bytes 1843208 | tf_op jit(solution)/shard_map/ppermute | solution.py:178
  20.1 9.9 %collective-permute-start.2 = (bf16[96,1536]{1,0:T(8,128)(2,1)S(1)}, bf16[96,1536]{1,0:T(8,128)(2,1)S(1)}, u32[]{:S(2)}, u32[]{:S(2)}) collective-permute-start(bf16[96,1536]{1,0:T(8,128)(2,1)S(1)} %shard_map.58), channel_id=1, source_target_pairs={{0,2},{1,3},{2,0},{3,1},{4,6},{5,7},{6,4},{7,5},{8,10},{9,11},{10,... | collective-permute-start | bytes 884744 | tf_op jit(solution)/shard_map/ppermute | solution.py:178
  22.8 13.6 %collective-permute-start.1 = (bf16[96,1664]{1,0:T(8,128)(2,1)S(1)}, bf16[96,1664]{1,0:T(8,128)(2,1)S(1)}, u32[]{:S(2)}, u32[]{:S(2)}) collective-permute-start(bf16[96,1664]{1,0:T(8,128)(2,1)S(1)} %shard_map.57), channel_id=1, source_target_pairs={{0,2},{1,3},{2,0},{3,1},{4,6},{5,7},{6,4},{7,5},{8,10},{9,11},{10,... | collective-permute-start | bytes 958472 | tf_op jit(solution)/shard_map/ppermute | solution.py:178
  29.9 1.6 %collective-permute-start.3 = (bf16[96,1536]{1,0:T(8,128)(2,1)S(1)}, bf16[96,1536]{1,0:T(8,128)(2,1)S(1)}, u32[]{:S(2)}, u32[]{:S(2)}) collective-permute-start(bf16[96,1536]{1,0:T(8,128)(2,1)S(1)} %collective-permute-done.2.refs_0_), channel_id=1, source_target_pairs={{0,1},{1,0},{2,3},{3,2},{4,5},{5,4},{6,7},{7,6},{8,9},{9,8},{10,11... | collective-permute-start | bytes 884744 | tf_op jit(solution)/shard_map/ppermute | solution.py:178
  36.4 9.7 %copy-start.1 = (s32[24,2]{0,1:T(2,128)S(1)}, s32[24,2]{0,1:T(2,128)}, u32[]{:S(2)}) copy-start(s32[24,2]{0,1:T(2,128)} %param.6) | copy-start | bytes 580
  36.4 9.7 %copy-start.2 = (f32[24,2]{0,1:T(2,128)S(1)}, f32[24,2]{0,1:T(2,128)}, u32[]{:S(2)}) copy-start(f32[24,2]{0,1:T(2,128)} %param.7) | copy-start | bytes 580
  40.6 24.2 %all-to-all-start = ((bf16[16,48,512]{2,1,0:T(8,128)(2,1)}), bf16[16,48,512]{2,1,0:T(8,128)(2,1)S(1)}, u32[]{:S(2)}, u32[]{:S(2)}) async-start(bf16[16,48,512]{2,1,0:T(8,128)(2,1)} %shard_map.62), calls=%async_computation | async-start | bytes 1572864 | tf_op jit(solution)/shard_map/all_to_all | solution.py:34

commit v12 on v11

--- a/solution.py
+++ b/solution.py
@@ -105,15 +105,18 @@
     out_ref[...] = in_ref[:, : out_ref.shape[1]]
 
 
-def select_kernel(tok_rows, capacity, own_ref, near_ref, out_ref):
+def select_kernel(tok_rows, capacity, own_ref, near_ref, *outs):
     expert, core = lax.axis_index("ep") ^ 2, lax.axis_index("ep") % 2
-    rows, span = out_ref.shape
-    stop = own_ref.shape[1] - 128
-    parts = [
-        picked(ref, source, expert, rows, tok_rows, capacity, stop - span, stop)
+    rows = outs[0].shape[0]
+    found = [
+        (rows_of(ref[:, :128], source, expert, rows, tok_rows, capacity), ref)
         for ref, source in ((own_ref, core), (near_ref, 1 - core))
     ]
-    out_ref[...] = (parts[0] + parts[1]).astype(out_ref.dtype)
+    start = own_ref.shape[1] - sum(out.shape[1] for out in outs)
+    for out in outs:
+        stop = start + out.shape[1]
+        out[...] = sum(transposed_dot(sel, ref[:, start:stop]) for sel, ref in found).astype(out.dtype)
+        start = stop
 
 
 def pick_kernel(tok_rows, capacity, swapped, *refs):
@@ -139,6 +142,13 @@
     gather_rows(x_ref, stay_ref[:, :cut], far.astype(x_ref.dtype))
     gate_ref[...] = exact_dot(x_ref[...], gate_all[0, :cut, :])
     up_ref[...] = exact_dot(x_ref[...], up_all[0, :cut, :])
+
+
+def middle_kernel(start, far_ref, stay_ref, gate_in, up_in, gate_all, up_all, gate_ref, up_ref, x_ref):
+    stop = start + far_ref.shape[1]
+    gather_rows(x_ref, stay_ref[:, start:stop], far_ref[...])
+    gate_ref[...] = gate_in[...] + exact_dot(x_ref[...], gate_all[0, start:stop, :])
+    up_ref[...] = up_in[...] + exact_dot(x_ref[...], up_all[0, start:stop, :])
 
 
 def second_kernel(folds, experts, far_ref, stay_ref, gate_in, up_in, gate_all, up_all, out_ref, x_ref, hidden_ref):
@@ -168,7 +178,8 @@
     experts = 4
     rows = peers * capacity
     half = rows // 2
-    cut = 11 * width // 24
+    cuts = (width // 6, 11 * width // 24, 3 * width // 4)
+    cut = cuts[0]
     kind = tokens.dtype
 
     def array(*shape):
@@ -187,31 +198,39 @@
     own = lax.all_gather(packed, "et", axis=0, tiled=True)
     part = local_kernel(cut_kernel, array(own.shape[0], 128 + cut), (own,))
     near, far = swap(own, 1), swap(part, 2)
-    later = local_kernel(functools.partial(select_kernel, tok_rows, capacity), array(half, width - cut), (own, near))
-    later_far = swap(later, 2)
+    kernel = functools.partial(select_kernel, tok_rows, capacity)
+    ends = (*cuts[1:], width)
+    laters = local_kernel(kernel, [array(half, stop - start) for start, stop in zip(cuts, ends)], (own, near))
+    later_fars = [swap(later, 2) for later in laters]
 
     def pick(blocks, swapped, span):
         kernel = functools.partial(pick_kernel, tok_rows, capacity, swapped)
         return local_kernel(kernel, array(half, span), blocks)
 
-    own, near, later = lax.optimization_barrier((own, near, later))
+    own, near, *laters = lax.optimization_barrier((own, near, *laters))
     stay = pick((own, near), (0, 1), width)
     far, stay = lax.optimization_barrier((far, stay))
     far_other = swap(far, 1)
     far_part = pick((far,), (0,), cut)
     far_other, far_part = lax.optimization_barrier((far_other, far_part))
-    gate_sum, up_sum = local_kernel(
-        functools.partial(first_kernel, tok_rows, capacity),
-        [jax.ShapeDtypeStruct((rows, units), jnp.float32)] * 2,
-        (far_other, far_part, stay, w_gate, w_up),
-        scratch=[pltpu.VMEM((rows, cut), kind)],
-    )
-    later_far, gate_sum = lax.optimization_barrier((later_far, gate_sum))
+
+    def sums(kernel, blocks, span):
+        out_shape = [jax.ShapeDtypeStruct((rows, units), jnp.float32)] * 2
+        return local_kernel(kernel, out_shape, (*blocks, w_gate, w_up), scratch=[pltpu.VMEM((rows, span), kind)])
+
+    gate_sum, up_sum = sums(
+        functools.partial(first_kernel, tok_rows, capacity), (far_other, far_part, stay), cut
+    )
+    for start, later_far in zip(cuts[:-1], later_fars):
+        later_far, gate_sum = lax.optimization_barrier((later_far, gate_sum))
+        kernel = functools.partial(middle_kernel, start)
+        gate_sum, up_sum = sums(kernel, (later_far, stay, gate_sum, up_sum), later_far.shape[1])
+    later_far, gate_sum = lax.optimization_barrier((later_fars[-1], gate_sum))
     return local_kernel(
         functools.partial(second_kernel, folds, experts),
         array(peers, capacity * folds, units // folds),
         (later_far, stay, gate_sum, up_sum, w_gate, w_up),
-        scratch=[pltpu.VMEM((rows, width - cut), kind), pltpu.VMEM((rows, units), jnp.float32)],
+        scratch=[pltpu.VMEM((rows, width - cuts[-1]), kind), pltpu.VMEM((rows, units), jnp.float32)],
     )
 
 

time: 66.3 us -> 64.8 us (0.977)
  waiting for transfers between devices: 26 us -> 21.7 us
  starting transfers between devices: 8.55 us -> 10.8 us
    ppermute x4 -> x6, waiting for transfers between devices: 7.72 us -> 3.5 us  [swap(): return lax.ppermute(block, 'ep', [(i, i ^ bit) for i in range(experts)])]
    ppermute x4 -> x6, starting transfers between devices: 3.11 us -> 5.24 us  [swap(): return lax.ppermute(block, 'ep', [(i, i ^ bit) for i in range(experts)])]
    pallas_call x9 -> x11, Pallas kernels: 12.5 us -> 12.9 us  [local_kernel(): pl.pallas_call(kernel, out_shape=out_shape, in_specs=[WHOLE] * len(args)...]
  transfers between devices with their start and end apart: 5 -> 7, of which waited for: 5 -> 5; matrix products, arithmetic and copies ran while one was open for 0% -> 0% of each run, Pallas kernels for 9% -> 12%
where the time goes in v12:
time: 64.8 us; the launch traced here: 64.5 us
  waiting for transfers between devices  21.7 us (33%)
  blocking collectives  18.9 us (29%)
  Pallas kernels  12.9 us (20%)
  starting transfers between devices  10.8 us (17%)
    all_gather x1, blocking collectives, routed_by_columns(): own = lax.all_gather(packed, 'et', axis=0, tiled=True)  18.9 us
    all_to_all x1, waiting for transfers between devices, exchange(): lax.all_to_all(blocks, ('et', 'ep'), split_axis=0, concat_axis=0, tiled=T...  18.2 us
    pallas_call x11, Pallas kernels, local_kernel(): pl.pallas_call(kernel, out_shape=out_shape, in_specs=[WHOLE] * len(args)...  12.9 us
    all_to_all x1, starting transfers between devices, exchange(): lax.all_to_all(blocks, ('et', 'ep'), split_axis=0, concat_axis=0, tiled=T...  5.58 us
    ppermute x6, starting transfers between devices, swap(): return lax.ppermute(block, 'ep', [(i, i ^ bit) for i in range(experts)])  5.24 us
    ppermute x6, waiting for transfers between devices, swap(): return lax.ppermute(block, 'ep', [(i, i ^ bit) for i in range(experts)])  3.5 us
  transfers between devices with their start and end apart: 7, of which 5 were waited for; matrix products, arithmetic and copies ran while one was open for 0% of the time, Pallas kernels for 12%

profile of v12, /device:TPU:0, one launch (start us, length us, event | category | flops | bytes accessed | tf_op | source)
XLA Modules:
  0.0 64.5 jit_solution(6703553568923837166)
XLA Ops:
  0.0 0.0 slice-start
  0.0 1.1 %shard_map.56 = bf16[24,3200]{1,0:T(8,128)(2,1)S(1)} custom-call(s32[2,24]{1,0:T(2,128)} %bitcast.4, bf16[24,3072]{1,0:T(8,128)(2,1)} %tokens_hbm.1, bf16[1,3072,2048]{2,1,0:T(8,128)(2,1)} %gate_all.7, bf16[1,3072,2048]{2,1,0:T(8,128)(2,1)} %up_all.7), custom_call_target="tpu_custom_call" | custom-call | tf_op jit(solution)/shard_map/pallas_call | solution.py:38
  1.1 18.9 %all_gather.3.own_ref.in_ref.refs_0_ = bf16[96,3200]{1,0:T(8,128)(2,1)S(1)} all-gather(bf16[24,3200]{1,0:T(8,128)(2,1)S(1)} %shard_map.56), channel_id=1, replica_groups=mesh['groups'=2,'et'=4,'ep'=4] {'et'}, dimensions={0}, use_global_device_ids=true | all-gather | bytes 768000 | tf_op jit(solution)/shard_map/all_gather | solution.py:198
  20.0 0.0 collective-permute-start
  20.0 1.6 %collective-permute-start.4 = (bf16[96,640]{1,0:T(8,128)(2,1)S(1)}, bf16[96,640]{1,0:T(8,128)(2,1)S(1)}, u32[]{:S(2)}, u32[]{:S(2)}) collective-permute-start(bf16[96,640]{1,0:T(8,128)(2,1)S(1)} %shard_map.58), channel_id=1, source_target_pairs={{0,2},{1,3},{2,0},{3,1},{4,6},{5,7},{6,4},{7,5},{8,10},{9,11},{10,... | collective-permute-start | bytes 368648 | tf_op jit(solution)/shard_map/ppermute | solution.py:189
  21.6 0.5 collective-permute-done.near_ref.refs_1_
  22.1 0.8 %shard_map.57 = (bf16[96,896]{1,0:T(8,128)(2,1)S(1)}, bf16[96,896]{1,0:T(8,128)(2,1)S(1)}, bf16[96,768]{1,0:T(8,128)(2,1)S(1)}) custom-call(bf16[96,3200]{1,0:T(8,128)(2,1)S(1)} %all_gather.3.own_ref.in_ref.refs_0_, bf16[96,3200]{1,0:T(8,128)(2,1)S(1)} %collective-permute-done.near_ref.refs_1_), custom_call_target="tpu_custom_call" | custom-call | tf_op jit(solution)/shard_map/pallas_call | solution.py:38
  22.9 1.6 %collective-permute-start.3 = (bf16[96,896]{1,0:T(8,128)(2,1)S(1)}, bf16[96,896]{1,0:T(8,128)(2,1)S(1)}, u32[]{:S(2)}, u32[]{:S(2)}) collective-permute-start(bf16[96,896]{1,0:T(8,128)(2,1)S(1)} %get-tuple-element.32), channel_id=1, source_target_pairs={{0,2},{1,3},{2,0},{3,1},{4,6},{5,7},{6,4},{7,5},{8,10},{9,11},{10,... | collective-permute-start | bytes 516104 | tf_op jit(solution)/shard_map/ppermute | solution.py:189
  24.5 0.5 collective-permute-start.2
  25.0 1.5 %collective-permute-start.1 = (bf16[96,768]{1,0:T(8,128)(2,1)S(1)}, bf16[96,768]{1,0:T(8,128)(2,1)S(1)}, u32[]{:S(2)}, u32[]{:S(2)}) collective-permute-start(bf16[96,768]{1,0:T(8,128)(2,1)S(1)} %get-tuple-element.30), channel_id=1, source_target_pairs={{0,2},{1,3},{2,0},{3,1},{4,6},{5,7},{6,4},{7,5},{8,10},{9,11},{10,... | collective-permute-start | bytes 442376 | tf_op jit(solution)/shard_map/ppermute | solution.py:189
  26.5 0.8 %shard_map.59.stay_ref = bf16[96,3072]{1,0:T(8,128)(2,1)S(1)} custom-call(bf16[96,3200]{1,0:T(8,128)(2,1)S(1)} %all_gather.3.own_ref.in_ref.refs_0_, bf16[96,3200]{1,0:T(8,128)(2,1)S(1)} %collective-permute-done.near_ref.refs_1_), custom_call_target="tpu_custom_call" | custom-call | tf_op jit(solution)/shard_map/pallas_call | solution.py:38
  27.3 0.0 collective-permute-done.4.refs_0_
  27.3 0.1 collective-permute-start.5
  27.4 0.6 shard_map.60.part_ref
  28.0 0.8 %collective-permute-done.5.other_ref = bf16[96,640]{1,0:T(8,128)(2,1)S(1)} collective-permute-done((bf16[96,640]{1,0:T(8,128)(2,1)S(1)}, bf16[96,640]{1,0:T(8,128)(2,1)S(1)}, u32[]{:S(2)}, u32[]{:S(2)}) %collective-permute-start.5) | collective-permute-done | bytes 122912 | tf_op jit(solution)/shard_map/ppermute | solution.py:189
  28.8 0.0 slice-done
  28.8 0.0 slice-done.1
  28.8 0.0 slice-done.2
  28.8 0.0 copy-done
  28.8 1.5 %shard_map.61 = (f32[192,2048]{1,0:T(8,128)S(1)}, f32[192,2048]{1,0:T(8,128)S(1)}) custom-call(bf16[96,640]{1,0:T(8,128)(2,1)S(1)} %collective-permute-done.5.other_ref, bf16[96,512]{1,0:T(8,128)(2,1)S(1)} %shard_map.60.part_ref, bf16[96,3072]{1,0:T(8,128)(2,1)S(1)} %shard_map.59.stay_ref, bf16[1,3072,2048]{2,1,0:T(8,128)(2,1)S(1)} %bitcast.3, ...), custom_call_target="tpu_custom_call" | custom-call | tf_op jit(solution)/shard_map/pallas_call | solution.py:38
  30.3 0.0 collective-permute-done.3.far_ref
  30.3 1.9 %shard_map.62 = (f32[192,2048]{1,0:T(8,128)S(1)}, f32[192,2048]{1,0:T(8,128)S(1)}) custom-call(bf16[96,896]{1,0:T(8,128)(2,1)S(1)} %collective-permute-done.3.far_ref, bf16[96,3072]{1,0:T(8,128)(2,1)S(1)} %shard_map.59.stay_ref, f32[192,2048]{1,0:T(8,128)S(1)} %get-tuple-element.41.gate_in, f32[192,2048]{1,0:T(8,128)S(1)} %get-tuple-element.42.up_in, ...), custom_call_target="tpu_custom_call" | custom-call | tf_op jit(solution)/shard_map/pallas_call | solution.py:38
  32.2 1.6 %collective-permute-done.2.far_ref = bf16[96,896]{1,0:T(8,128)(2,1)S(1)} collective-permute-done((bf16[96,896]{1,0:T(8,128)(2,1)S(1)}, bf16[96,896]{1,0:T(8,128)(2,1)S(1)}, u32[]{:S(2)}, u32[]{:S(2)}) %collective-permute-start.2) | collective-permute-done | bytes 172064 | tf_op jit(solution)/shard_map/ppermute | solution.py:189
  33.8 1.9 %shard_map.63 = (f32[192,2048]{1,0:T(8,128)S(1)}, f32[192,2048]{1,0:T(8,128)S(1)}) custom-call(bf16[96,896]{1,0:T(8,128)(2,1)S(1)} %collective-permute-done.2.far_ref, bf16[96,3072]{1,0:T(8,128)(2,1)S(1)} %shard_map.59.stay_ref, f32[192,2048]{1,0:T(8,128)S(1)} %get-tuple-element.45.gate_in, f32[192,2048]{1,0:T(8,128)S(1)} %get-tuple-element.46.up_in, ...), custom_call_target="tpu_custom_call" | custom-call | tf_op jit(solution)/shard_map/pallas_call | solution.py:38
  35.7 0.7 %collective-permute-done.1.far_ref = bf16[96,768]{1,0:T(8,128)(2,1)S(1)} collective-permute-done((bf16[96,768]{1,0:T(8,128)(2,1)S(1)}, bf16[96,768]{1,0:T(8,128)(2,1)S(1)}, u32[]{:S(2)}, u32[]{:S(2)}) %collective-permute-start.1) | collective-permute-done | bytes 147488 | tf_op jit(solution)/shard_map/ppermute | solution.py:189
  36.4 2.6 %shard_map.64 = bf16[16,48,512]{2,1,0:T(8,128)(2,1)} custom-call(bf16[96,768]{1,0:T(8,128)(2,1)S(1)} %collective-permute-done.1.far_ref, bf16[96,3072]{1,0:T(8,128)(2,1)S(1)} %shard_map.59.stay_ref, f32[192,2048]{1,0:T(8,128)S(1)} %get-tuple-element.49.gate_in, f32[192,2048]{1,0:T(8,128)S(1)} %get-tuple-element.50.up_in, bf16[1,3072,2048]{2,1,0:T(8,128)(2,1)S(1)} %bitcast.3, ...), custom_call_target="tpu_custom_call" | custom-call | tf_op jit(solution)/shard_map/pallas_call | solution.py:38
  38.9 5.6 %all-to-all-start = ((bf16[16,48,512]{2,1,0:T(8,128)(2,1)}), bf16[16,48,512]{2,1,0:T(8,128)(2,1)S(1)}, u32[]{:S(2)}, u32[]{:S(2)}) async-start(bf16[16,48,512]{2,1,0:T(8,128)(2,1)} %shard_map.64), calls=%async_computation | async-start | bytes 1572864 | tf_op jit(solution)/shard_map/all_to_all | solution.py:34
  44.5 0.0 copy-done.1
  44.5 0.0 copy-done.2
  44.5 0.4 shard_map.55
  45.0 18.2 %all-to-all-done.recv_ref = bf16[16,48,512]{2,1,0:T(8,128)(2,1)S(1)} async-done(((bf16[16,48,512]{2,1,0:T(8,128)(2,1)}), bf16[16,48,512]{2,1,0:T(8,128)(2,1)S(1)}, u32[]{:S(2)}, u32[]{:S(2)}) %all-to-all-start) | async-done | bytes 786464 | tf_op jit(solution)/shard_map/all_to_all | solution.py:34
  63.2 1.3 %shard_map.65 = bf16[24,2,8192]{2,1,0:T(2,128)(2,1)} custom-call(bf16[192,192]{1,0:T(8,128)(2,1)S(1)} %get-tuple-element.28.picks_ref, f32[48,128]{1,0:T(8,128)S(1)} %get-tuple-element.29.column_ref, bf16[16,48,512]{2,1,0:T(8,128)(2,1)S(1)} %all-to-all-done.recv_ref), custom_call_target="tpu_custom_call" | custom-call | bytes 1572864 | tf_op jit(solution)/shard_map/pallas_call | solution.py:38
  (7 shorter events, 0.0 us)
Async XLA Ops:
  0.0 28.8 %slice-start = ((s8[12582912]{0:T(1024)(128)(4,1)}), s8[4194304]{0:T(1024)(128)(4,1)S(1)}, s32[]{:S(2)}) async-start(s8[12582912]{0:T(1024)(128)(4,1)} %bitcast.2), calls=%async_computation.1 | async-start | bytes 8388608
  0.0 28.8 %slice-start.1 = ((s8[12582912]{0:T(1024)(128)(4,1)}), s8[4194304]{0:T(1024)(128)(4,1)S(1)}, s32[]{:S(2)}) async-start(s8[12582912]{0:T(1024)(128)(4,1)} %bitcast.2), calls=%async_computation.2 | async-start | bytes 8388608
  0.0 28.8 %slice-start.2 = ((s8[12582912]{0:T(1024)(128)(4,1)}), s8[4194304]{0:T(1024)(128)(4,1)S(1)}, s32[]{:S(2)}) async-start(s8[12582912]{0:T(1024)(128)(4,1)} %bitcast.2), calls=%async_computation.3 | async-start | bytes 8388608
  0.0 28.8 %copy-start = (bf16[1,3072,2048]{2,1,0:T(8,128)(2,1)S(1)}, bf16[1,3072,2048]{2,1,0:T(8,128)(2,1)}, u32[]{:S(2)}) copy-start(bf16[1,3072,2048]{2,1,0:T(8,128)(2,1)} %up_all.7) | copy-start | bytes 37748740
  20.0 2.0 %collective-permute-start = (bf16[96,3200]{1,0:T(8,128)(2,1)S(1)}, bf16[96,3200]{1,0:T(8,128)(2,1)S(1)}, u32[]{:S(2)}, u32[]{:S(2)}) collective-permute-start(bf16[96,3200]{1,0:T(8,128)(2,1)S(1)} %all_gather.3.own_ref.in_ref.refs_0_), channel_id=1, source_target_pairs={{0,1},{1,0},{2,3},{3,2},{4,5},{5,4},{6,7},{7,6},{8,9},{9,8},{10,11... | collective-permute-start | bytes 1843208 | tf_op jit(solution)/shard_map/ppermute | solution.py:189
  20.0 7.3 %collective-permute-start.4 = (bf16[96,640]{1,0:T(8,128)(2,1)S(1)}, bf16[96,640]{1,0:T(8,128)(2,1)S(1)}, u32[]{:S(2)}, u32[]{:S(2)}) collective-permute-start(bf16[96,640]{1,0:T(8,128)(2,1)S(1)} %shard_map.58), channel_id=1, source_target_pairs={{0,2},{1,3},{2,0},{3,1},{4,6},{5,7},{6,4},{7,5},{8,10},{9,11},{10,... | collective-permute-start | bytes 368648 | tf_op jit(solution)/shard_map/ppermute | solution.py:189
  22.9 7.4 %collective-permute-start.3 = (bf16[96,896]{1,0:T(8,128)(2,1)S(1)}, bf16[96,896]{1,0:T(8,128)(2,1)S(1)}, u32[]{:S(2)}, u32[]{:S(2)}) collective-permute-start(bf16[96,896]{1,0:T(8,128)(2,1)S(1)} %get-tuple-element.32), channel_id=1, source_target_pairs={{0,2},{1,3},{2,0},{3,1},{4,6},{5,7},{6,4},{7,5},{8,10},{9,11},{10,... | collective-permute-start | bytes 516104 | tf_op jit(solution)/shard_map/ppermute | solution.py:189
  24.5 9.4 %collective-permute-start.2 = (bf16[96,896]{1,0:T(8,128)(2,1)S(1)}, bf16[96,896]{1,0:T(8,128)(2,1)S(1)}, u32[]{:S(2)}, u32[]{:S(2)}) collective-permute-start(bf16[96,896]{1,0:T(8,128)(2,1)S(1)} %get-tuple-element.31), channel_id=1, source_target_pairs={{0,2},{1,3},{2,0},{3,1},{4,6},{5,7},{6,4},{7,5},{8,10},{9,11},{10,... | collective-permute-start | bytes 516104 | tf_op jit(solution)/shard_map/ppermute | solution.py:189
  25.0 11.4 %collective-permute-start.1 = (bf16[96,768]{1,0:T(8,128)(2,1)S(1)}, bf16[96,768]{1,0:T(8,128)(2,1)S(1)}, u32[]{:S(2)}, u32[]{:S(2)}) collective-permute-start(bf16[96,768]{1,0:T(8,128)(2,1)S(1)} %get-tuple-element.30), channel_id=1, source_target_pairs={{0,2},{1,3},{2,0},{3,1},{4,6},{5,7},{6,4},{7,5},{8,10},{9,11},{10,... | collective-permute-start | bytes 442376 | tf_op jit(solution)/shard_map/ppermute | solution.py:189
  27.3 1.4 %collective-permute-start.5 = (bf16[96,640]{1,0:T(8,128)(2,1)S(1)}, bf16[96,640]{1,0:T(8,128)(2,1)S(1)}, u32[]{:S(2)}, u32[]{:S(2)}) collective-permute-start(bf16[96,640]{1,0:T(8,128)(2,1)S(1)} %collective-permute-done.4.refs_0_), channel_id=1, source_target_pairs={{0,1},{1,0},{2,3},{3,2},{4,5},{5,4},{6,7},{7,6},{8,9},{9,8},{10,11... | collective-permute-start | bytes 368648 | tf_op jit(solution)/shard_map/ppermute | solution.py:189
  38.9 5.6 %copy-start.1 = (s32[24,2]{0,1:T(2,128)S(1)}, s32[24,2]{0,1:T(2,128)}, u32[]{:S(2)}) copy-start(s32[24,2]{0,1:T(2,128)} %param.6) | copy-start | bytes 580
  38.9 5.6 %copy-start.2 = (f32[24,2]{0,1:T(2,128)S(1)}, f32[24,2]{0,1:T(2,128)}, u32[]{:S(2)}) copy-start(f32[24,2]{0,1:T(2,128)} %param.7) | copy-start | bytes 580
  38.9 24.3 %all-to-all-start = ((bf16[16,48,512]{2,1,0:T(8,128)(2,1)}), bf16[16,48,512]{2,1,0:T(8,128)(2,1)S(1)}, u32[]{:S(2)}, u32[]{:S(2)}) async-start(bf16[16,48,512]{2,1,0:T(8,128)(2,1)} %shard_map.64), calls=%async_computation | async-start | bytes 1572864 | tf_op jit(solution)/shard_map/all_to_all | solution.py:34

commit v13 on v12

--- a/solution.py
+++ b/solution.py
@@ -82,7 +82,7 @@
     copy.wait()
 
 
-def rows_of(ids_block, source, expert, rows, tok_rows, capacity):
+def rows_of(ids_block, group, source, expert, rows, tok_rows, capacity):
     tall = ids_block.shape[0]
     names = ids_block.astype(jnp.float32)
     expert = expert.astype(jnp.float32)
@@ -91,25 +91,33 @@
     lower = ((later > earlier) & (later // tok_rows == earlier // tok_rows)).astype(jnp.bfloat16)
     flags = jnp.broadcast_to(named.astype(jnp.float32), (tall, 128)).astype(jnp.bfloat16)
     before = exact_dot(lower, flags)[:, 0:1].astype(jnp.int32)
-    layer = iota((tall, 1), 0) // tok_rows
-    target = jnp.where(named, (layer * 2 + source) * capacity + before, -1)
+    target = jnp.where(named & (group >= 0), (group * 2 + source) * capacity + before, -1)
     return (iota((tall, rows), 1) == target).astype(jnp.bfloat16)
 
 
-def picked(ref, source, expert, rows, tok_rows, capacity, start, stop):
-    sel = rows_of(ref[:, :128], source, expert, rows, tok_rows, capacity)
+def picked(ref, group, source, expert, rows, tok_rows, capacity, start, stop):
+    sel = rows_of(ref[:, :128], group, source, expert, rows, tok_rows, capacity)
     return transposed_dot(sel, ref[:, 128 + start : 128 + stop])
 
 
-def cut_kernel(in_ref, out_ref):
-    out_ref[...] = in_ref[:, : out_ref.shape[1]]
+def layer_of(ref, tok_rows):
+    return iota((ref.shape[0], 1), 0) // tok_rows
+
+
+def cut_kernel(tok_rows, in_ref, out_ref):
+    shape = (out_ref.shape[0], in_ref.shape[0])
+    row, place = iota(shape, 0), iota(shape, 1)
+    layer = (row // tok_rows + 1) ^ lax.axis_index("et")
+    move = (place == layer * tok_rows + row % tok_rows).astype(in_ref.dtype)
+    out_ref[...] = exact_dot(move, in_ref[:, : out_ref.shape[1]]).astype(out_ref.dtype)
 
 
 def select_kernel(tok_rows, capacity, own_ref, near_ref, *outs):
     expert, core = lax.axis_index("ep") ^ 2, lax.axis_index("ep") % 2
     rows = outs[0].shape[0]
+    group = (layer_of(own_ref, tok_rows) ^ lax.axis_index("et")) - 1
     found = [
-        (rows_of(ref[:, :128], source, expert, rows, tok_rows, capacity), ref)
+        (rows_of(ref[:, :128], group, source, expert, rows, tok_rows, capacity), ref)
         for ref, source in ((own_ref, core), (near_ref, 1 - core))
     ]
     start = own_ref.shape[1] - sum(out.shape[1] for out in outs)
@@ -119,41 +127,58 @@
         start = stop
 
 
-def pick_kernel(tok_rows, capacity, swapped, *refs):
-    blocks, rows_ref = refs[:-1], refs[-1]
+def stay_kernel(tok_rows, capacity, own_ref, near_ref, early_ref, early_other, stay_ref, first_ref):
+    expert, core = lax.axis_index("ep"), lax.axis_index("ep") % 2
+    group = layer_of(own_ref, tok_rows) ^ lax.axis_index("et")
+    for out, refs, place in (
+        (stay_ref, (own_ref, near_ref), group),
+        (first_ref, (early_ref, early_other), layer_of(early_ref, tok_rows)),
+    ):
+        rows, width = out.shape
+        out[...] = sum(
+            picked(ref, place, core ^ other, expert, rows, tok_rows, capacity, 0, width)
+            for other, ref in enumerate(refs)
+        ).astype(out.dtype)
+
+
+def pick_kernel(tok_rows, capacity, ref, rows_ref):
     rows, width = rows_ref.shape
     expert, core = lax.axis_index("ep"), lax.axis_index("ep") % 2
-    rows_ref[...] = sum(
-        picked(ref, core ^ other, expert, rows, tok_rows, capacity, 0, width) for ref, other in zip(blocks, swapped)
-    ).astype(rows_ref.dtype)
-
-
-def gather_rows(x_ref, stay, far):
+    group = layer_of(ref, tok_rows)
+    rows_ref[...] = picked(ref, group, core, expert, rows, tok_rows, capacity, 0, width).astype(rows_ref.dtype)
+
+
+def gather_rows(x_ref, stay, first, far):
     rows = stay.shape[0]
     chip = lax.axis_index("ep") // 2
     x_ref[pl.ds(pl.multiple_of(chip * rows, rows), rows), :] = stay
-    x_ref[pl.ds(pl.multiple_of((1 - chip) * rows, rows), rows), :] = far
-
-
-def first_kernel(tok_rows, capacity, other_ref, part_ref, stay_ref, gate_all, up_all, gate_ref, up_ref, x_ref):
+    far = jnp.concatenate([first.astype(jnp.float32), far.astype(jnp.float32)], axis=0)
+    x_ref[pl.ds(pl.multiple_of((1 - chip) * rows, rows), rows), :] = far.astype(x_ref.dtype)
+
+
+def first_kernel(tok_rows, capacity, other_ref, part_ref, stay_ref, early_ref, gate_all, up_all, *refs):
+    gate_ref, up_ref, x_ref = refs
     rows, cut = part_ref.shape
     expert, core = lax.axis_index("ep"), lax.axis_index("ep") % 2
-    far = picked(other_ref, 1 - core, expert, rows, tok_rows, capacity, 0, cut) + part_ref[...].astype(jnp.float32)
-    gather_rows(x_ref, stay_ref[:, :cut], far.astype(x_ref.dtype))
+    group = layer_of(other_ref, tok_rows)
+    far = picked(other_ref, group, 1 - core, expert, rows, tok_rows, capacity, 0, cut)
+    far = far + part_ref[...].astype(jnp.float32)
+    gather_rows(x_ref, stay_ref[:, :cut], early_ref[:, :cut], far)
     gate_ref[...] = exact_dot(x_ref[...], gate_all[0, :cut, :])
     up_ref[...] = exact_dot(x_ref[...], up_all[0, :cut, :])
 
 
-def middle_kernel(start, far_ref, stay_ref, gate_in, up_in, gate_all, up_all, gate_ref, up_ref, x_ref):
+def middle_kernel(start, far_ref, stay_ref, early_ref, gate_in, up_in, gate_all, up_all, gate_ref, up_ref, x_ref):
     stop = start + far_ref.shape[1]
-    gather_rows(x_ref, stay_ref[:, start:stop], far_ref[...])
+    gather_rows(x_ref, stay_ref[:, start:stop], early_ref[:, start:stop], far_ref[...])
     gate_ref[...] = gate_in[...] + exact_dot(x_ref[...], gate_all[0, start:stop, :])
     up_ref[...] = up_in[...] + exact_dot(x_ref[...], up_all[0, start:stop, :])
 
 
-def second_kernel(folds, experts, far_ref, stay_ref, gate_in, up_in, gate_all, up_all, out_ref, x_ref, hidden_ref):
+def second_kernel(folds, experts, far_ref, stay_ref, early_ref, gate_in, up_in, gate_all, up_all, *refs):
+    out_ref, x_ref, hidden_ref = refs
     cut = stay_ref.shape[1] - far_ref.shape[1]
-    gather_rows(x_ref, stay_ref[:, cut:], far_ref[...])
+    gather_rows(x_ref, stay_ref[:, cut:], early_ref[:, cut:], far_ref[...])
     gate_val = gate_in[...] + exact_dot(x_ref[...], gate_all[0, cut:, :])
     up_val = up_in[...] + exact_dot(x_ref[...], up_all[0, cut:, :])
     hidden_ref[...] = gate_val / (1.0 + jnp.exp(-gate_val)) * up_val
@@ -164,12 +189,15 @@
     peers = out_ref.shape[0]
     capacity = hidden_ref.shape[0] // peers
     span = hidden_ref.shape[1] // folds
-    for peer in range(peers):
-        layer, chip, core = peer // experts, peer % experts // 2, peer % 2
-        start = (chip * (peers // 2) + layer * 2 + core) * capacity
-        rows = hidden_ref[start : start + capacity, :]
-        pieces = [rows[:, fold * span : (fold + 1) * span] for fold in range(folds)]
-        out_ref[peer] = jnp.concatenate(pieces, axis=0).astype(out_ref.dtype)
+    mine = lax.axis_index("et")
+    for peer in range(0, peers, 2):
+        layer, chip = peer // experts, peer % experts // 2
+        start = chip * (peers // 2) * capacity + (layer ^ mine) * (2 * capacity)
+        both = hidden_ref[pl.ds(pl.multiple_of(start, 8), 2 * capacity), :]
+        for core in range(2):
+            rows = both[core * capacity : (core + 1) * capacity]
+            pieces = [rows[:, fold * span : (fold + 1) * span] for fold in range(folds)]
+            out_ref[peer + core] = jnp.concatenate(pieces, axis=0).astype(out_ref.dtype)
 
 
 def routed_by_columns(tokens, expert_ids, w_gate, w_up, peers, capacity, folds):
@@ -195,23 +223,24 @@
         (expert_ids.T, tokens, w_gate, w_up),
         scratch=[pltpu.VMEM((2, tok_rows), jnp.int32), pltpu.SemaphoreType.DMA((2,))],
     )
+    early = swap(packed, 2)
     own = lax.all_gather(packed, "et", axis=0, tiled=True)
-    part = local_kernel(cut_kernel, array(own.shape[0], 128 + cut), (own,))
-    near, far = swap(own, 1), swap(part, 2)
+    own, early = lax.optimization_barrier((own, early))
+    others = own.shape[0] - tok_rows
+    rest = half - 2 * capacity
+    part = local_kernel(functools.partial(cut_kernel, tok_rows), array(others, 128 + cut), (own,))
+    near, far, early_other = swap(own, 1), swap(part, 2), swap(early, 1)
     kernel = functools.partial(select_kernel, tok_rows, capacity)
     ends = (*cuts[1:], width)
-    laters = local_kernel(kernel, [array(half, stop - start) for start, stop in zip(cuts, ends)], (own, near))
+    laters = local_kernel(kernel, [array(rest, stop - start) for start, stop in zip(cuts, ends)], (own, near))
     later_fars = [swap(later, 2) for later in laters]
-
-    def pick(blocks, swapped, span):
-        kernel = functools.partial(pick_kernel, tok_rows, capacity, swapped)
-        return local_kernel(kernel, array(half, span), blocks)
-
     own, near, *laters = lax.optimization_barrier((own, near, *laters))
-    stay = pick((own, near), (0, 1), width)
+    kernel = functools.partial(stay_kernel, tok_rows, capacity)
+    outs = [array(half, width), array(2 * capacity, width)]
+    stay, first = local_kernel(kernel, outs, (own, near, early, early_other))
     far, stay = lax.optimization_barrier((far, stay))
     far_other = swap(far, 1)
-    far_part = pick((far,), (0,), cut)
+    far_part = local_kernel(functools.partial(pick_kernel, tok_rows, capacity), array(rest, cut), (far,))
     far_other, far_part = lax.optimization_barrier((far_other, far_part))
 
     def sums(kernel, blocks, span):
@@ -219,17 +248,17 @@
         return local_kernel(kernel, out_shape, (*blocks, w_gate, w_up), scratch=[pltpu.VMEM((rows, span), kind)])
 
     gate_sum, up_sum = sums(
-        functools.partial(first_kernel, tok_rows, capacity), (far_other, far_part, stay), cut
+        functools.partial(first_kernel, tok_rows, capacity), (far_other, far_part, stay, first), cut
     )
     for start, later_far in zip(cuts[:-1], later_fars):
         later_far, gate_sum = lax.optimization_barrier((later_far, gate_sum))
         kernel = functools.partial(middle_kernel, start)
-        gate_sum, up_sum = sums(kernel, (later_far, stay, gate_sum, up_sum), later_far.shape[1])
+        gate_sum, up_sum = sums(kernel, (later_far, stay, first, gate_sum, up_sum), later_far.shape[1])
     later_far, gate_sum = lax.optimization_barrier((later_fars[-1], gate_sum))
     return local_kernel(
         functools.partial(second_kernel, folds, experts),
         array(peers, capacity * folds, units // folds),
-        (later_far, stay, gate_sum, up_sum, w_gate, w_up),
+        (later_far, stay, first, gate_sum, up_sum, w_gate, w_up),
         scratch=[pltpu.VMEM((rows, width - cuts[-1]), kind), pltpu.VMEM((rows, units), jnp.float32)],
     )
 

time: 64.8 us -> 63.4 us (0.978)
  blocking collectives: 18.9 us -> 17.1 us
  starting transfers between devices: 10.8 us -> 12.5 us
  waiting for transfers between devices: 21.7 us -> 20.1 us
    ppermute x6 -> x8, starting transfers between devices: 5.24 us -> 7.03 us  [swap(): return lax.ppermute(block, 'ep', [(i, i ^ bit) for i in range(experts)])]
    all_gather x1, blocking collectives: 18.9 us -> 17.1 us  [routed_by_columns(): own = lax.all_gather(packed, 'et', axis=0, tiled=True)]
    ppermute x6 -> x8, waiting for transfers between devices: 3.5 us -> 1.82 us  [swap(): return lax.ppermute(block, 'ep', [(i, i ^ bit) for i in range(experts)])]
  transfers between devices with their start and end apart: 7 -> 9, of which waited for: 5 -> 4; matrix products, arithmetic and copies ran while one was open for 0% -> 0% of each run, Pallas kernels for 12% -> 13%
where the time goes in v13:
time: 63.4 us; the launch traced here: 63.1 us
  waiting for transfers between devices  20.1 us (32%)
  blocking collectives  17.1 us (27%)
  Pallas kernels  13.3 us (21%)
  starting transfers between devices  12.5 us (20%)
    all_to_all x1, waiting for transfers between devices, exchange(): lax.all_to_all(blocks, ('et', 'ep'), split_axis=0, concat_axis=0, tiled=T...  18.2 us
    all_gather x1, blocking collectives, routed_by_columns(): own = lax.all_gather(packed, 'et', axis=0, tiled=True)  17.1 us
    pallas_call x11, Pallas kernels, local_kernel(): pl.pallas_call(kernel, out_shape=out_shape, in_specs=[WHOLE] * len(args)...  13.3 us
    ppermute x8, starting transfers between devices, swap(): return lax.ppermute(block, 'ep', [(i, i ^ bit) for i in range(experts)])  7.03 us
    all_to_all x1, starting transfers between devices, exchange(): lax.all_to_all(blocks, ('et', 'ep'), split_axis=0, concat_axis=0, tiled=T...  5.42 us
    ppermute x8, waiting for transfers between devices, swap(): return lax.ppermute(block, 'ep', [(i, i ^ bit) for i in range(experts)])  1.82 us
  transfers between devices with their start and end apart: 9, of which 4 were waited for; matrix products, arithmetic and copies ran while one was open for 0% of the time, Pallas kernels for 13%

profile of v13, /device:TPU:0, one launch (start us, length us, event | category | flops | bytes accessed | tf_op | source)
XLA Modules:
  0.0 63.1 jit_solution(17970707583962182138)
XLA Ops:
  0.0 1.1 %shard_map.56 = bf16[24,3200]{1,0:T(8,128)(2,1)S(1)} custom-call(s32[2,24]{1,0:T(2,128)} %bitcast.4, bf16[24,3072]{1,0:T(8,128)(2,1)} %tokens_hbm.1, bf16[1,3072,2048]{2,1,0:T(8,128)(2,1)} %gate_all.7, bf16[1,3072,2048]{2,1,0:T(8,128)(2,1)} %up_all.7), custom_call_target="tpu_custom_call" | custom-call | tf_op jit(solution)/shard_map/pallas_call | solution.py:38
  1.1 3.0 %collective-permute-start = (bf16[24,3200]{1,0:T(8,128)(2,1)S(1)}, bf16[24,3200]{1,0:T(8,128)(2,1)S(1)}, u32[]{:S(2)}, u32[]{:S(2)}) collective-permute-start(bf16[24,3200]{1,0:T(8,128)(2,1)S(1)} %shard_map.56), channel_id=1, source_target_pairs={{0,2},{1,3},{2,0},{3,1},{4,6},{5,7},{6,4},{7,5},{8,10},{9,11},{10,... | collective-permute-start | bytes 460808 | tf_op jit(solution)/shard_map/ppermute | solution.py:217
  4.1 17.1 %all_gather.3.own_ref.in_ref = bf16[96,3200]{1,0:T(8,128)(2,1)S(1)} all-gather(bf16[24,3200]{1,0:T(8,128)(2,1)S(1)} %shard_map.56), channel_id=1, replica_groups=mesh['groups'=2,'et'=4,'ep'=4] {'et'}, dimensions={0}, use_global_device_ids=true | all-gather | bytes 768000 | tf_op jit(solution)/shard_map/all_gather | solution.py:227
  21.3 0.0 collective-permute-done.early_ref
  21.3 0.0 collective-permute-start.1
  21.3 0.5 collective-permute-start.6
  21.8 0.2 shard_map.58
  22.0 0.6 collective-permute-start.5
  22.6 0.8 %collective-permute-done.1.near_ref = bf16[96,3200]{1,0:T(8,128)(2,1)S(1)} collective-permute-done((bf16[96,3200]{1,0:T(8,128)(2,1)S(1)}, bf16[96,3200]{1,0:T(8,128)(2,1)S(1)}, u32[]{:S(2)}, u32[]{:S(2)}) %collective-permute-start.1) | collective-permute-done | bytes 614432 | tf_op jit(solution)/shard_map/ppermute | solution.py:217
  23.3 0.8 %shard_map.57 = (bf16[72,896]{1,0:T(8,128)(2,1)S(1)}, bf16[72,896]{1,0:T(8,128)(2,1)S(1)}, bf16[72,768]{1,0:T(8,128)(2,1)S(1)}) custom-call(bf16[96,3200]{1,0:T(8,128)(2,1)S(1)} %all_gather.3.own_ref.in_ref, bf16[96,3200]{1,0:T(8,128)(2,1)S(1)} %collective-permute-done.1.near_ref), custom_call_target="tpu_custom_call" | custom-call | tf_op jit(solution)/shard_map/pallas_call | solution.py:38
  24.1 0.8 %collective-permute-start.4 = (bf16[72,896]{1,0:T(8,128)(2,1)S(1)}, bf16[72,896]{1,0:T(8,128)(2,1)S(1)}, u32[]{:S(2)}, u32[]{:S(2)}) collective-permute-start(bf16[72,896]{1,0:T(8,128)(2,1)S(1)} %get-tuple-element.37), channel_id=1, source_target_pairs={{0,2},{1,3},{2,0},{3,1},{4,6},{5,7},{6,4},{7,5},{8,10},{9,11},{10,... | collective-permute-start | bytes 387080 | tf_op jit(solution)/shard_map/ppermute | solution.py:217
  24.9 1.3 %collective-permute-start.3 = (bf16[72,896]{1,0:T(8,128)(2,1)S(1)}, bf16[72,896]{1,0:T(8,128)(2,1)S(1)}, u32[]{:S(2)}, u32[]{:S(2)}) collective-permute-start(bf16[72,896]{1,0:T(8,128)(2,1)S(1)} %get-tuple-element.36), channel_id=1, source_target_pairs={{0,2},{1,3},{2,0},{3,1},{4,6},{5,7},{6,4},{7,5},{8,10},{9,11},{10,... | collective-permute-start | bytes 387080 | tf_op jit(solution)/shard_map/ppermute | solution.py:217
  26.2 0.7 %collective-permute-start.2 = (bf16[72,768]{1,0:T(8,128)(2,1)S(1)}, bf16[72,768]{1,0:T(8,128)(2,1)S(1)}, u32[]{:S(2)}, u32[]{:S(2)}) collective-permute-start(bf16[72,768]{1,0:T(8,128)(2,1)S(1)} %get-tuple-element.35), channel_id=1, source_target_pairs={{0,2},{1,3},{2,0},{3,1},{4,6},{5,7},{6,4},{7,5},{8,10},{9,11},{10,... | collective-permute-start | bytes 331784 | tf_op jit(solution)/shard_map/ppermute | solution.py:217
  26.9 0.0 collective-permute-done.6.early_other
  26.9 1.2 %shard_map.59 = (bf16[96,3072]{1,0:T(8,128)(2,1)S(1)}, bf16[24,3072]{1,0:T(8,128)(2,1)S(1)}) custom-call(bf16[96,3200]{1,0:T(8,128)(2,1)S(1)} %all_gather.3.own_ref.in_ref, bf16[96,3200]{1,0:T(8,128)(2,1)S(1)} %collective-permute-done.1.near_ref, bf16[24,3200]{1,0:T(8,128)(2,1)S(1)} %collective-permute-done.early_ref, ...), custom_call_target="tpu_custom_call" | custom-call | tf_op jit(solution)/shard_map/pallas_call | solution.py:38
  28.2 0.0 collective-permute-done.5.ref
  28.2 0.1 collective-permute-start.7
  28.3 0.5 shard_map.60.part_ref
  28.8 0.7 %collective-permute-done.7.other_ref = bf16[72,640]{1,0:T(8,128)(2,1)S(1)} collective-permute-done((bf16[72,640]{1,0:T(8,128)(2,1)S(1)}, bf16[72,640]{1,0:T(8,128)(2,1)S(1)}, u32[]{:S(2)}, u32[]{:S(2)}) %collective-permute-start.7) | collective-permute-done | bytes 92192 | tf_op jit(solution)/shard_map/ppermute | solution.py:217
  29.5 0.0 slice-done
  29.5 0.0 slice-done.1
  29.6 1.5 %shard_map.61 = (f32[192,2048]{1,0:T(8,128)S(1)}, f32[192,2048]{1,0:T(8,128)S(1)}) custom-call(bf16[72,640]{1,0:T(8,128)(2,1)S(1)} %collective-permute-done.7.other_ref, bf16[72,512]{1,0:T(8,128)(2,1)S(1)} %shard_map.60.part_ref, bf16[96,3072]{1,0:T(8,128)(2,1)S(1)} %get-tuple-element.45.stay_ref, bf16[24,3072]{1,0:T(8,128)(2,1)S(1)} %get-tuple-element.46.early_ref, ...), custom_call_target="tpu_custom_call" | custom-call | tf_op jit(solution)/shard_map/pallas_call | solution.py:38
  31.1 0.0 collective-permute-done.4.far_ref
  31.1 1.9 %shard_map.62 = (f32[192,2048]{1,0:T(8,128)S(1)}, f32[192,2048]{1,0:T(8,128)S(1)}) custom-call(bf16[72,896]{1,0:T(8,128)(2,1)S(1)} %collective-permute-done.4.far_ref, bf16[96,3072]{1,0:T(8,128)(2,1)S(1)} %get-tuple-element.45.stay_ref, bf16[24,3072]{1,0:T(8,128)(2,1)S(1)} %get-tuple-element.46.early_ref, f32[192,2048]{1,0:T(8,128)S(1)} %get-tuple-element.49.gate_in, ...), custom_call_target="tpu_custom_call" | custom-call | tf_op jit(solution)/shard_map/pallas_call | solution.py:38
  32.9 0.3 collective-permute-done.3.far_ref
  33.3 1.8 %shard_map.63 = (f32[192,2048]{1,0:T(8,128)S(1)}, f32[192,2048]{1,0:T(8,128)S(1)}) custom-call(bf16[72,896]{1,0:T(8,128)(2,1)S(1)} %collective-permute-done.3.far_ref, bf16[96,3072]{1,0:T(8,128)(2,1)S(1)} %get-tuple-element.45.stay_ref, bf16[24,3072]{1,0:T(8,128)(2,1)S(1)} %get-tuple-element.46.early_ref, f32[192,2048]{1,0:T(8,128)S(1)} %get-tuple-element.53.gate_in, ...), custom_call_target="tpu_custom_call" | custom-call | tf_op jit(solution)/shard_map/pallas_call | solution.py:38
  35.1 0.0 collective-permute-done.2.far_ref
  35.1 2.6 %shard_map.64 = bf16[16,48,512]{2,1,0:T(8,128)(2,1)} custom-call(bf16[72,768]{1,0:T(8,128)(2,1)S(1)} %collective-permute-done.2.far_ref, bf16[96,3072]{1,0:T(8,128)(2,1)S(1)} %get-tuple-element.45.stay_ref, bf16[24,3072]{1,0:T(8,128)(2,1)S(1)} %get-tuple-element.46.early_ref, f32[192,2048]{1,0:T(8,128)S(1)} %get-tuple-element.57.gate_in, ...), custom_call_target="tpu_custom_call" | custom-call | tf_op jit(solution)/shard_map/pallas_call | solution.py:38
  37.7 5.4 %all-to-all-start = ((bf16[16,48,512]{2,1,0:T(8,128)(2,1)}), bf16[16,48,512]{2,1,0:T(8,128)(2,1)S(1)}, u32[]{:S(2)}, u32[]{:S(2)}) async-start(bf16[16,48,512]{2,1,0:T(8,128)(2,1)} %shard_map.64), calls=%async_computation | async-start | bytes 1572864 | tf_op jit(solution)/shard_map/all_to_all | solution.py:34
  43.2 0.4 shard_map.55
  43.6 18.2 %all-to-all-done.recv_ref = bf16[16,48,512]{2,1,0:T(8,128)(2,1)S(1)} async-done(((bf16[16,48,512]{2,1,0:T(8,128)(2,1)}), bf16[16,48,512]{2,1,0:T(8,128)(2,1)S(1)}, u32[]{:S(2)}, u32[]{:S(2)}) %all-to-all-start) | async-done | bytes 786464 | tf_op jit(solution)/shard_map/all_to_all | solution.py:34
  61.9 1.3 %shard_map.65 = bf16[24,2,8192]{2,1,0:T(2,128)(2,1)} custom-call(bf16[192,192]{1,0:T(8,128)(2,1)S(1)} %get-tuple-element.32.picks_ref, f32[48,128]{1,0:T(8,128)S(1)} %get-tuple-element.33.column_ref, bf16[16,48,512]{2,1,0:T(8,128)(2,1)S(1)} %all-to-all-done.recv_ref), custom_call_target="tpu_custom_call" | custom-call | bytes 1572864 | tf_op jit(solution)/shard_map/pallas_call | solution.py:38
  (11 shorter events, 0.0 us)
Async XLA Ops:
  0.0 29.5 %slice-start = ((s8[12582912]{0:T(1024)(128)(4,1)}), s8[4194304]{0:T(1024)(128)(4,1)S(1)}, s32[]{:S(2)}) async-start(s8[12582912]{0:T(1024)(128)(4,1)} %bitcast.2), calls=%async_computation.1 | async-start | bytes 8388608
  0.0 29.5 %slice-start.1 = ((s8[12582912]{0:T(1024)(128)(4,1)}), s8[4194304]{0:T(1024)(128)(4,1)S(1)}, s32[]{:S(2)}) async-start(s8[12582912]{0:T(1024)(128)(4,1)} %bitcast.2), calls=%async_computation.2 | async-start | bytes 8388608
  0.0 29.5 %slice-start.2 = ((s8[12582912]{0:T(1024)(128)(4,1)}), s8[4194304]{0:T(1024)(128)(4,1)S(1)}, s32[]{:S(2)}) async-start(s8[12582912]{0:T(1024)(128)(4,1)} %bitcast.2), calls=%async_computation.3 | async-start | bytes 8388608
  0.0 29.5 %copy-start = (bf16[1,3072,2048]{2,1,0:T(8,128)(2,1)S(1)}, bf16[1,3072,2048]{2,1,0:T(8,128)(2,1)}, u32[]{:S(2)}) copy-start(bf16[1,3072,2048]{2,1,0:T(8,128)(2,1)} %up_all.7) | copy-start | bytes 37748740
  1.1 20.2 %collective-permute-start = (bf16[24,3200]{1,0:T(8,128)(2,1)S(1)}, bf16[24,3200]{1,0:T(8,128)(2,1)S(1)}, u32[]{:S(2)}, u32[]{:S(2)}) collective-permute-start(bf16[24,3200]{1,0:T(8,128)(2,1)S(1)} %shard_map.56), channel_id=1, source_target_pairs={{0,2},{1,3},{2,0},{3,1},{4,6},{5,7},{6,4},{7,5},{8,10},{9,11},{10,... | collective-permute-start | bytes 460808 | tf_op jit(solution)/shard_map/ppermute | solution.py:217
  21.3 2.0 %collective-permute-start.1 = (bf16[96,3200]{1,0:T(8,128)(2,1)S(1)}, bf16[96,3200]{1,0:T(8,128)(2,1)S(1)}, u32[]{:S(2)}, u32[]{:S(2)}) collective-permute-start(bf16[96,3200]{1,0:T(8,128)(2,1)S(1)} %all_gather.3.own_ref.in_ref), channel_id=1, source_target_pairs={{0,1},{1,0},{2,3},{3,2},{4,5},{5,4},{6,7},{7,6},{8,9},{9,8},{10,11... | collective-permute-start | bytes 1843208 | tf_op jit(solution)/shard_map/ppermute | solution.py:217
  21.3 5.6 %collective-permute-start.6 = (bf16[24,3200]{1,0:T(8,128)(2,1)S(1)}, bf16[24,3200]{1,0:T(8,128)(2,1)S(1)}, u32[]{:S(2)}, u32[]{:S(2)}) collective-permute-start(bf16[24,3200]{1,0:T(8,128)(2,1)S(1)} %collective-permute-done.early_ref), channel_id=1, source_target_pairs={{0,1},{1,0},{2,3},{3,2},{4,5},{5,4},{6,7},{7,6},{8,9},{9,8},{10,11... | collective-permute-start | bytes 460808 | tf_op jit(solution)/shard_map/ppermute | solution.py:217
  22.0 6.2 %collective-permute-start.5 = (bf16[72,640]{1,0:T(8,128)(2,1)S(1)}, bf16[72,640]{1,0:T(8,128)(2,1)S(1)}, u32[]{:S(2)}, u32[]{:S(2)}) collective-permute-start(bf16[72,640]{1,0:T(8,128)(2,1)S(1)} %shard_map.58), channel_id=1, source_target_pairs={{0,2},{1,3},{2,0},{3,1},{4,6},{5,7},{6,4},{7,5},{8,10},{9,11},{10,... | collective-permute-start | bytes 276488 | tf_op jit(solution)/shard_map/ppermute | solution.py:217
  24.1 7.0 %collective-permute-start.4 = (bf16[72,896]{1,0:T(8,128)(2,1)S(1)}, bf16[72,896]{1,0:T(8,128)(2,1)S(1)}, u32[]{:S(2)}, u32[]{:S(2)}) collective-permute-start(bf16[72,896]{1,0:T(8,128)(2,1)S(1)} %get-tuple-element.37), channel_id=1, source_target_pairs={{0,2},{1,3},{2,0},{3,1},{4,6},{5,7},{6,4},{7,5},{8,10},{9,11},{10,... | collective-permute-start | bytes 387080 | tf_op jit(solution)/shard_map/ppermute | solution.py:217
  24.9 8.4 %collective-permute-start.3 = (bf16[72,896]{1,0:T(8,128)(2,1)S(1)}, bf16[72,896]{1,0:T(8,128)(2,1)S(1)}, u32[]{:S(2)}, u32[]{:S(2)}) collective-permute-start(bf16[72,896]{1,0:T(8,128)(2,1)S(1)} %get-tuple-element.36), channel_id=1, source_target_pairs={{0,2},{1,3},{2,0},{3,1},{4,6},{5,7},{6,4},{7,5},{8,10},{9,11},{10,... | collective-permute-start | bytes 387080 | tf_op jit(solution)/shard_map/ppermute | solution.py:217
  26.2 8.9 %collective-permute-start.2 = (bf16[72,768]{1,0:T(8,128)(2,1)S(1)}, bf16[72,768]{1,0:T(8,128)(2,1)S(1)}, u32[]{:S(2)}, u32[]{:S(2)}) collective-permute-start(bf16[72,768]{1,0:T(8,128)(2,1)S(1)} %get-tuple-element.35), channel_id=1, source_target_pairs={{0,2},{1,3},{2,0},{3,1},{4,6},{5,7},{6,4},{7,5},{8,10},{9,11},{10,... | collective-permute-start | bytes 331784 | tf_op jit(solution)/shard_map/ppermute | solution.py:217
  28.2 1.4 %collective-permute-start.7 = (bf16[72,640]{1,0:T(8,128)(2,1)S(1)}, bf16[72,640]{1,0:T(8,128)(2,1)S(1)}, u32[]{:S(2)}, u32[]{:S(2)}) collective-permute-start(bf16[72,640]{1,0:T(8,128)(2,1)S(1)} %collective-permute-done.5.ref), channel_id=1, source_target_pairs={{0,1},{1,0},{2,3},{3,2},{4,5},{5,4},{6,7},{7,6},{8,9},{9,8},{10,11... | collective-permute-start | bytes 276488 | tf_op jit(solution)/shard_map/ppermute | solution.py:217
  37.7 5.4 %copy-start.1 = (s32[24,2]{0,1:T(2,128)S(1)}, s32[24,2]{0,1:T(2,128)}, u32[]{:S(2)}) copy-start(s32[24,2]{0,1:T(2,128)} %param.6) | copy-start | bytes 580
  37.7 5.4 %copy-start.2 = (f32[24,2]{0,1:T(2,128)S(1)}, f32[24,2]{0,1:T(2,128)}, u32[]{:S(2)}) copy-start(f32[24,2]{0,1:T(2,128)} %param.7) | copy-start | bytes 580
  37.7 24.1 %all-to-all-start = ((bf16[16,48,512]{2,1,0:T(8,128)(2,1)}), bf16[16,48,512]{2,1,0:T(8,128)(2,1)S(1)}, u32[]{:S(2)}, u32[]{:S(2)}) async-start(bf16[16,48,512]{2,1,0:T(8,128)(2,1)} %shard_map.64), calls=%async_computation | async-start | bytes 1572864 | tf_op jit(solution)/shard_map/all_to_all | solution.py:34

commit v14 on v13

--- a/solution.py
+++ b/solution.py
@@ -257,7 +257,7 @@
     later_far, gate_sum = lax.optimization_barrier((later_fars[-1], gate_sum))
     return local_kernel(
         functools.partial(second_kernel, folds, experts),
-        array(peers, capacity * folds, units // folds),
+        pltpu.VMEM((peers, capacity * folds, units // folds), kind),
         (later_far, stay, first, gate_sum, up_sum, w_gate, w_up),
         scratch=[pltpu.VMEM((rows, width - cuts[-1]), kind), pltpu.VMEM((rows, units), jnp.float32)],
     )

time: 63.4 us -> 63.4 us (level)
  no operation moved by 1% of the time
where the time goes in v14:
time: 63.4 us; the launch traced here: 63.1 us
  waiting for transfers between devices  20.1 us (32%)
  blocking collectives  17.1 us (27%)
  Pallas kernels  13.3 us (21%)
  starting transfers between devices  12.5 us (20%)
    all_to_all x1, waiting for transfers between devices, exchange(): lax.all_to_all(blocks, ('et', 'ep'), split_axis=0, concat_axis=0, tiled=T...  18.2 us
    all_gather x1, blocking collectives, routed_by_columns(): own = lax.all_gather(packed, 'et', axis=0, tiled=True)  17.1 us
    pallas_call x11, Pallas kernels, local_kernel(): pl.pallas_call(kernel, out_shape=out_shape, in_specs=[WHOLE] * len(args)...  13.3 us
    ppermute x8, starting transfers between devices, swap(): return lax.ppermute(block, 'ep', [(i, i ^ bit) for i in range(experts)])  7.03 us
    all_to_all x1, starting transfers between devices, exchange(): lax.all_to_all(blocks, ('et', 'ep'), split_axis=0, concat_axis=0, tiled=T...  5.42 us
    ppermute x8, waiting for transfers between devices, swap(): return lax.ppermute(block, 'ep', [(i, i ^ bit) for i in range(experts)])  1.82 us
  transfers between devices with their start and end apart: 9, of which 4 were waited for; matrix products, arithmetic and copies ran while one was open for 0% of the time, Pallas kernels for 13%

profile of v14, /device:TPU:0, one launch (start us, length us, event | category | flops | bytes accessed | tf_op | source)
XLA Modules:
  0.0 63.1 jit_solution(17970707583962182138)
XLA Ops:
  0.0 1.1 %shard_map.56 = bf16[24,3200]{1,0:T(8,128)(2,1)S(1)} custom-call(s32[2,24]{1,0:T(2,128)} %bitcast.4, bf16[24,3072]{1,0:T(8,128)(2,1)} %tokens_hbm.1, bf16[1,3072,2048]{2,1,0:T(8,128)(2,1)} %gate_all.7, bf16[1,3072,2048]{2,1,0:T(8,128)(2,1)} %up_all.7), custom_call_target="tpu_custom_call" | custom-call | tf_op jit(solution)/shard_map/pallas_call | solution.py:38
  1.1 3.0 %collective-permute-start = (bf16[24,3200]{1,0:T(8,128)(2,1)S(1)}, bf16[24,3200]{1,0:T(8,128)(2,1)S(1)}, u32[]{:S(2)}, u32[]{:S(2)}) collective-permute-start(bf16[24,3200]{1,0:T(8,128)(2,1)S(1)} %shard_map.56), channel_id=1, source_target_pairs={{0,2},{1,3},{2,0},{3,1},{4,6},{5,7},{6,4},{7,5},{8,10},{9,11},{10,... | collective-permute-start | bytes 460808 | tf_op jit(solution)/shard_map/ppermute | solution.py:217
  4.1 17.1 %all_gather.3.own_ref.in_ref = bf16[96,3200]{1,0:T(8,128)(2,1)S(1)} all-gather(bf16[24,3200]{1,0:T(8,128)(2,1)S(1)} %shard_map.56), channel_id=1, replica_groups=mesh['groups'=2,'et'=4,'ep'=4] {'et'}, dimensions={0}, use_global_device_ids=true | all-gather | bytes 768000 | tf_op jit(solution)/shard_map/all_gather | solution.py:227
  21.3 0.0 collective-permute-done.early_ref
  21.3 0.0 collective-permute-start.1
  21.3 0.5 collective-permute-start.6
  21.8 0.2 shard_map.58
  22.0 0.6 collective-permute-start.5
  22.6 0.8 %collective-permute-done.1.near_ref = bf16[96,3200]{1,0:T(8,128)(2,1)S(1)} collective-permute-done((bf16[96,3200]{1,0:T(8,128)(2,1)S(1)}, bf16[96,3200]{1,0:T(8,128)(2,1)S(1)}, u32[]{:S(2)}, u32[]{:S(2)}) %collective-permute-start.1) | collective-permute-done | bytes 614432 | tf_op jit(solution)/shard_map/ppermute | solution.py:217
  23.3 0.8 %shard_map.57 = (bf16[72,896]{1,0:T(8,128)(2,1)S(1)}, bf16[72,896]{1,0:T(8,128)(2,1)S(1)}, bf16[72,768]{1,0:T(8,128)(2,1)S(1)}) custom-call(bf16[96,3200]{1,0:T(8,128)(2,1)S(1)} %all_gather.3.own_ref.in_ref, bf16[96,3200]{1,0:T(8,128)(2,1)S(1)} %collective-permute-done.1.near_ref), custom_call_target="tpu_custom_call" | custom-call | tf_op jit(solution)/shard_map/pallas_call | solution.py:38
  24.1 0.8 %collective-permute-start.4 = (bf16[72,896]{1,0:T(8,128)(2,1)S(1)}, bf16[72,896]{1,0:T(8,128)(2,1)S(1)}, u32[]{:S(2)}, u32[]{:S(2)}) collective-permute-start(bf16[72,896]{1,0:T(8,128)(2,1)S(1)} %get-tuple-element.37), channel_id=1, source_target_pairs={{0,2},{1,3},{2,0},{3,1},{4,6},{5,7},{6,4},{7,5},{8,10},{9,11},{10,... | collective-permute-start | bytes 387080 | tf_op jit(solution)/shard_map/ppermute | solution.py:217
  24.9 1.3 %collective-permute-start.3 = (bf16[72,896]{1,0:T(8,128)(2,1)S(1)}, bf16[72,896]{1,0:T(8,128)(2,1)S(1)}, u32[]{:S(2)}, u32[]{:S(2)}) collective-permute-start(bf16[72,896]{1,0:T(8,128)(2,1)S(1)} %get-tuple-element.36), channel_id=1, source_target_pairs={{0,2},{1,3},{2,0},{3,1},{4,6},{5,7},{6,4},{7,5},{8,10},{9,11},{10,... | collective-permute-start | bytes 387080 | tf_op jit(solution)/shard_map/ppermute | solution.py:217
  26.2 0.7 %collective-permute-start.2 = (bf16[72,768]{1,0:T(8,128)(2,1)S(1)}, bf16[72,768]{1,0:T(8,128)(2,1)S(1)}, u32[]{:S(2)}, u32[]{:S(2)}) collective-permute-start(bf16[72,768]{1,0:T(8,128)(2,1)S(1)} %get-tuple-element.35), channel_id=1, source_target_pairs={{0,2},{1,3},{2,0},{3,1},{4,6},{5,7},{6,4},{7,5},{8,10},{9,11},{10,... | collective-permute-start | bytes 331784 | tf_op jit(solution)/shard_map/ppermute | solution.py:217
  26.9 0.0 collective-permute-done.6.early_other
  26.9 1.2 %shard_map.59 = (bf16[96,3072]{1,0:T(8,128)(2,1)S(1)}, bf16[24,3072]{1,0:T(8,128)(2,1)S(1)}) custom-call(bf16[96,3200]{1,0:T(8,128)(2,1)S(1)} %all_gather.3.own_ref.in_ref, bf16[96,3200]{1,0:T(8,128)(2,1)S(1)} %collective-permute-done.1.near_ref, bf16[24,3200]{1,0:T(8,128)(2,1)S(1)} %collective-permute-done.early_ref, ...), custom_call_target="tpu_custom_call" | custom-call | tf_op jit(solution)/shard_map/pallas_call | solution.py:38
  28.2 0.0 collective-permute-done.5.ref
  28.2 0.1 collective-permute-start.7
  28.3 0.5 shard_map.60.part_ref
  28.8 0.7 %collective-permute-done.7.other_ref = bf16[72,640]{1,0:T(8,128)(2,1)S(1)} collective-permute-done((bf16[72,640]{1,0:T(8,128)(2,1)S(1)}, bf16[72,640]{1,0:T(8,128)(2,1)S(1)}, u32[]{:S(2)}, u32[]{:S(2)}) %collective-permute-start.7) | collective-permute-done | bytes 92192 | tf_op jit(solution)/shard_map/ppermute | solution.py:217
  29.5 0.0 slice-done
  29.5 0.0 slice-done.1
  29.6 1.5 %shard_map.61 = (f32[192,2048]{1,0:T(8,128)S(1)}, f32[192,2048]{1,0:T(8,128)S(1)}) custom-call(bf16[72,640]{1,0:T(8,128)(2,1)S(1)} %collective-permute-done.7.other_ref, bf16[72,512]{1,0:T(8,128)(2,1)S(1)} %shard_map.60.part_ref, bf16[96,3072]{1,0:T(8,128)(2,1)S(1)} %get-tuple-element.45.stay_ref, bf16[24,3072]{1,0:T(8,128)(2,1)S(1)} %get-tuple-element.46.early_ref, ...), custom_call_target="tpu_custom_call" | custom-call | tf_op jit(solution)/shard_map/pallas_call | solution.py:38
  31.1 0.0 collective-permute-done.4.far_ref
  31.1 1.9 %shard_map.62 = (f32[192,2048]{1,0:T(8,128)S(1)}, f32[192,2048]{1,0:T(8,128)S(1)}) custom-call(bf16[72,896]{1,0:T(8,128)(2,1)S(1)} %collective-permute-done.4.far_ref, bf16[96,3072]{1,0:T(8,128)(2,1)S(1)} %get-tuple-element.45.stay_ref, bf16[24,3072]{1,0:T(8,128)(2,1)S(1)} %get-tuple-element.46.early_ref, f32[192,2048]{1,0:T(8,128)S(1)} %get-tuple-element.49.gate_in, ...), custom_call_target="tpu_custom_call" | custom-call | tf_op jit(solution)/shard_map/pallas_call | solution.py:38
  32.9 0.3 collective-permute-done.3.far_ref
  33.3 1.8 %shard_map.63 = (f32[192,2048]{1,0:T(8,128)S(1)}, f32[192,2048]{1,0:T(8,128)S(1)}) custom-call(bf16[72,896]{1,0:T(8,128)(2,1)S(1)} %collective-permute-done.3.far_ref, bf16[96,3072]{1,0:T(8,128)(2,1)S(1)} %get-tuple-element.45.stay_ref, bf16[24,3072]{1,0:T(8,128)(2,1)S(1)} %get-tuple-element.46.early_ref, f32[192,2048]{1,0:T(8,128)S(1)} %get-tuple-element.53.gate_in, ...), custom_call_target="tpu_custom_call" | custom-call | tf_op jit(solution)/shard_map/pallas_call | solution.py:38
  35.1 0.0 collective-permute-done.2.far_ref
  35.1 2.6 %shard_map.64 = bf16[16,48,512]{2,1,0:T(8,128)(2,1)} custom-call(bf16[72,768]{1,0:T(8,128)(2,1)S(1)} %collective-permute-done.2.far_ref, bf16[96,3072]{1,0:T(8,128)(2,1)S(1)} %get-tuple-element.45.stay_ref, bf16[24,3072]{1,0:T(8,128)(2,1)S(1)} %get-tuple-element.46.early_ref, f32[192,2048]{1,0:T(8,128)S(1)} %get-tuple-element.57.gate_in, ...), custom_call_target="tpu_custom_call" | custom-call | tf_op jit(solution)/shard_map/pallas_call | solution.py:38
  37.7 5.4 %all-to-all-start = ((bf16[16,48,512]{2,1,0:T(8,128)(2,1)}), bf16[16,48,512]{2,1,0:T(8,128)(2,1)S(1)}, u32[]{:S(2)}, u32[]{:S(2)}) async-start(bf16[16,48,512]{2,1,0:T(8,128)(2,1)} %shard_map.64), calls=%async_computation | async-start | bytes 1572864 | tf_op jit(solution)/shard_map/all_to_all | solution.py:34
  43.2 0.4 shard_map.55
  43.6 18.2 %all-to-all-done.recv_ref = bf16[16,48,512]{2,1,0:T(8,128)(2,1)S(1)} async-done(((bf16[16,48,512]{2,1,0:T(8,128)(2,1)}), bf16[16,48,512]{2,1,0:T(8,128)(2,1)S(1)}, u32[]{:S(2)}, u32[]{:S(2)}) %all-to-all-start) | async-done | bytes 786464 | tf_op jit(solution)/shard_map/all_to_all | solution.py:34
  61.9 1.3 %shard_map.65 = bf16[24,2,8192]{2,1,0:T(2,128)(2,1)} custom-call(bf16[192,192]{1,0:T(8,128)(2,1)S(1)} %get-tuple-element.32.picks_ref, f32[48,128]{1,0:T(8,128)S(1)} %get-tuple-element.33.column_ref, bf16[16,48,512]{2,1,0:T(8,128)(2,1)S(1)} %all-to-all-done.recv_ref), custom_call_target="tpu_custom_call" | custom-call | bytes 1572864 | tf_op jit(solution)/shard_map/pallas_call | solution.py:38
  (11 shorter events, 0.0 us)
Async XLA Ops:
  0.0 29.5 %slice-start = ((s8[12582912]{0:T(1024)(128)(4,1)}), s8[4194304]{0:T(1024)(128)(4,1)S(1)}, s32[]{:S(2)}) async-start(s8[12582912]{0:T(1024)(128)(4,1)} %bitcast.2), calls=%async_computation.1 | async-start | bytes 8388608
  0.0 29.5 %slice-start.1 = ((s8[12582912]{0:T(1024)(128)(4,1)}), s8[4194304]{0:T(1024)(128)(4,1)S(1)}, s32[]{:S(2)}) async-start(s8[12582912]{0:T(1024)(128)(4,1)} %bitcast.2), calls=%async_computation.2 | async-start | bytes 8388608
  0.0 29.5 %slice-start.2 = ((s8[12582912]{0:T(1024)(128)(4,1)}), s8[4194304]{0:T(1024)(128)(4,1)S(1)}, s32[]{:S(2)}) async-start(s8[12582912]{0:T(1024)(128)(4,1)} %bitcast.2), calls=%async_computation.3 | async-start | bytes 8388608
  0.0 29.5 %copy-start = (bf16[1,3072,2048]{2,1,0:T(8,128)(2,1)S(1)}, bf16[1,3072,2048]{2,1,0:T(8,128)(2,1)}, u32[]{:S(2)}) copy-start(bf16[1,3072,2048]{2,1,0:T(8,128)(2,1)} %up_all.7) | copy-start | bytes 37748740
  1.1 20.2 %collective-permute-start = (bf16[24,3200]{1,0:T(8,128)(2,1)S(1)}, bf16[24,3200]{1,0:T(8,128)(2,1)S(1)}, u32[]{:S(2)}, u32[]{:S(2)}) collective-permute-start(bf16[24,3200]{1,0:T(8,128)(2,1)S(1)} %shard_map.56), channel_id=1, source_target_pairs={{0,2},{1,3},{2,0},{3,1},{4,6},{5,7},{6,4},{7,5},{8,10},{9,11},{10,... | collective-permute-start | bytes 460808 | tf_op jit(solution)/shard_map/ppermute | solution.py:217
  21.3 2.0 %collective-permute-start.1 = (bf16[96,3200]{1,0:T(8,128)(2,1)S(1)}, bf16[96,3200]{1,0:T(8,128)(2,1)S(1)}, u32[]{:S(2)}, u32[]{:S(2)}) collective-permute-start(bf16[96,3200]{1,0:T(8,128)(2,1)S(1)} %all_gather.3.own_ref.in_ref), channel_id=1, source_target_pairs={{0,1},{1,0},{2,3},{3,2},{4,5},{5,4},{6,7},{7,6},{8,9},{9,8},{10,11... | collective-permute-start | bytes 1843208 | tf_op jit(solution)/shard_map/ppermute | solution.py:217
  21.3 5.6 %collective-permute-start.6 = (bf16[24,3200]{1,0:T(8,128)(2,1)S(1)}, bf16[24,3200]{1,0:T(8,128)(2,1)S(1)}, u32[]{:S(2)}, u32[]{:S(2)}) collective-permute-start(bf16[24,3200]{1,0:T(8,128)(2,1)S(1)} %collective-permute-done.early_ref), channel_id=1, source_target_pairs={{0,1},{1,0},{2,3},{3,2},{4,5},{5,4},{6,7},{7,6},{8,9},{9,8},{10,11... | collective-permute-start | bytes 460808 | tf_op jit(solution)/shard_map/ppermute | solution.py:217
  22.0 6.2 %collective-permute-start.5 = (bf16[72,640]{1,0:T(8,128)(2,1)S(1)}, bf16[72,640]{1,0:T(8,128)(2,1)S(1)}, u32[]{:S(2)}, u32[]{:S(2)}) collective-permute-start(bf16[72,640]{1,0:T(8,128)(2,1)S(1)} %shard_map.58), channel_id=1, source_target_pairs={{0,2},{1,3},{2,0},{3,1},{4,6},{5,7},{6,4},{7,5},{8,10},{9,11},{10,... | collective-permute-start | bytes 276488 | tf_op jit(solution)/shard_map/ppermute | solution.py:217
  24.1 7.0 %collective-permute-start.4 = (bf16[72,896]{1,0:T(8,128)(2,1)S(1)}, bf16[72,896]{1,0:T(8,128)(2,1)S(1)}, u32[]{:S(2)}, u32[]{:S(2)}) collective-permute-start(bf16[72,896]{1,0:T(8,128)(2,1)S(1)} %get-tuple-element.37), channel_id=1, source_target_pairs={{0,2},{1,3},{2,0},{3,1},{4,6},{5,7},{6,4},{7,5},{8,10},{9,11},{10,... | collective-permute-start | bytes 387080 | tf_op jit(solution)/shard_map/ppermute | solution.py:217
  24.9 8.4 %collective-permute-start.3 = (bf16[72,896]{1,0:T(8,128)(2,1)S(1)}, bf16[72,896]{1,0:T(8,128)(2,1)S(1)}, u32[]{:S(2)}, u32[]{:S(2)}) collective-permute-start(bf16[72,896]{1,0:T(8,128)(2,1)S(1)} %get-tuple-element.36), channel_id=1, source_target_pairs={{0,2},{1,3},{2,0},{3,1},{4,6},{5,7},{6,4},{7,5},{8,10},{9,11},{10,... | collective-permute-start | bytes 387080 | tf_op jit(solution)/shard_map/ppermute | solution.py:217
  26.2 8.9 %collective-permute-start.2 = (bf16[72,768]{1,0:T(8,128)(2,1)S(1)}, bf16[72,768]{1,0:T(8,128)(2,1)S(1)}, u32[]{:S(2)}, u32[]{:S(2)}) collective-permute-start(bf16[72,768]{1,0:T(8,128)(2,1)S(1)} %get-tuple-element.35), channel_id=1, source_target_pairs={{0,2},{1,3},{2,0},{3,1},{4,6},{5,7},{6,4},{7,5},{8,10},{9,11},{10,... | collective-permute-start | bytes 331784 | tf_op jit(solution)/shard_map/ppermute | solution.py:217
  28.2 1.4 %collective-permute-start.7 = (bf16[72,640]{1,0:T(8,128)(2,1)S(1)}, bf16[72,640]{1,0:T(8,128)(2,1)S(1)}, u32[]{:S(2)}, u32[]{:S(2)}) collective-permute-start(bf16[72,640]{1,0:T(8,128)(2,1)S(1)} %collective-permute-done.5.ref), channel_id=1, source_target_pairs={{0,1},{1,0},{2,3},{3,2},{4,5},{5,4},{6,7},{7,6},{8,9},{9,8},{10,11... | collective-permute-start | bytes 276488 | tf_op jit(solution)/shard_map/ppermute | solution.py:217
  37.7 5.4 %copy-start.1 = (s32[24,2]{0,1:T(2,128)S(1)}, s32[24,2]{0,1:T(2,128)}, u32[]{:S(2)}) copy-start(s32[24,2]{0,1:T(2,128)} %param.6) | copy-start | bytes 580
  37.7 5.4 %copy-start.2 = (f32[24,2]{0,1:T(2,128)S(1)}, f32[24,2]{0,1:T(2,128)}, u32[]{:S(2)}) copy-start(f32[24,2]{0,1:T(2,128)} %param.7) | copy-start | bytes 580
  37.7 24.1 %all-to-all-start = ((bf16[16,48,512]{2,1,0:T(8,128)(2,1)}), bf16[16,48,512]{2,1,0:T(8,128)(2,1)S(1)}, u32[]{:S(2)}, u32[]{:S(2)}) async-start(bf16[16,48,512]{2,1,0:T(8,128)(2,1)} %shard_map.64), calls=%async_computation | async-start | bytes 1572864 | tf_op jit(solution)/shard_map/all_to_all | solution.py:34

commit v15 on v14

--- a/solution.py
+++ b/solution.py
@@ -238,10 +238,9 @@
     kernel = functools.partial(stay_kernel, tok_rows, capacity)
     outs = [array(half, width), array(2 * capacity, width)]
     stay, first = local_kernel(kernel, outs, (own, near, early, early_other))
-    far, stay = lax.optimization_barrier((far, stay))
     far_other = swap(far, 1)
     far_part = local_kernel(functools.partial(pick_kernel, tok_rows, capacity), array(rest, cut), (far,))
-    far_other, far_part = lax.optimization_barrier((far_other, far_part))
+    far_other, far_part, stay = lax.optimization_barrier((far_other, far_part, stay))
 
     def sums(kernel, blocks, span):
         out_shape = [jax.ShapeDtypeStruct((rows, units), jnp.float32)] * 2
@@ -286,11 +285,12 @@
         picks_ref[fold * both : (fold + 1) * both, :] = (lane == target + fold * capacity).astype(picks_ref.dtype)
 
 
-def final_kernel(experts, folds, picks_ref, column_ref, recv_ref, out_ref):
+def final_kernel(experts, folds, picks_ref, column_ref, recv_ref, out_hbm, out_ref, sems):
     tok_rows = out_ref.shape[0]
     both = 2 * tok_rows
     peers, tall, span = recv_ref.shape
     column = column_ref[:, 0:1]
+    copies = []
     for part in range(peers // experts):
         block = recv_ref[part * experts : (part + 1) * experts].reshape(experts * tall, span)
         rows = exact_dot(picks_ref[...], block)
@@ -298,6 +298,12 @@
             scaled = rows[fold * both : (fold + 1) * both] * column
             start = (part * folds + fold) * span
             out_ref[:, :, start : start + span] = scaled.astype(out_ref.dtype).reshape(tok_rows, 2, span)
+        columns = slice(part * folds * span, (part + 1) * folds * span)
+        copy = pltpu.make_async_copy(out_ref.at[:, :, columns], out_hbm.at[:, :, columns], sems.at[part])
+        copy.start()
+        copies.append(copy)
+    for copy in copies:
+        copy.wait()
 
 
 def finish(expert_ids, gate_weights, received, experts, folds):
@@ -315,12 +321,14 @@
         moved=1 << 20,
     )
     units = peers // experts * folds * span
-    return local_kernel(
+    return pl.pallas_call(
         functools.partial(final_kernel, experts, folds),
-        jax.ShapeDtypeStruct((tok_rows, 2, units), kind),
-        (picks, column, received),
-        moved=4 * received.size,
-    )
+        out_shape=jax.ShapeDtypeStruct((tok_rows, 2, units), kind),
+        in_specs=[WHOLE] * 3,
+        out_specs=OUTSIDE,
+        scratch_shapes=[pltpu.VMEM((tok_rows, 2, units), kind), pltpu.SemaphoreType.DMA((peers // experts,))],
+        compiler_params=pltpu.CompilerParams(vmem_limit_bytes=12 << 20),
+    )(picks, column, received)
 
 
 def body(tokens, expert_ids, gate_weights, w_gate, w_up):

time: 63.4 us -> 62.8 us (level)
  starting transfers between devices: 12.5 us -> 11.4 us
    pallas_call x11 -> x10, Pallas kernels: 13.3 us -> 12 us  [local_kernel(): pl.pallas_call(kernel, out_shape=out_shape, in_specs=[WHOLE] * len(args)...]
    pallas_call x0 -> x1, Pallas kernels: none -> 1.12 us  [finish(): pl.pallas_call(functools.partial(final_kernel, experts, folds), out_shape...]
where the time goes in v15:
time: 62.8 us; the launch traced here: 62.5 us
  waiting for transfers between devices  20.6 us (33%)
  blocking collectives  17.1 us (27%)
  Pallas kernels  13.1 us (21%)
  starting transfers between devices  11.4 us (18%)
    all_to_all x1, waiting for transfers between devices, exchange(): lax.all_to_all(blocks, ('et', 'ep'), split_axis=0, concat_axis=0, tiled=T...  18.2 us
    all_gather x1, blocking collectives, routed_by_columns(): own = lax.all_gather(packed, 'et', axis=0, tiled=True)  17.1 us
    pallas_call x10, Pallas kernels, local_kernel(): pl.pallas_call(kernel, out_shape=out_shape, in_specs=[WHOLE] * len(args)...  12 us
    ppermute x8, starting transfers between devices, swap(): return lax.ppermute(block, 'ep', [(i, i ^ bit) for i in range(experts)])  6.48 us
    all_to_all x1, starting transfers between devices, exchange(): lax.all_to_all(blocks, ('et', 'ep'), split_axis=0, concat_axis=0, tiled=T...  4.97 us
    ppermute x8, waiting for transfers between devices, swap(): return lax.ppermute(block, 'ep', [(i, i ^ bit) for i in range(experts)])  2.33 us
  transfers between devices with their start and end apart: 9, of which 4 were waited for; matrix products, arithmetic and copies ran while one was open for 0% of the time, Pallas kernels for 13%

profile of v15, /device:TPU:0, one launch (start us, length us, event | category | flops | bytes accessed | tf_op | source)
XLA Modules:
  0.0 62.5 jit_solution(16229680768550688024)
XLA Ops:
  0.0 1.1 %shard_map.56 = bf16[24,3200]{1,0:T(8,128)(2,1)S(1)} custom-call(s32[2,24]{1,0:T(2,128)} %bitcast.4, bf16[24,3072]{1,0:T(8,128)(2,1)} %tokens_hbm.1, bf16[1,3072,2048]{2,1,0:T(8,128)(2,1)} %gate_all.7, bf16[1,3072,2048]{2,1,0:T(8,128)(2,1)} %up_all.7), custom_call_target="tpu_custom_call" | custom-call | tf_op jit(solution)/shard_map/pallas_call | solution.py:38
  1.1 3.0 %collective-permute-start = (bf16[24,3200]{1,0:T(8,128)(2,1)S(1)}, bf16[24,3200]{1,0:T(8,128)(2,1)S(1)}, u32[]{:S(2)}, u32[]{:S(2)}) collective-permute-start(bf16[24,3200]{1,0:T(8,128)(2,1)S(1)} %shard_map.56), channel_id=1, source_target_pairs={{0,2},{1,3},{2,0},{3,1},{4,6},{5,7},{6,4},{7,5},{8,10},{9,11},{10,... | collective-permute-start | bytes 460808 | tf_op jit(solution)/shard_map/ppermute | solution.py:217
  4.1 17.1 %all_gather.3.own_ref.in_ref = bf16[96,3200]{1,0:T(8,128)(2,1)S(1)} all-gather(bf16[24,3200]{1,0:T(8,128)(2,1)S(1)} %shard_map.56), channel_id=1, replica_groups=mesh['groups'=2,'et'=4,'ep'=4] {'et'}, dimensions={0}, use_global_device_ids=true | all-gather | bytes 768000 | tf_op jit(solution)/shard_map/all_gather | solution.py:227
  21.3 0.0 collective-permute-done.early_ref
  21.3 0.0 collective-permute-start.1
  21.3 0.2 shard_map.58
  21.5 0.6 collective-permute-start.5
  22.1 0.2 collective-permute-start.7
  22.3 1.0 %collective-permute-done.1.near_ref = bf16[96,3200]{1,0:T(8,128)(2,1)S(1)} collective-permute-done((bf16[96,3200]{1,0:T(8,128)(2,1)S(1)}, bf16[96,3200]{1,0:T(8,128)(2,1)S(1)}, u32[]{:S(2)}, u32[]{:S(2)}) %collective-permute-start.1) | collective-permute-done | bytes 614432 | tf_op jit(solution)/shard_map/ppermute | solution.py:217
  23.3 0.8 %shard_map.57 = (bf16[72,896]{1,0:T(8,128)(2,1)S(1)}, bf16[72,896]{1,0:T(8,128)(2,1)S(1)}, bf16[72,768]{1,0:T(8,128)(2,1)S(1)}) custom-call(bf16[96,3200]{1,0:T(8,128)(2,1)S(1)} %all_gather.3.own_ref.in_ref, bf16[96,3200]{1,0:T(8,128)(2,1)S(1)} %collective-permute-done.1.near_ref), custom_call_target="tpu_custom_call" | custom-call | tf_op jit(solution)/shard_map/pallas_call | solution.py:38
  24.1 0.6 collective-permute-start.4
  24.7 1.5 %collective-permute-start.3 = (bf16[72,896]{1,0:T(8,128)(2,1)S(1)}, bf16[72,896]{1,0:T(8,128)(2,1)S(1)}, u32[]{:S(2)}, u32[]{:S(2)}) collective-permute-start(bf16[72,896]{1,0:T(8,128)(2,1)S(1)} %get-tuple-element.35), channel_id=1, source_target_pairs={{0,2},{1,3},{2,0},{3,1},{4,6},{5,7},{6,4},{7,5},{8,10},{9,11},{10,... | collective-permute-start | bytes 387080 | tf_op jit(solution)/shard_map/ppermute | solution.py:217
  26.2 0.5 collective-permute-start.2
  26.7 0.0 collective-permute-done.5.ref
  26.7 0.0 collective-permute-start.6
  26.7 0.5 shard_map.59.part_ref
  27.3 0.0 collective-permute-done.7.early_other
  27.3 1.2 %shard_map.60 = (bf16[96,3072]{1,0:T(8,128)(2,1)S(1)}, bf16[24,3072]{1,0:T(8,128)(2,1)S(1)}) custom-call(bf16[96,3200]{1,0:T(8,128)(2,1)S(1)} %all_gather.3.own_ref.in_ref, bf16[96,3200]{1,0:T(8,128)(2,1)S(1)} %collective-permute-done.1.near_ref, bf16[24,3200]{1,0:T(8,128)(2,1)S(1)} %collective-permute-done.early_ref, ...), custom_call_target="tpu_custom_call" | custom-call | tf_op jit(solution)/shard_map/pallas_call | solution.py:38
  28.5 0.0 collective-permute-done.6.other_ref
  28.5 0.0 slice-done
  28.5 0.0 slice-done.1
  28.6 1.5 %shard_map.61 = (f32[192,2048]{1,0:T(8,128)S(1)}, f32[192,2048]{1,0:T(8,128)S(1)}) custom-call(bf16[72,640]{1,0:T(8,128)(2,1)S(1)} %collective-permute-done.6.other_ref, bf16[72,512]{1,0:T(8,128)(2,1)S(1)} %shard_map.59.part_ref, bf16[96,3072]{1,0:T(8,128)(2,1)S(1)} %get-tuple-element.43.stay_ref, bf16[24,3072]{1,0:T(8,128)(2,1)S(1)} %get-tuple-element.44.early_ref, ...), custom_call_target="tpu_custom_call" | custom-call | tf_op jit(solution)/shard_map/pallas_call | solution.py:38
  30.1 0.4 collective-permute-done.4.far_ref
  30.5 1.8 %shard_map.62 = (f32[192,2048]{1,0:T(8,128)S(1)}, f32[192,2048]{1,0:T(8,128)S(1)}) custom-call(bf16[72,896]{1,0:T(8,128)(2,1)S(1)} %collective-permute-done.4.far_ref, bf16[96,3072]{1,0:T(8,128)(2,1)S(1)} %get-tuple-element.43.stay_ref, bf16[24,3072]{1,0:T(8,128)(2,1)S(1)} %get-tuple-element.44.early_ref, f32[192,2048]{1,0:T(8,128)S(1)} %get-tuple-element.47.gate_in, ...), custom_call_target="tpu_custom_call" | custom-call | tf_op jit(solution)/shard_map/pallas_call | solution.py:38
  32.3 0.9 %collective-permute-done.3.far_ref = bf16[72,896]{1,0:T(8,128)(2,1)S(1)} collective-permute-done((bf16[72,896]{1,0:T(8,128)(2,1)S(1)}, bf16[72,896]{1,0:T(8,128)(2,1)S(1)}, u32[]{:S(2)}, u32[]{:S(2)}) %collective-permute-start.3) | collective-permute-done | bytes 129056 | tf_op jit(solution)/shard_map/ppermute | solution.py:217
  33.2 1.8 %shard_map.63 = (f32[192,2048]{1,0:T(8,128)S(1)}, f32[192,2048]{1,0:T(8,128)S(1)}) custom-call(bf16[72,896]{1,0:T(8,128)(2,1)S(1)} %collective-permute-done.3.far_ref, bf16[96,3072]{1,0:T(8,128)(2,1)S(1)} %get-tuple-element.43.stay_ref, bf16[24,3072]{1,0:T(8,128)(2,1)S(1)} %get-tuple-element.44.early_ref, f32[192,2048]{1,0:T(8,128)S(1)} %get-tuple-element.51.gate_in, ...), custom_call_target="tpu_custom_call" | custom-call | tf_op jit(solution)/shard_map/pallas_call | solution.py:38
  35.1 0.0 collective-permute-done.2.far_ref
  35.1 2.6 %shard_map.64 = bf16[16,48,512]{2,1,0:T(8,128)(2,1)} custom-call(bf16[72,768]{1,0:T(8,128)(2,1)S(1)} %collective-permute-done.2.far_ref, bf16[96,3072]{1,0:T(8,128)(2,1)S(1)} %get-tuple-element.43.stay_ref, bf16[24,3072]{1,0:T(8,128)(2,1)S(1)} %get-tuple-element.44.early_ref, f32[192,2048]{1,0:T(8,128)S(1)} %get-tuple-element.55.gate_in, ...), custom_call_target="tpu_custom_call" | custom-call | tf_op jit(solution)/shard_map/pallas_call | solution.py:38
  37.7 5.0 %all-to-all-start = ((bf16[16,48,512]{2,1,0:T(8,128)(2,1)}), bf16[16,48,512]{2,1,0:T(8,128)(2,1)S(1)}, u32[]{:S(2)}, u32[]{:S(2)}) async-start(bf16[16,48,512]{2,1,0:T(8,128)(2,1)} %shard_map.64), calls=%async_computation | async-start | bytes 1572864 | tf_op jit(solution)/shard_map/all_to_all | solution.py:34
  42.7 0.4 shard_map.55
  43.1 18.2 %all-to-all-done.recv_ref = bf16[16,48,512]{2,1,0:T(8,128)(2,1)S(1)} async-done(((bf16[16,48,512]{2,1,0:T(8,128)(2,1)}), bf16[16,48,512]{2,1,0:T(8,128)(2,1)S(1)}, u32[]{:S(2)}, u32[]{:S(2)}) %all-to-all-start) | async-done | bytes 786464 | tf_op jit(solution)/shard_map/all_to_all | solution.py:34
  61.4 1.1 %shard_map.65 = bf16[24,2,8192]{2,1,0:T(2,128)(2,1)} custom-call(bf16[192,192]{1,0:T(8,128)(2,1)S(1)} %get-tuple-element.31.picks_ref, f32[48,128]{1,0:T(8,128)S(1)} %get-tuple-element.32.column_ref, bf16[16,48,512]{2,1,0:T(8,128)(2,1)S(1)} %all-to-all-done.recv_ref), custom_call_target="tpu_custom_call" | custom-call | tf_op jit(solution)/shard_map/pallas_call | solution.py:324
  (11 shorter events, 0.0 us)
Async XLA Ops:
  0.0 28.5 %slice-start = ((s8[12582912]{0:T(1024)(128)(4,1)}), s8[4194304]{0:T(1024)(128)(4,1)S(1)}, s32[]{:S(2)}) async-start(s8[12582912]{0:T(1024)(128)(4,1)} %bitcast.2), calls=%async_computation.1 | async-start | bytes 8388608
  0.0 28.5 %slice-start.1 = ((s8[12582912]{0:T(1024)(128)(4,1)}), s8[4194304]{0:T(1024)(128)(4,1)S(1)}, s32[]{:S(2)}) async-start(s8[12582912]{0:T(1024)(128)(4,1)} %bitcast.2), calls=%async_computation.2 | async-start | bytes 8388608
  0.0 28.5 %slice-start.2 = ((s8[12582912]{0:T(1024)(128)(4,1)}), s8[4194304]{0:T(1024)(128)(4,1)S(1)}, s32[]{:S(2)}) async-start(s8[12582912]{0:T(1024)(128)(4,1)} %bitcast.2), calls=%async_computation.3 | async-start | bytes 8388608
  0.0 28.5 %copy-start = (bf16[1,3072,2048]{2,1,0:T(8,128)(2,1)S(1)}, bf16[1,3072,2048]{2,1,0:T(8,128)(2,1)}, u32[]{:S(2)}) copy-start(bf16[1,3072,2048]{2,1,0:T(8,128)(2,1)} %up_all.7) | copy-start | bytes 37748740
  1.1 20.2 %collective-permute-start = (bf16[24,3200]{1,0:T(8,128)(2,1)S(1)}, bf16[24,3200]{1,0:T(8,128)(2,1)S(1)}, u32[]{:S(2)}, u32[]{:S(2)}) collective-permute-start(bf16[24,3200]{1,0:T(8,128)(2,1)S(1)} %shard_map.56), channel_id=1, source_target_pairs={{0,2},{1,3},{2,0},{3,1},{4,6},{5,7},{6,4},{7,5},{8,10},{9,11},{10,... | collective-permute-start | bytes 460808 | tf_op jit(solution)/shard_map/ppermute | solution.py:217
  21.3 2.0 %collective-permute-start.1 = (bf16[96,3200]{1,0:T(8,128)(2,1)S(1)}, bf16[96,3200]{1,0:T(8,128)(2,1)S(1)}, u32[]{:S(2)}, u32[]{:S(2)}) collective-permute-start(bf16[96,3200]{1,0:T(8,128)(2,1)S(1)} %all_gather.3.own_ref.in_ref), channel_id=1, source_target_pairs={{0,1},{1,0},{2,3},{3,2},{4,5},{5,4},{6,7},{7,6},{8,9},{9,8},{10,11... | collective-permute-start | bytes 1843208 | tf_op jit(solution)/shard_map/ppermute | solution.py:217
  21.5 5.3 %collective-permute-start.5 = (bf16[72,640]{1,0:T(8,128)(2,1)S(1)}, bf16[72,640]{1,0:T(8,128)(2,1)S(1)}, u32[]{:S(2)}, u32[]{:S(2)}) collective-permute-start(bf16[72,640]{1,0:T(8,128)(2,1)S(1)} %shard_map.58), channel_id=1, source_target_pairs={{0,2},{1,3},{2,0},{3,1},{4,6},{5,7},{6,4},{7,5},{8,10},{9,11},{10,... | collective-permute-start | bytes 276488 | tf_op jit(solution)/shard_map/ppermute | solution.py:217
  22.1 5.2 %collective-permute-start.7 = (bf16[24,3200]{1,0:T(8,128)(2,1)S(1)}, bf16[24,3200]{1,0:T(8,128)(2,1)S(1)}, u32[]{:S(2)}, u32[]{:S(2)}) collective-permute-start(bf16[24,3200]{1,0:T(8,128)(2,1)S(1)} %collective-permute-done.early_ref), channel_id=1, source_target_pairs={{0,1},{1,0},{2,3},{3,2},{4,5},{5,4},{6,7},{7,6},{8,9},{9,8},{10,11... | collective-permute-start | bytes 460808 | tf_op jit(solution)/shard_map/ppermute | solution.py:217
  24.1 6.4 %collective-permute-start.4 = (bf16[72,896]{1,0:T(8,128)(2,1)S(1)}, bf16[72,896]{1,0:T(8,128)(2,1)S(1)}, u32[]{:S(2)}, u32[]{:S(2)}) collective-permute-start(bf16[72,896]{1,0:T(8,128)(2,1)S(1)} %get-tuple-element.36), channel_id=1, source_target_pairs={{0,2},{1,3},{2,0},{3,1},{4,6},{5,7},{6,4},{7,5},{8,10},{9,11},{10,... | collective-permute-start | bytes 387080 | tf_op jit(solution)/shard_map/ppermute | solution.py:217
  24.7 8.5 %collective-permute-start.3 = (bf16[72,896]{1,0:T(8,128)(2,1)S(1)}, bf16[72,896]{1,0:T(8,128)(2,1)S(1)}, u32[]{:S(2)}, u32[]{:S(2)}) collective-permute-start(bf16[72,896]{1,0:T(8,128)(2,1)S(1)} %get-tuple-element.35), channel_id=1, source_target_pairs={{0,2},{1,3},{2,0},{3,1},{4,6},{5,7},{6,4},{7,5},{8,10},{9,11},{10,... | collective-permute-start | bytes 387080 | tf_op jit(solution)/shard_map/ppermute | solution.py:217
  26.2 8.9 %collective-permute-start.2 = (bf16[72,768]{1,0:T(8,128)(2,1)S(1)}, bf16[72,768]{1,0:T(8,128)(2,1)S(1)}, u32[]{:S(2)}, u32[]{:S(2)}) collective-permute-start(bf16[72,768]{1,0:T(8,128)(2,1)S(1)} %get-tuple-element.34), channel_id=1, source_target_pairs={{0,2},{1,3},{2,0},{3,1},{4,6},{5,7},{6,4},{7,5},{8,10},{9,11},{10,... | collective-permute-start | bytes 331784 | tf_op jit(solution)/shard_map/ppermute | solution.py:217
  26.7 1.8 %collective-permute-start.6 = (bf16[72,640]{1,0:T(8,128)(2,1)S(1)}, bf16[72,640]{1,0:T(8,128)(2,1)S(1)}, u32[]{:S(2)}, u32[]{:S(2)}) collective-permute-start(bf16[72,640]{1,0:T(8,128)(2,1)S(1)} %collective-permute-done.5.ref), channel_id=1, source_target_pairs={{0,1},{1,0},{2,3},{3,2},{4,5},{5,4},{6,7},{7,6},{8,9},{9,8},{10,11... | collective-permute-start | bytes 276488 | tf_op jit(solution)/shard_map/ppermute | solution.py:217
  37.7 5.0 %copy-start.1 = (s32[24,2]{0,1:T(2,128)S(1)}, s32[24,2]{0,1:T(2,128)}, u32[]{:S(2)}) copy-start(s32[24,2]{0,1:T(2,128)} %param.6) | copy-start | bytes 580
  37.7 5.0 %copy-start.2 = (f32[24,2]{0,1:T(2,128)S(1)}, f32[24,2]{0,1:T(2,128)}, u32[]{:S(2)}) copy-start(f32[24,2]{0,1:T(2,128)} %param.7) | copy-start | bytes 580
  37.7 23.7 %all-to-all-start = ((bf16[16,48,512]{2,1,0:T(8,128)(2,1)}), bf16[16,48,512]{2,1,0:T(8,128)(2,1)S(1)}, u32[]{:S(2)}, u32[]{:S(2)}) async-start(bf16[16,48,512]{2,1,0:T(8,128)(2,1)} %shard_map.64), calls=%async_computation | async-start | bytes 1572864 | tf_op jit(solution)/shard_map/all_to_all | solution.py:34

commit v16 on v15

--- a/solution.py
+++ b/solution.py
@@ -112,7 +112,7 @@
     out_ref[...] = exact_dot(move, in_ref[:, : out_ref.shape[1]]).astype(out_ref.dtype)
 
 
-def select_kernel(tok_rows, capacity, own_ref, near_ref, *outs):
+def select_kernel(tok_rows, capacity, start, own_ref, near_ref, *outs):
     expert, core = lax.axis_index("ep") ^ 2, lax.axis_index("ep") % 2
     rows = outs[0].shape[0]
     group = (layer_of(own_ref, tok_rows) ^ lax.axis_index("et")) - 1
@@ -120,7 +120,7 @@
         (rows_of(ref[:, :128], group, source, expert, rows, tok_rows, capacity), ref)
         for ref, source in ((own_ref, core), (near_ref, 1 - core))
     ]
-    start = own_ref.shape[1] - sum(out.shape[1] for out in outs)
+    start = 128 + start
     for out in outs:
         stop = start + out.shape[1]
         out[...] = sum(transposed_dot(sel, ref[:, start:stop]) for sel, ref in found).astype(out.dtype)
@@ -230,9 +230,15 @@
     rest = half - 2 * capacity
     part = local_kernel(functools.partial(cut_kernel, tok_rows), array(others, 128 + cut), (own,))
     near, far, early_other = swap(own, 1), swap(part, 2), swap(early, 1)
-    kernel = functools.partial(select_kernel, tok_rows, capacity)
     ends = (*cuts[1:], width)
-    laters = local_kernel(kernel, [array(rest, stop - start) for start, stop in zip(cuts, ends)], (own, near))
+    spans = [array(rest, stop - start) for start, stop in zip(cuts, ends)]
+    laters = [
+        part
+        for low, high in ((0, 1), (1, len(cuts)))
+        for part in local_kernel(
+            functools.partial(select_kernel, tok_rows, capacity, cuts[low]), spans[low:high], (own, near)
+        )
+    ]
     later_fars = [swap(later, 2) for later in laters]
     own, near, *laters = lax.optimization_barrier((own, near, *laters))
     kernel = functools.partial(stay_kernel, tok_rows, capacity)

time: 62.8 us -> 63.2 us (level)
  waiting for transfers between devices: 20.6 us -> 19.8 us
  starting transfers between devices: 11.4 us -> 12.1 us
    ppermute x8, waiting for transfers between devices: 2.33 us -> 1.57 us  [swap(): return lax.ppermute(block, 'ep', [(i, i ^ bit) for i in range(experts)])]
    pallas_call x10 -> x11, Pallas kernels: 12 us -> 12.6 us  [local_kernel(): pl.pallas_call(kernel, out_shape=out_shape, in_specs=[WHOLE] * len(args)...]
  transfers between devices with their start and end apart: 9 -> 9, of which waited for: 4 -> 3; matrix products, arithmetic and copies ran while one was open for 0% -> 0% of each run, Pallas kernels for 13% -> 14%
where the time goes in v16:
time: 63.2 us; the launch traced here: 62.9 us
  waiting for transfers between devices  19.8 us (31%)
  blocking collectives  17.1 us (27%)
  Pallas kernels  13.7 us (22%)
  starting transfers between devices  12.1 us (19%)
    all_to_all x1, waiting for transfers between devices, exchange(): lax.all_to_all(blocks, ('et', 'ep'), split_axis=0, concat_axis=0, tiled=T...  18.2 us
    all_gather x1, blocking collectives, routed_by_columns(): own = lax.all_gather(packed, 'et', axis=0, tiled=True)  17.1 us
    pallas_call x11, Pallas kernels, local_kernel(): pl.pallas_call(kernel, out_shape=out_shape, in_specs=[WHOLE] * len(args)...  12.6 us
    ppermute x8, starting transfers between devices, swap(): return lax.ppermute(block, 'ep', [(i, i ^ bit) for i in range(experts)])  6.54 us
    all_to_all x1, starting transfers between devices, exchange(): lax.all_to_all(blocks, ('et', 'ep'), split_axis=0, concat_axis=0, tiled=T...  5.53 us
    ppermute x8, waiting for transfers between devices, swap(): return lax.ppermute(block, 'ep', [(i, i ^ bit) for i in range(experts)])  1.57 us
  transfers between devices with their start and end apart: 9, of which 3 were waited for; matrix products, arithmetic and copies ran while one was open for 0% of the time, Pallas kernels for 14%

profile of v16, /device:TPU:0, one launch (start us, length us, event | category | flops | bytes accessed | tf_op | source)
XLA Modules:
  0.0 62.9 jit_solution(7599082261081629644)
XLA Ops:
  0.0 1.1 %shard_map.56 = bf16[24,3200]{1,0:T(8,128)(2,1)S(1)} custom-call(s32[2,24]{1,0:T(2,128)} %bitcast.4, bf16[24,3072]{1,0:T(8,128)(2,1)} %tokens_hbm.1, bf16[1,3072,2048]{2,1,0:T(8,128)(2,1)} %gate_all.7, bf16[1,3072,2048]{2,1,0:T(8,128)(2,1)} %up_all.7), custom_call_target="tpu_custom_call" | custom-call | tf_op jit(solution)/shard_map/pallas_call | solution.py:38
  1.1 3.0 %collective-permute-start = (bf16[24,3200]{1,0:T(8,128)(2,1)S(1)}, bf16[24,3200]{1,0:T(8,128)(2,1)S(1)}, u32[]{:S(2)}, u32[]{:S(2)}) collective-permute-start(bf16[24,3200]{1,0:T(8,128)(2,1)S(1)} %shard_map.56), channel_id=1, source_target_pairs={{0,2},{1,3},{2,0},{3,1},{4,6},{5,7},{6,4},{7,5},{8,10},{9,11},{10,... | collective-permute-start | bytes 460808 | tf_op jit(solution)/shard_map/ppermute | solution.py:217
  4.1 17.1 %all_gather.3.own_ref.in_ref = bf16[96,3200]{1,0:T(8,128)(2,1)S(1)} all-gather(bf16[24,3200]{1,0:T(8,128)(2,1)S(1)} %shard_map.56), channel_id=1, replica_groups=mesh['groups'=2,'et'=4,'ep'=4] {'et'}, dimensions={0}, use_global_device_ids=true | all-gather | bytes 768000 | tf_op jit(solution)/shard_map/all_gather | solution.py:227
  21.3 0.0 collective-permute-done.early_ref
  21.3 0.0 collective-permute-start.1
  21.3 0.2 shard_map.59
  21.5 0.6 collective-permute-start.5
  22.1 0.2 collective-permute-start.7
  22.3 1.0 %collective-permute-done.1.near_ref = bf16[96,3200]{1,0:T(8,128)(2,1)S(1)} collective-permute-done((bf16[96,3200]{1,0:T(8,128)(2,1)S(1)}, bf16[96,3200]{1,0:T(8,128)(2,1)S(1)}, u32[]{:S(2)}, u32[]{:S(2)}) %collective-permute-start.1) | collective-permute-done | bytes 614432 | tf_op jit(solution)/shard_map/ppermute | solution.py:217
  23.3 0.7 %shard_map.58 = bf16[72,896]{1,0:T(8,128)(2,1)S(1)} custom-call(bf16[96,3200]{1,0:T(8,128)(2,1)S(1)} %all_gather.3.own_ref.in_ref, bf16[96,3200]{1,0:T(8,128)(2,1)S(1)} %collective-permute-done.1.near_ref), custom_call_target="tpu_custom_call" | custom-call | tf_op jit(solution)/shard_map/pallas_call | solution.py:38
  24.0 0.6 collective-permute-start.4
  24.6 0.7 %shard_map.57 = (bf16[72,896]{1,0:T(8,128)(2,1)S(1)}, bf16[72,768]{1,0:T(8,128)(2,1)S(1)}) custom-call(bf16[96,3200]{1,0:T(8,128)(2,1)S(1)} %all_gather.3.own_ref.in_ref, bf16[96,3200]{1,0:T(8,128)(2,1)S(1)} %collective-permute-done.1.near_ref), custom_call_target="tpu_custom_call" | custom-call | tf_op jit(solution)/shard_map/pallas_call | solution.py:38
  25.3 1.6 %collective-permute-start.3 = (bf16[72,896]{1,0:T(8,128)(2,1)S(1)}, bf16[72,896]{1,0:T(8,128)(2,1)S(1)}, u32[]{:S(2)}, u32[]{:S(2)}) collective-permute-start(bf16[72,896]{1,0:T(8,128)(2,1)S(1)} %get-tuple-element.34), channel_id=1, source_target_pairs={{0,2},{1,3},{2,0},{3,1},{4,6},{5,7},{6,4},{7,5},{8,10},{9,11},{10,... | collective-permute-start | bytes 387080 | tf_op jit(solution)/shard_map/ppermute | solution.py:217
  26.9 0.5 collective-permute-start.2
  27.4 0.0 collective-permute-done.5.ref
  27.4 0.0 collective-permute-start.6
  27.4 0.5 shard_map.60.part_ref
  27.9 0.0 collective-permute-done.7.early_other
  27.9 1.2 %shard_map.61 = (bf16[96,3072]{1,0:T(8,128)(2,1)S(1)}, bf16[24,3072]{1,0:T(8,128)(2,1)S(1)}) custom-call(bf16[96,3200]{1,0:T(8,128)(2,1)S(1)} %all_gather.3.own_ref.in_ref, bf16[96,3200]{1,0:T(8,128)(2,1)S(1)} %collective-permute-done.1.near_ref, bf16[24,3200]{1,0:T(8,128)(2,1)S(1)} %collective-permute-done.early_ref, ...), custom_call_target="tpu_custom_call" | custom-call | tf_op jit(solution)/shard_map/pallas_call | solution.py:38
  29.2 0.0 collective-permute-done.6.other_ref
  29.2 0.0 slice-done
  29.2 1.5 %shard_map.62 = (f32[192,2048]{1,0:T(8,128)S(1)}, f32[192,2048]{1,0:T(8,128)S(1)}) custom-call(bf16[72,640]{1,0:T(8,128)(2,1)S(1)} %collective-permute-done.6.other_ref, bf16[72,512]{1,0:T(8,128)(2,1)S(1)} %shard_map.60.part_ref, bf16[96,3072]{1,0:T(8,128)(2,1)S(1)} %get-tuple-element.41.stay_ref, bf16[24,3072]{1,0:T(8,128)(2,1)S(1)} %get-tuple-element.42.early_ref, ...), custom_call_target="tpu_custom_call" | custom-call | tf_op jit(solution)/shard_map/pallas_call | solution.py:38
  30.8 0.0 collective-permute-done.4.far_ref
  30.8 1.8 %shard_map.63 = (f32[192,2048]{1,0:T(8,128)S(1)}, f32[192,2048]{1,0:T(8,128)S(1)}) custom-call(bf16[72,896]{1,0:T(8,128)(2,1)S(1)} %collective-permute-done.4.far_ref, bf16[96,3072]{1,0:T(8,128)(2,1)S(1)} %get-tuple-element.41.stay_ref, bf16[24,3072]{1,0:T(8,128)(2,1)S(1)} %get-tuple-element.42.early_ref, f32[192,2048]{1,0:T(8,128)S(1)} %get-tuple-element.45.gate_in, ...), custom_call_target="tpu_custom_call" | custom-call | tf_op jit(solution)/shard_map/pallas_call | solution.py:38
  32.6 0.5 collective-permute-done.3.far_ref
  33.1 1.8 %shard_map.64 = (f32[192,2048]{1,0:T(8,128)S(1)}, f32[192,2048]{1,0:T(8,128)S(1)}) custom-call(bf16[72,896]{1,0:T(8,128)(2,1)S(1)} %collective-permute-done.3.far_ref, bf16[96,3072]{1,0:T(8,128)(2,1)S(1)} %get-tuple-element.41.stay_ref, bf16[24,3072]{1,0:T(8,128)(2,1)S(1)} %get-tuple-element.42.early_ref, f32[192,2048]{1,0:T(8,128)S(1)} %get-tuple-element.49.gate_in, ...), custom_call_target="tpu_custom_call" | custom-call | tf_op jit(solution)/shard_map/pallas_call | solution.py:38
  35.0 0.0 collective-permute-done.2.far_ref
  35.0 2.6 %shard_map.65 = bf16[16,48,512]{2,1,0:T(8,128)(2,1)} custom-call(bf16[72,768]{1,0:T(8,128)(2,1)S(1)} %collective-permute-done.2.far_ref, bf16[96,3072]{1,0:T(8,128)(2,1)S(1)} %get-tuple-element.41.stay_ref, bf16[24,3072]{1,0:T(8,128)(2,1)S(1)} %get-tuple-element.42.early_ref, f32[192,2048]{1,0:T(8,128)S(1)} %get-tuple-element.53.gate_in, ...), custom_call_target="tpu_custom_call" | custom-call | tf_op jit(solution)/shard_map/pallas_call | solution.py:38
  37.6 5.5 %all-to-all-start = ((bf16[16,48,512]{2,1,0:T(8,128)(2,1)}), bf16[16,48,512]{2,1,0:T(8,128)(2,1)S(1)}, u32[]{:S(2)}, u32[]{:S(2)}) async-start(bf16[16,48,512]{2,1,0:T(8,128)(2,1)} %shard_map.65), calls=%async_computation | async-start | bytes 1572864 | tf_op jit(solution)/shard_map/all_to_all | solution.py:34
  43.1 0.4 shard_map.55
  43.6 18.2 %all-to-all-done.recv_ref = bf16[16,48,512]{2,1,0:T(8,128)(2,1)S(1)} async-done(((bf16[16,48,512]{2,1,0:T(8,128)(2,1)}), bf16[16,48,512]{2,1,0:T(8,128)(2,1)S(1)}, u32[]{:S(2)}, u32[]{:S(2)}) %all-to-all-start) | async-done | bytes 786464 | tf_op jit(solution)/shard_map/all_to_all | solution.py:34
  61.8 1.1 %shard_map.66 = bf16[24,2,8192]{2,1,0:T(2,128)(2,1)} custom-call(bf16[192,192]{1,0:T(8,128)(2,1)S(1)} %get-tuple-element.30.picks_ref, f32[48,128]{1,0:T(8,128)S(1)} %get-tuple-element.31.column_ref, bf16[16,48,512]{2,1,0:T(8,128)(2,1)S(1)} %all-to-all-done.recv_ref), custom_call_target="tpu_custom_call" | custom-call | tf_op jit(solution)/shard_map/pallas_call | solution.py:330
  (12 shorter events, 0.0 us)
Async XLA Ops:
  0.0 29.2 %slice-start = ((s8[12582912]{0:T(1024)(128)(4,1)}), s8[4194304]{0:T(1024)(128)(4,1)S(1)}, s32[]{:S(2)}) async-start(s8[12582912]{0:T(1024)(128)(4,1)} %bitcast.2), calls=%async_computation.1 | async-start | bytes 8388608
  0.0 29.2 %slice-start.1 = ((s8[12582912]{0:T(1024)(128)(4,1)}), s8[4194304]{0:T(1024)(128)(4,1)S(1)}, s32[]{:S(2)}) async-start(s8[12582912]{0:T(1024)(128)(4,1)} %bitcast.2), calls=%async_computation.2 | async-start | bytes 8388608
  0.0 29.2 %slice-start.2 = ((s8[12582912]{0:T(1024)(128)(4,1)}), s8[4194304]{0:T(1024)(128)(4,1)S(1)}, s32[]{:S(2)}) async-start(s8[12582912]{0:T(1024)(128)(4,1)} %bitcast.2), calls=%async_computation.3 | async-start | bytes 8388608
  0.0 29.2 %copy-start = (bf16[1,3072,2048]{2,1,0:T(8,128)(2,1)S(1)}, bf16[1,3072,2048]{2,1,0:T(8,128)(2,1)}, u32[]{:S(2)}) copy-start(bf16[1,3072,2048]{2,1,0:T(8,128)(2,1)} %up_all.7) | copy-start | bytes 37748740
  1.1 20.2 %collective-permute-start = (bf16[24,3200]{1,0:T(8,128)(2,1)S(1)}, bf16[24,3200]{1,0:T(8,128)(2,1)S(1)}, u32[]{:S(2)}, u32[]{:S(2)}) collective-permute-start(bf16[24,3200]{1,0:T(8,128)(2,1)S(1)} %shard_map.56), channel_id=1, source_target_pairs={{0,2},{1,3},{2,0},{3,1},{4,6},{5,7},{6,4},{7,5},{8,10},{9,11},{10,... | collective-permute-start | bytes 460808 | tf_op jit(solution)/shard_map/ppermute | solution.py:217
  21.3 2.0 %collective-permute-start.1 = (bf16[96,3200]{1,0:T(8,128)(2,1)S(1)}, bf16[96,3200]{1,0:T(8,128)(2,1)S(1)}, u32[]{:S(2)}, u32[]{:S(2)}) collective-permute-start(bf16[96,3200]{1,0:T(8,128)(2,1)S(1)} %all_gather.3.own_ref.in_ref), channel_id=1, source_target_pairs={{0,1},{1,0},{2,3},{3,2},{4,5},{5,4},{6,7},{7,6},{8,9},{9,8},{10,11... | collective-permute-start | bytes 1843208 | tf_op jit(solution)/shard_map/ppermute | solution.py:217
  21.5 5.9 %collective-permute-start.5 = (bf16[72,640]{1,0:T(8,128)(2,1)S(1)}, bf16[72,640]{1,0:T(8,128)(2,1)S(1)}, u32[]{:S(2)}, u32[]{:S(2)}) collective-permute-start(bf16[72,640]{1,0:T(8,128)(2,1)S(1)} %shard_map.59), channel_id=1, source_target_pairs={{0,2},{1,3},{2,0},{3,1},{4,6},{5,7},{6,4},{7,5},{8,10},{9,11},{10,... | collective-permute-start | bytes 276488 | tf_op jit(solution)/shard_map/ppermute | solution.py:217
  22.1 5.9 %collective-permute-start.7 = (bf16[24,3200]{1,0:T(8,128)(2,1)S(1)}, bf16[24,3200]{1,0:T(8,128)(2,1)S(1)}, u32[]{:S(2)}, u32[]{:S(2)}) collective-permute-start(bf16[24,3200]{1,0:T(8,128)(2,1)S(1)} %collective-permute-done.early_ref), channel_id=1, source_target_pairs={{0,1},{1,0},{2,3},{3,2},{4,5},{5,4},{6,7},{7,6},{8,9},{9,8},{10,11... | collective-permute-start | bytes 460808 | tf_op jit(solution)/shard_map/ppermute | solution.py:217
  24.0 6.8 %collective-permute-start.4 = (bf16[72,896]{1,0:T(8,128)(2,1)S(1)}, bf16[72,896]{1,0:T(8,128)(2,1)S(1)}, u32[]{:S(2)}, u32[]{:S(2)}) collective-permute-start(bf16[72,896]{1,0:T(8,128)(2,1)S(1)} %shard_map.58), channel_id=1, source_target_pairs={{0,2},{1,3},{2,0},{3,1},{4,6},{5,7},{6,4},{7,5},{8,10},{9,11},{10,... | collective-permute-start | bytes 387080 | tf_op jit(solution)/shard_map/ppermute | solution.py:217
  25.3 7.8 %collective-permute-start.3 = (bf16[72,896]{1,0:T(8,128)(2,1)S(1)}, bf16[72,896]{1,0:T(8,128)(2,1)S(1)}, u32[]{:S(2)}, u32[]{:S(2)}) collective-permute-start(bf16[72,896]{1,0:T(8,128)(2,1)S(1)} %get-tuple-element.34), channel_id=1, source_target_pairs={{0,2},{1,3},{2,0},{3,1},{4,6},{5,7},{6,4},{7,5},{8,10},{9,11},{10,... | collective-permute-start | bytes 387080 | tf_op jit(solution)/shard_map/ppermute | solution.py:217
  26.9 8.1 %collective-permute-start.2 = (bf16[72,768]{1,0:T(8,128)(2,1)S(1)}, bf16[72,768]{1,0:T(8,128)(2,1)S(1)}, u32[]{:S(2)}, u32[]{:S(2)}) collective-permute-start(bf16[72,768]{1,0:T(8,128)(2,1)S(1)} %get-tuple-element.33), channel_id=1, source_target_pairs={{0,2},{1,3},{2,0},{3,1},{4,6},{5,7},{6,4},{7,5},{8,10},{9,11},{10,... | collective-permute-start | bytes 331784 | tf_op jit(solution)/shard_map/ppermute | solution.py:217
  27.4 1.8 %collective-permute-start.6 = (bf16[72,640]{1,0:T(8,128)(2,1)S(1)}, bf16[72,640]{1,0:T(8,128)(2,1)S(1)}, u32[]{:S(2)}, u32[]{:S(2)}) collective-permute-start(bf16[72,640]{1,0:T(8,128)(2,1)S(1)} %collective-permute-done.5.ref), channel_id=1, source_target_pairs={{0,1},{1,0},{2,3},{3,2},{4,5},{5,4},{6,7},{7,6},{8,9},{9,8},{10,11... | collective-permute-start | bytes 276488 | tf_op jit(solution)/shard_map/ppermute | solution.py:217
  37.6 5.5 %copy-start.1 = (s32[24,2]{0,1:T(2,128)S(1)}, s32[24,2]{0,1:T(2,128)}, u32[]{:S(2)}) copy-start(s32[24,2]{0,1:T(2,128)} %param.6) | copy-start | bytes 580
  37.6 5.6 %copy-start.2 = (f32[24,2]{0,1:T(2,128)S(1)}, f32[24,2]{0,1:T(2,128)}, u32[]{:S(2)}) copy-start(f32[24,2]{0,1:T(2,128)} %param.7) | copy-start | bytes 580
  37.6 24.2 %all-to-all-start = ((bf16[16,48,512]{2,1,0:T(8,128)(2,1)}), bf16[16,48,512]{2,1,0:T(8,128)(2,1)S(1)}, u32[]{:S(2)}, u32[]{:S(2)}) async-start(bf16[16,48,512]{2,1,0:T(8,128)(2,1)} %shard_map.65), calls=%async_computation | async-start | bytes 1572864 | tf_op jit(solution)/shard_map/all_to_all | solution.py:34

commit v17 on v15

--- a/solution.py
+++ b/solution.py
@@ -181,7 +181,8 @@
     gather_rows(x_ref, stay_ref[:, cut:], early_ref[:, cut:], far_ref[...])
     gate_val = gate_in[...] + exact_dot(x_ref[...], gate_all[0, cut:, :])
     up_val = up_in[...] + exact_dot(x_ref[...], up_all[0, cut:, :])
-    hidden_ref[...] = gate_val / (1.0 + jnp.exp(-gate_val)) * up_val
+    half = 0.5 * gate_val
+    hidden_ref[...] = (half + half * jnp.tanh(half)) * up_val
     store_blocks(folds, experts, hidden_ref, out_ref)
 
 

time: 62.8 us -> 62.8 us (level)
  no operation moved by 1% of the time
where the time goes in v17:
time: 62.8 us; the launch traced here: 62.5 us
  waiting for transfers between devices  20.6 us (33%)
  blocking collectives  17.1 us (27%)
  Pallas kernels  13.1 us (21%)
  starting transfers between devices  11.4 us (18%)
    all_to_all x1, waiting for transfers between devices, exchange(): lax.all_to_all(blocks, ('et', 'ep'), split_axis=0, concat_axis=0, tiled=T...  18.2 us
    all_gather x1, blocking collectives, routed_by_columns(): own = lax.all_gather(packed, 'et', axis=0, tiled=True)  17.1 us
    pallas_call x10, Pallas kernels, local_kernel(): pl.pallas_call(kernel, out_shape=out_shape, in_specs=[WHOLE] * len(args)...  12 us
    ppermute x8, starting transfers between devices, swap(): return lax.ppermute(block, 'ep', [(i, i ^ bit) for i in range(experts)])  6.48 us
    all_to_all x1, starting transfers between devices, exchange(): lax.all_to_all(blocks, ('et', 'ep'), split_axis=0, concat_axis=0, tiled=T...  4.95 us
    ppermute x8, waiting for transfers between devices, swap(): return lax.ppermute(block, 'ep', [(i, i ^ bit) for i in range(experts)])  2.33 us
  transfers between devices with their start and end apart: 9, of which 4 were waited for; matrix products, arithmetic and copies ran while one was open for 0% of the time, Pallas kernels for 13%

profile of v17, /device:TPU:0, one launch (start us, length us, event | category | flops | bytes accessed | tf_op | source)
XLA Modules:
  0.0 62.5 jit_solution(7371060719819702386)
XLA Ops:
  0.0 1.1 %shard_map.56 = bf16[24,3200]{1,0:T(8,128)(2,1)S(1)} custom-call(s32[2,24]{1,0:T(2,128)} %bitcast.4, bf16[24,3072]{1,0:T(8,128)(2,1)} %tokens_hbm.1, bf16[1,3072,2048]{2,1,0:T(8,128)(2,1)} %gate_all.7, bf16[1,3072,2048]{2,1,0:T(8,128)(2,1)} %up_all.7), custom_call_target="tpu_custom_call" | custom-call | tf_op jit(solution)/shard_map/pallas_call | solution.py:38
  1.1 3.0 %collective-permute-start = (bf16[24,3200]{1,0:T(8,128)(2,1)S(1)}, bf16[24,3200]{1,0:T(8,128)(2,1)S(1)}, u32[]{:S(2)}, u32[]{:S(2)}) collective-permute-start(bf16[24,3200]{1,0:T(8,128)(2,1)S(1)} %shard_map.56), channel_id=1, source_target_pairs={{0,2},{1,3},{2,0},{3,1},{4,6},{5,7},{6,4},{7,5},{8,10},{9,11},{10,... | collective-permute-start | bytes 460808 | tf_op jit(solution)/shard_map/ppermute | solution.py:218
  4.1 17.1 %all_gather.3.own_ref.in_ref = bf16[96,3200]{1,0:T(8,128)(2,1)S(1)} all-gather(bf16[24,3200]{1,0:T(8,128)(2,1)S(1)} %shard_map.56), channel_id=1, replica_groups=mesh['groups'=2,'et'=4,'ep'=4] {'et'}, dimensions={0}, use_global_device_ids=true | all-gather | bytes 768000 | tf_op jit(solution)/shard_map/all_gather | solution.py:228
  21.3 0.0 collective-permute-done.early_ref
  21.3 0.0 collective-permute-start.1
  21.3 0.2 shard_map.58
  21.5 0.6 collective-permute-start.5
  22.1 0.2 collective-permute-start.7
  22.3 1.0 %collective-permute-done.1.near_ref = bf16[96,3200]{1,0:T(8,128)(2,1)S(1)} collective-permute-done((bf16[96,3200]{1,0:T(8,128)(2,1)S(1)}, bf16[96,3200]{1,0:T(8,128)(2,1)S(1)}, u32[]{:S(2)}, u32[]{:S(2)}) %collective-permute-start.1) | collective-permute-done | bytes 614432 | tf_op jit(solution)/shard_map/ppermute | solution.py:218
  23.3 0.8 %shard_map.57 = (bf16[72,896]{1,0:T(8,128)(2,1)S(1)}, bf16[72,896]{1,0:T(8,128)(2,1)S(1)}, bf16[72,768]{1,0:T(8,128)(2,1)S(1)}) custom-call(bf16[96,3200]{1,0:T(8,128)(2,1)S(1)} %all_gather.3.own_ref.in_ref, bf16[96,3200]{1,0:T(8,128)(2,1)S(1)} %collective-permute-done.1.near_ref), custom_call_target="tpu_custom_call" | custom-call | tf_op jit(solution)/shard_map/pallas_call | solution.py:38
  24.1 0.6 collective-permute-start.4
  24.7 1.5 %collective-permute-start.3 = (bf16[72,896]{1,0:T(8,128)(2,1)S(1)}, bf16[72,896]{1,0:T(8,128)(2,1)S(1)}, u32[]{:S(2)}, u32[]{:S(2)}) collective-permute-start(bf16[72,896]{1,0:T(8,128)(2,1)S(1)} %get-tuple-element.35), channel_id=1, source_target_pairs={{0,2},{1,3},{2,0},{3,1},{4,6},{5,7},{6,4},{7,5},{8,10},{9,11},{10,... | collective-permute-start | bytes 387080 | tf_op jit(solution)/shard_map/ppermute | solution.py:218
  26.2 0.5 collective-permute-start.2
  26.7 0.0 collective-permute-done.5.ref
  26.7 0.0 collective-permute-start.6
  26.7 0.5 shard_map.59.part_ref
  27.3 0.0 collective-permute-done.7.early_other
  27.3 1.2 %shard_map.60 = (bf16[96,3072]{1,0:T(8,128)(2,1)S(1)}, bf16[24,3072]{1,0:T(8,128)(2,1)S(1)}) custom-call(bf16[96,3200]{1,0:T(8,128)(2,1)S(1)} %all_gather.3.own_ref.in_ref, bf16[96,3200]{1,0:T(8,128)(2,1)S(1)} %collective-permute-done.1.near_ref, bf16[24,3200]{1,0:T(8,128)(2,1)S(1)} %collective-permute-done.early_ref, ...), custom_call_target="tpu_custom_call" | custom-call | tf_op jit(solution)/shard_map/pallas_call | solution.py:38
  28.5 0.0 collective-permute-done.6.other_ref
  28.6 1.5 %shard_map.61 = (f32[192,2048]{1,0:T(8,128)S(1)}, f32[192,2048]{1,0:T(8,128)S(1)}) custom-call(bf16[72,640]{1,0:T(8,128)(2,1)S(1)} %collective-permute-done.6.other_ref, bf16[72,512]{1,0:T(8,128)(2,1)S(1)} %shard_map.59.part_ref, bf16[96,3072]{1,0:T(8,128)(2,1)S(1)} %get-tuple-element.43.stay_ref, bf16[24,3072]{1,0:T(8,128)(2,1)S(1)} %get-tuple-element.44.early_ref, ...), custom_call_target="tpu_custom_call" | custom-call | tf_op jit(solution)/shard_map/pallas_call | solution.py:38
  30.1 0.4 collective-permute-done.4.far_ref
  30.5 1.8 %shard_map.62 = (f32[192,2048]{1,0:T(8,128)S(1)}, f32[192,2048]{1,0:T(8,128)S(1)}) custom-call(bf16[72,896]{1,0:T(8,128)(2,1)S(1)} %collective-permute-done.4.far_ref, bf16[96,3072]{1,0:T(8,128)(2,1)S(1)} %get-tuple-element.43.stay_ref, bf16[24,3072]{1,0:T(8,128)(2,1)S(1)} %get-tuple-element.44.early_ref, f32[192,2048]{1,0:T(8,128)S(1)} %get-tuple-element.47.gate_in, ...), custom_call_target="tpu_custom_call" | custom-call | tf_op jit(solution)/shard_map/pallas_call | solution.py:38
  32.3 0.9 %collective-permute-done.3.far_ref = bf16[72,896]{1,0:T(8,128)(2,1)S(1)} collective-permute-done((bf16[72,896]{1,0:T(8,128)(2,1)S(1)}, bf16[72,896]{1,0:T(8,128)(2,1)S(1)}, u32[]{:S(2)}, u32[]{:S(2)}) %collective-permute-start.3) | collective-permute-done | bytes 129056 | tf_op jit(solution)/shard_map/ppermute | solution.py:218
  33.2 1.8 %shard_map.63 = (f32[192,2048]{1,0:T(8,128)S(1)}, f32[192,2048]{1,0:T(8,128)S(1)}) custom-call(bf16[72,896]{1,0:T(8,128)(2,1)S(1)} %collective-permute-done.3.far_ref, bf16[96,3072]{1,0:T(8,128)(2,1)S(1)} %get-tuple-element.43.stay_ref, bf16[24,3072]{1,0:T(8,128)(2,1)S(1)} %get-tuple-element.44.early_ref, f32[192,2048]{1,0:T(8,128)S(1)} %get-tuple-element.51.gate_in, ...), custom_call_target="tpu_custom_call" | custom-call | tf_op jit(solution)/shard_map/pallas_call | solution.py:38
  35.1 0.0 collective-permute-done.2.far_ref
  35.1 2.6 %shard_map.64 = bf16[16,48,512]{2,1,0:T(8,128)(2,1)} custom-call(bf16[72,768]{1,0:T(8,128)(2,1)S(1)} %collective-permute-done.2.far_ref, bf16[96,3072]{1,0:T(8,128)(2,1)S(1)} %get-tuple-element.43.stay_ref, bf16[24,3072]{1,0:T(8,128)(2,1)S(1)} %get-tuple-element.44.early_ref, f32[192,2048]{1,0:T(8,128)S(1)} %get-tuple-element.55.gate_in, ...), custom_call_target="tpu_custom_call" | custom-call | tf_op jit(solution)/shard_map/pallas_call | solution.py:38
  37.7 5.0 %all-to-all-start = ((bf16[16,48,512]{2,1,0:T(8,128)(2,1)}), bf16[16,48,512]{2,1,0:T(8,128)(2,1)S(1)}, u32[]{:S(2)}, u32[]{:S(2)}) async-start(bf16[16,48,512]{2,1,0:T(8,128)(2,1)} %shard_map.64), calls=%async_computation | async-start | bytes 1572864 | tf_op jit(solution)/shard_map/all_to_all | solution.py:34
  42.7 0.0 copy-done.1
  42.7 0.0 copy-done.2
  42.7 0.4 shard_map.55
  43.1 18.2 %all-to-all-done.recv_ref = bf16[16,48,512]{2,1,0:T(8,128)(2,1)S(1)} async-done(((bf16[16,48,512]{2,1,0:T(8,128)(2,1)}), bf16[16,48,512]{2,1,0:T(8,128)(2,1)S(1)}, u32[]{:S(2)}, u32[]{:S(2)}) %all-to-all-start) | async-done | bytes 786464 | tf_op jit(solution)/shard_map/all_to_all | solution.py:34
  61.4 1.1 %shard_map.65 = bf16[24,2,8192]{2,1,0:T(2,128)(2,1)} custom-call(bf16[192,192]{1,0:T(8,128)(2,1)S(1)} %get-tuple-element.31.picks_ref, f32[48,128]{1,0:T(8,128)S(1)} %get-tuple-element.32.column_ref, bf16[16,48,512]{2,1,0:T(8,128)(2,1)S(1)} %all-to-all-done.recv_ref), custom_call_target="tpu_custom_call" | custom-call | tf_op jit(solution)/shard_map/pallas_call | solution.py:325
  (11 shorter events, 0.0 us)
Async XLA Ops:
  0.0 28.5 %slice-start = ((s8[12582912]{0:T(1024)(128)(4,1)}), s8[4194304]{0:T(1024)(128)(4,1)S(1)}, s32[]{:S(2)}) async-start(s8[12582912]{0:T(1024)(128)(4,1)} %bitcast.2), calls=%async_computation.1 | async-start | bytes 8388608
  0.0 28.5 %slice-start.1 = ((s8[12582912]{0:T(1024)(128)(4,1)}), s8[4194304]{0:T(1024)(128)(4,1)S(1)}, s32[]{:S(2)}) async-start(s8[12582912]{0:T(1024)(128)(4,1)} %bitcast.2), calls=%async_computation.2 | async-start | bytes 8388608
  0.0 28.5 %slice-start.2 = ((s8[12582912]{0:T(1024)(128)(4,1)}), s8[4194304]{0:T(1024)(128)(4,1)S(1)}, s32[]{:S(2)}) async-start(s8[12582912]{0:T(1024)(128)(4,1)} %bitcast.2), calls=%async_computation.3 | async-start | bytes 8388608
  0.0 28.5 %copy-start = (bf16[1,3072,2048]{2,1,0:T(8,128)(2,1)S(1)}, bf16[1,3072,2048]{2,1,0:T(8,128)(2,1)}, u32[]{:S(2)}) copy-start(bf16[1,3072,2048]{2,1,0:T(8,128)(2,1)} %up_all.7) | copy-start | bytes 37748740
  1.1 20.2 %collective-permute-start = (bf16[24,3200]{1,0:T(8,128)(2,1)S(1)}, bf16[24,3200]{1,0:T(8,128)(2,1)S(1)}, u32[]{:S(2)}, u32[]{:S(2)}) collective-permute-start(bf16[24,3200]{1,0:T(8,128)(2,1)S(1)} %shard_map.56), channel_id=1, source_target_pairs={{0,2},{1,3},{2,0},{3,1},{4,6},{5,7},{6,4},{7,5},{8,10},{9,11},{10,... | collective-permute-start | bytes 460808 | tf_op jit(solution)/shard_map/ppermute | solution.py:218
  21.3 2.0 %collective-permute-start.1 = (bf16[96,3200]{1,0:T(8,128)(2,1)S(1)}, bf16[96,3200]{1,0:T(8,128)(2,1)S(1)}, u32[]{:S(2)}, u32[]{:S(2)}) collective-permute-start(bf16[96,3200]{1,0:T(8,128)(2,1)S(1)} %all_gather.3.own_ref.in_ref), channel_id=1, source_target_pairs={{0,1},{1,0},{2,3},{3,2},{4,5},{5,4},{6,7},{7,6},{8,9},{9,8},{10,11... | collective-permute-start | bytes 1843208 | tf_op jit(solution)/shard_map/ppermute | solution.py:218
  21.5 5.3 %collective-permute-start.5 = (bf16[72,640]{1,0:T(8,128)(2,1)S(1)}, bf16[72,640]{1,0:T(8,128)(2,1)S(1)}, u32[]{:S(2)}, u32[]{:S(2)}) collective-permute-start(bf16[72,640]{1,0:T(8,128)(2,1)S(1)} %shard_map.58), channel_id=1, source_target_pairs={{0,2},{1,3},{2,0},{3,1},{4,6},{5,7},{6,4},{7,5},{8,10},{9,11},{10,... | collective-permute-start | bytes 276488 | tf_op jit(solution)/shard_map/ppermute | solution.py:218
  22.1 5.2 %collective-permute-start.7 = (bf16[24,3200]{1,0:T(8,128)(2,1)S(1)}, bf16[24,3200]{1,0:T(8,128)(2,1)S(1)}, u32[]{:S(2)}, u32[]{:S(2)}) collective-permute-start(bf16[24,3200]{1,0:T(8,128)(2,1)S(1)} %collective-permute-done.early_ref), channel_id=1, source_target_pairs={{0,1},{1,0},{2,3},{3,2},{4,5},{5,4},{6,7},{7,6},{8,9},{9,8},{10,11... | collective-permute-start | bytes 460808 | tf_op jit(solution)/shard_map/ppermute | solution.py:218
  24.1 6.4 %collective-permute-start.4 = (bf16[72,896]{1,0:T(8,128)(2,1)S(1)}, bf16[72,896]{1,0:T(8,128)(2,1)S(1)}, u32[]{:S(2)}, u32[]{:S(2)}) collective-permute-start(bf16[72,896]{1,0:T(8,128)(2,1)S(1)} %get-tuple-element.36), channel_id=1, source_target_pairs={{0,2},{1,3},{2,0},{3,1},{4,6},{5,7},{6,4},{7,5},{8,10},{9,11},{10,... | collective-permute-start | bytes 387080 | tf_op jit(solution)/shard_map/ppermute | solution.py:218
  24.7 8.5 %collective-permute-start.3 = (bf16[72,896]{1,0:T(8,128)(2,1)S(1)}, bf16[72,896]{1,0:T(8,128)(2,1)S(1)}, u32[]{:S(2)}, u32[]{:S(2)}) collective-permute-start(bf16[72,896]{1,0:T(8,128)(2,1)S(1)} %get-tuple-element.35), channel_id=1, source_target_pairs={{0,2},{1,3},{2,0},{3,1},{4,6},{5,7},{6,4},{7,5},{8,10},{9,11},{10,... | collective-permute-start | bytes 387080 | tf_op jit(solution)/shard_map/ppermute | solution.py:218
  26.2 8.9 %collective-permute-start.2 = (bf16[72,768]{1,0:T(8,128)(2,1)S(1)}, bf16[72,768]{1,0:T(8,128)(2,1)S(1)}, u32[]{:S(2)}, u32[]{:S(2)}) collective-permute-start(bf16[72,768]{1,0:T(8,128)(2,1)S(1)} %get-tuple-element.34), channel_id=1, source_target_pairs={{0,2},{1,3},{2,0},{3,1},{4,6},{5,7},{6,4},{7,5},{8,10},{9,11},{10,... | collective-permute-start | bytes 331784 | tf_op jit(solution)/shard_map/ppermute | solution.py:218
  26.7 1.8 %collective-permute-start.6 = (bf16[72,640]{1,0:T(8,128)(2,1)S(1)}, bf16[72,640]{1,0:T(8,128)(2,1)S(1)}, u32[]{:S(2)}, u32[]{:S(2)}) collective-permute-start(bf16[72,640]{1,0:T(8,128)(2,1)S(1)} %collective-permute-done.5.ref), channel_id=1, source_target_pairs={{0,1},{1,0},{2,3},{3,2},{4,5},{5,4},{6,7},{7,6},{8,9},{9,8},{10,11... | collective-permute-start | bytes 276488 | tf_op jit(solution)/shard_map/ppermute | solution.py:218
  37.7 5.0 %copy-start.1 = (s32[24,2]{0,1:T(2,128)S(1)}, s32[24,2]{0,1:T(2,128)}, u32[]{:S(2)}) copy-start(s32[24,2]{0,1:T(2,128)} %param.6) | copy-start | bytes 580
  37.7 5.0 %copy-start.2 = (f32[24,2]{0,1:T(2,128)S(1)}, f32[24,2]{0,1:T(2,128)}, u32[]{:S(2)}) copy-start(f32[24,2]{0,1:T(2,128)} %param.7) | copy-start | bytes 580
  37.7 23.7 %all-to-all-start = ((bf16[16,48,512]{2,1,0:T(8,128)(2,1)}), bf16[16,48,512]{2,1,0:T(8,128)(2,1)S(1)}, u32[]{:S(2)}, u32[]{:S(2)}) async-start(bf16[16,48,512]{2,1,0:T(8,128)(2,1)} %shard_map.64), calls=%async_computation | async-start | bytes 1572864 | tf_op jit(solution)/shard_map/all_to_all | solution.py:34
